TPU v7x, 32 devices: a whole 2x2x4 slice. The times are simulated.
32 devices in a mesh: dp: 16 (over z, y, x), ctx: 2 (over core).
Axes of the slice: x: 2, y: 2, z: 4, core: 2. Of those that a mesh axis runs over, the one named last changes fastest.
Arguments:
- inputs: bfloat16 [2, 16, 1024, 960], P(None, 'dp', 'ctx'), may hold values from -6 to 6
- segment_ids: int32 [2, 16, 1024], P(None, 'dp'), may hold values from 0 to 3, as said below
- positions: int32 [2, 16, 1024], P(None, 'dp'), may hold values from 0 to 767, as said below
- w_query: bfloat16 [960, 960], P('dp', 'ctx'), may hold values from -0.1875 to 0.1875
- w_key: bfloat16 [960, 320], P('dp', 'ctx'), may hold values from -0.1875 to 0.1875
- w_value: bfloat16 [960, 320], P('dp', 'ctx'), may hold values from -0.1875 to 0.1875
- w_out: bfloat16 [960, 960], P('dp', 'ctx'), may hold values from -0.5 to 0.5
- w_gate: bfloat16 [960, 2560], P('dp', 'ctx'), may hold values from -0.1875 to 0.1875
- w_up: bfloat16 [960, 2560], P('dp', 'ctx'), may hold values from -0.1875 to 0.1875
- w_down: bfloat16 [2560, 960], P('dp', 'ctx'), may hold values from -0.125 to 0.125
- gain_attn: bfloat16 [960], P('dp'), may hold values from 0.5 to 1.5
- gain_ffn: bfloat16 [960], P('dp'), may hold values from 0.5 to 1.5
- cotangent: bfloat16 [2, 16, 1024, 960], P(None, 'dp', 'ctx'), may hold values from -6 to 6
Outputs:
- outputs: bfloat16 [2, 16, 1024, 960], P(None, 'dp', 'ctx')
- grad_inputs: float32 [2, 16, 1024, 960], P(None, 'dp', 'ctx')
- grad_w_query: float32 [960, 960], P('dp', 'ctx')
- grad_w_key: float32 [960, 320], P('dp', 'ctx')
- grad_w_value: float32 [960, 320], P('dp', 'ctx')
- grad_w_out: float32 [960, 960], P('dp', 'ctx')
- grad_w_gate: float32 [960, 2560], P('dp', 'ctx')
- grad_w_up: float32 [960, 2560], P('dp', 'ctx')
- grad_w_down: float32 [2560, 960], P('dp', 'ctx')
- grad_gain_attn: float32 [960], P('dp')
- grad_gain_ffn: float32 [960], P('dp')
Inputs may be any that keep to these rules, and one draw needn't show every extreme that they name: `segment_ids`: along each sequence the ids never fall, each of the 4 ids is used, and one document has exactly 768 tokens. `positions`: the number of earlier tokens of the same document in the sequence.
All inputs are finite; a program needn't handle non-finite values.
Results may differ from a plain program's by a relative error of at most 0.02.
Values may be sent and summed in bfloat16 or wider, within the bound.
No kernel may reach another device: no remote copies, remote signals or barrier semaphores. Data moves between devices by JAX's collectives and lax.ppermute only.
A program may use at most 192 MiB of HBM per device.

v0:
```python
import functools

import jax
import jax.numpy as jnp
from jax import lax
from jax.experimental import pallas as pl
from jax.experimental.pallas import tpu as pltpu
from jax.sharding import PartitionSpec as P

HEADS = 15
KV_HEADS = 5
HEAD = 64
MICRO = 2
GROUP = 3
DOCS = 4

EPSILON = 1e-05
MASKED = -1e30
LANES = 128
QKV = (HEADS + 2 * KV_HEADS) * HEAD
QKV_PAD = 1664
VMEM_LIMIT = 56 * 1024 * 1024
PACK = 1408
VMEM_SMALL = 24 * 1024 * 1024
WIDE_HEADS = HEADS * LANES
F32 = jnp.float32
BF16 = jnp.bfloat16


def up(value, step):
    return -(-value // step) * step


def mm(left, right):
    return lax.dot_general(left, right, (((1,), (0,)), ((), ())), preferred_element_type=F32)


def mm_nt(left, right):
    return lax.dot_general(left, right, (((1,), (1,)), ((), ())), preferred_element_type=F32)


def mm_tn(left, right):
    return lax.dot_general(left, right, (((0,), (0,)), ((), ())), preferred_element_type=F32)


def call(body, out_shape, grid, in_specs, out_specs, scratch=(), flops=0, moved=0, prefetch=0, alias=None,
         vmem=VMEM_LIMIT):
    return pl.pallas_call(
        body,
        out_shape=out_shape,
        grid_spec=pltpu.PrefetchScalarGridSpec(
            num_scalar_prefetch=prefetch,
            grid=grid,
            in_specs=in_specs,
            out_specs=out_specs,
            scratch_shapes=scratch,
        ),
        input_output_aliases=alias or {},
        compiler_params=pltpu.CompilerParams(vmem_limit_bytes=vmem),
        cost_estimate=pl.CostEstimate(flops=flops, bytes_accessed=moved, transcendentals=0),
    )


def whole(shape):
    return pl.BlockSpec(shape, lambda *_: (0,) * len(shape), pipeline_mode=pl.Buffered(1))


def lane_of(rows):
    return lax.broadcasted_iota(jnp.int32, (rows, LANES), 1)


def three_terms(column):
    high = column.astype(BF16).astype(F32)
    rest = column - high
    mid = rest.astype(BF16).astype(F32)
    return high, mid, rest - mid


def put_terms(base, column, lane, first):
    high, mid, low = three_terms(column)
    base = jnp.where(lane == first, high, base)
    base = jnp.where(lane == first + 1, mid, base)
    return jnp.where(lane == first + 2, low, base)


def build_weights(place_ref, piece_refs, stage_ref, w_ref, wo_ref):
    core, z, y, x = (place_ref[n] for n in range(4))
    for swapped in range(2):
        near_a, far_a, near_b, far_b = piece_refs[4 * swapped : 4 * swapped + 4]
        to = jnp.bitwise_xor(core, swapped)
        for dy in range(2):
            for dx in range(2):
                for k in range(4):
                    block = lax.rem(z + 4 - k, 4) * 4 + (y ^ dy) * 2 + (x ^ dx)
                    row = pl.multiple_of(block * 64, 64)
                    stage_ref[to, pl.ds(row, 32), :] = (far_a if dy else near_a)[4 * dx + k]
                    stage_ref[to, pl.ds(row + 32, 32), :] = (far_b if dx else near_b)[4 * dy + k]
    n_q, n_k = HEADS * HEAD // 2, KV_HEADS * HEAD // 2
    for j in range(2):
        w_ref[:, n_q * j : n_q * (j + 1)] = stage_ref[j, :, :n_q]
        for part in range(2):
            to, at = 2 * n_q + n_k * (2 * part + j), n_q + n_k * part
            w_ref[:, to : to + n_k] = stage_ref[j, :, at : at + n_k]
        half = wo_ref.shape[1] // 2
        wo_ref[:, half * j : half * (j + 1)] = stage_ref[j, :, PACK - half :]
    w_ref[:, QKV:] = jnp.zeros((w_ref.shape[0], QKV_PAD - QKV), BF16)


def projections(xp, scale, w_ref, gain_ref, cos_ref, sa_ref, sb_ref, aq_ref, ak_ref,
                xp_ref, a_ref, q_ref, k_ref, v_ref):
    a = (xp * scale * gain_ref[:1]).astype(BF16)
    xp_ref[...] = xp.astype(BF16)
    a_ref[...] = a
    t = mm(a, w_ref[...])
    lane = lane_of(t.shape[0])
    low = lane < HEAD
    cos, sa, sb, aq, ak = cos_ref[...], sa_ref[...], sb_ref[...], aq_ref[...], ak_ref[...]
    for pair in range((HEADS + KV_HEADS) // 2):
        tt = t[:, LANES * pair : LANES * (pair + 1)]
        rot = tt * cos + pltpu.roll(tt, 32, 1) * sa + pltpu.roll(tt, 96, 1) * sb
        for half in range(2):
            head = 2 * pair + half
            val = rot if half == 0 else pltpu.roll(rot, 64, 1)
            if head < HEADS:
                q_ref[head] = jnp.where(low, val * HEAD ** -0.5, aq).astype(BF16)
            else:
                k_ref[head - HEADS] = jnp.where(low, val, ak).astype(BF16)
    av = jnp.where(lane < HEAD + 3, -1.0, 0.0)
    for head in range(KV_HEADS):
        first = (HEADS + KV_HEADS) * HEAD + LANES * (head // 2)
        tt = t[:, first : first + LANES]
        val = tt if head % 2 == 0 else pltpu.roll(tt, 64, 1)
        v_ref[head] = jnp.where(low, val, av).astype(BF16)


def own_or_other(place_ref, own_ref, other_ref):
    first = pl.program_id(0) < pl.num_programs(0) // 2
    mine = first == (place_ref[0] == 0)
    return jnp.where(mine, own_ref[...], other_ref[...])


def pre_body(width, place_ref, own_ref, other_ref, e_ref, *refs):
    pieces, refs = refs[:8], refs[8:]
    *rest, w_ref, wo_ref, gain_ref, stage_ref = refs

    @pl.when(pl.program_id(0) == 0)
    def _():
        build_weights(place_ref, pieces, stage_ref, w_ref, wo_ref)
        gain_ref[...] = stage_ref[0, :, 768:896].astype(F32).T[32:40]

    xp = mm_tn(own_or_other(place_ref, own_ref, other_ref), e_ref[:width, :])
    scale = lax.rsqrt(jnp.sum(xp * xp, axis=-1, keepdims=True) / width + EPSILON)
    projections(xp, scale, w_ref, gain_ref, *rest)


def halves_specs(rows, width, block):
    steps = rows // block
    return [pl.BlockSpec((width, block), lambda i, *_: (0, i % steps))] * 2


def pre_attention(place, own, other, spread, pieces, cos, sa, sb, aq, ak, block=512):
    width, half = own.shape
    seq, wide = 2 * half, spread.shape[1]
    rows = lambda n: pl.BlockSpec((block, n), lambda i, *_: (i, 0))
    heads = lambda n: pl.BlockSpec((n, block, LANES), lambda i, *_: (0, i, 0))
    return call(
        functools.partial(pre_body, width),
        [
            jax.ShapeDtypeStruct((seq, wide), BF16),
            jax.ShapeDtypeStruct((seq, wide), BF16),
            jax.ShapeDtypeStruct((HEADS, seq, LANES), BF16),
            jax.ShapeDtypeStruct((KV_HEADS, seq, LANES), BF16),
            jax.ShapeDtypeStruct((KV_HEADS, seq, LANES), BF16),
            jax.ShapeDtypeStruct((wide, QKV_PAD), BF16),
            jax.ShapeDtypeStruct((wide, wide), BF16),
            jax.ShapeDtypeStruct((8, wide), F32),
        ],
        (seq // block,),
        halves_specs(half, width, block)
        + [whole(spread.shape)]
        + [whole(w.shape) for w in pieces]
        + [rows(LANES)] * 5,
        [rows(wide), rows(wide), heads(HEADS), heads(KV_HEADS), heads(KV_HEADS)]
        + [whole((wide, QKV_PAD)), whole((wide, wide)), whole((8, wide))],
        scratch=[pltpu.VMEM((2, wide, PACK), BF16)],
        flops=2 * seq * wide * (width + QKV_PAD),
        moved=20_000_000,
        prefetch=1,
    )(place, own, other, spread, *pieces, cos, sa, sb, aq, ak)


def attend_body(block, q_ref, k_ref, v_ref, o_ref, q2_ref):
    seq = k_ref.shape[1]
    rows = GROUP * block
    below = lax.broadcasted_iota(jnp.int32, (block, block), 0) >= lax.broadcasted_iota(
        jnp.int32, (block, block), 1
    )
    below = jnp.concatenate([below.astype(F32)] * GROUP, axis=0) > 0.5
    lane = lane_of(rows)
    for i in range(seq // block):
        span = slice(block * i, block * (i + 1))
        q = q_ref[:, span, :].reshape(rows, LANES)
        s_in = jnp.where(below, mm_nt(q, k_ref[0, span, :]), MASKED)
        top = jnp.max(s_in, axis=-1, keepdims=True)
        if i:
            s_left = mm_nt(q, k_ref[0, : block * i, :])
            top = jnp.maximum(top, jnp.max(s_left, axis=-1, keepdims=True))
        ext = mm(jnp.exp(s_in - top).astype(BF16), v_ref[0, span, :])
        if i:
            ext = ext + mm(jnp.exp(s_left - top).astype(BF16), v_ref[0, : block * i, :])
        total = -ext[:, HEAD : HEAD + 1]
        o = ext / total
        o = jnp.where(lane < HEAD, o, pltpu.roll(o, 64, 1))
        o_ref[:, span, :] = o.reshape(GROUP, block, LANES).astype(BF16)
        q2 = put_terms(q.astype(F32), top + jnp.log(total), lane, HEAD + DOCS)
        q2_ref[:, span, :] = q2.reshape(GROUP, block, LANES).astype(BF16)


def attend(q, k, v, block=256):
    seq = q.shape[1]
    group = pl.BlockSpec((GROUP, seq, LANES), lambda n: (n, 0, 0))
    one = pl.BlockSpec((1, seq, LANES), lambda n: (n, 0, 0))
    shape = jax.ShapeDtypeStruct(q.shape, BF16)
    return call(
        functools.partial(attend_body, block),
        [shape, shape],
        (KV_HEADS,),
        [group, one, one],
        [group, group],
        flops=4 * HEADS * seq * seq * LANES,
        moved=15_000_000,
    )(q, k, v)


def attend_back_body(block, q_ref, k_ref, v_ref, do_ref, cos_ref, sa_ref, sb_ref,
                     dq_ref, dk_ref, dv_ref, acc_ref):
    seq = k_ref.shape[1]
    above = lax.broadcasted_iota(jnp.int32, (block, block), 0) <= lax.broadcasted_iota(
        jnp.int32, (block, block), 1
    )
    lane = lane_of(seq)

    def unrotate(t, span):
        rows = span.stop - span.start
        rot = (
            t * cos_ref[span, :]
            - pltpu.roll(t, 32, 1) * sa_ref[span, :]
            - pltpu.roll(t, 96, 1) * sb_ref[span, :]
        )
        return twice(rot, rows)

    def twice(t, rows):
        return jnp.where(lane[:rows] < HEAD, t, pltpu.roll(t, 64, 1)).astype(BF16)

    for j in range(seq // block):
        span = slice(block * j, block * (j + 1))
        k, v = k_ref[0, span, :], v_ref[0, span, :]
        dk = jnp.zeros((block, LANES), F32)
        dv = jnp.zeros((block, LANES), F32)
        for g in range(GROUP):
            q, do = q_ref[g, block * j :, :], do_ref[g, block * j :, :]
            p = jnp.exp(mm_nt(k, q))
            inner = jnp.where(above, p[:, :block], 0.0)
            p = inner if p.shape[1] == block else jnp.concatenate([inner, p[:, block:]], axis=1)
            ds = (p * mm_nt(v, do)).astype(BF16)
            dv = dv + mm(p.astype(BF16), do)
            dk = dk + mm(ds, q)
            dq = mm_tn(ds, k)
            if j == 0:
                acc_ref[g] = dq
            else:
                acc_ref[g, block * j :, :] += dq
        dk_ref[0, span, :] = unrotate(dk, span)
        dv_ref[0, span, :] = twice(dv, block)
    for g in range(GROUP):
        dq_ref[g] = unrotate(acc_ref[g] * HEAD ** -0.5, slice(0, seq))


def attend_back(q, k, v, do, cos, sa, sb, first, count, block=256):
    seq = q.shape[1]
    group = lambda at: pl.BlockSpec((GROUP, seq, LANES), lambda n: (n + at, 0, 0))
    one = lambda at: pl.BlockSpec((1, seq, LANES), lambda n: (n + at, 0, 0))
    return call(
        functools.partial(attend_back_body, block),
        [
            jax.ShapeDtypeStruct((GROUP * count, seq, LANES), BF16),
            jax.ShapeDtypeStruct((count, seq, LANES), BF16),
            jax.ShapeDtypeStruct((count, seq, LANES), BF16),
        ],
        (count,),
        [group(first), one(first), one(first), group(first)] + [whole((seq, LANES))] * 3,
        [group(0), one(0), one(0)],
        scratch=[pltpu.VMEM((GROUP, seq, LANES), F32)],
        flops=10 * GROUP * count * seq * seq * LANES,
        moved=4_000_000 * count,
    )(q, k, v, do, cos, sa, sb)


def pairs_to(ref, get, heads, first=0):
    for pair in range((heads + 1) // 2):
        left = get(2 * pair)
        lane = lane_of(left.shape[0])
        right = get(2 * pair + 1).astype(F32) if 2 * pair + 1 < heads else 0.0
        both = jnp.where(lane < HEAD, left.astype(F32), right)
        ref[:, first + LANES * pair : first + LANES * (pair + 1)] = both.astype(BF16)


def mid_body(width, place_ref, o_ref, own_ref, other_ref, e_ref, u_ref, wo_ref, xp_ref, gain_ref,
             op_ref, m_ref, b_ref, df_ref):
    flat = jnp.concatenate([o_ref[head] for head in range(HEADS)], axis=1)
    op = mm_nt(flat, u_ref[: wo_ref.shape[0], :]).astype(BF16)
    op_ref[...] = op
    m = xp_ref[...].astype(F32) + mm(op, wo_ref[...])
    m_ref[...] = m
    scale = lax.rsqrt(jnp.sum(m * m, axis=-1, keepdims=True) / width + EPSILON)
    b_ref[...] = (m * scale * gain_ref[1:2]).astype(BF16)
    ct = own_or_other(place_ref, own_ref, other_ref)
    df_ref[...] = mm_tn(ct, e_ref[:width, :]).astype(BF16)


def middle(place, o, own, other, spread, unpack, w_out, xp, gain, block=512):
    width, half = own.shape
    seq, wide = 2 * half, spread.shape[1]
    rows = lambda n: pl.BlockSpec((block, n), lambda i, *_: (i, 0))
    return call(
        functools.partial(mid_body, width),
        [
            jax.ShapeDtypeStruct((seq, wide), BF16),
            jax.ShapeDtypeStruct((seq, wide), F32),
            jax.ShapeDtypeStruct((seq, wide), BF16),
            jax.ShapeDtypeStruct((seq, wide), BF16),
        ],
        (seq // block,),
        [
            pl.BlockSpec((HEADS, block, LANES), lambda i, *_: (0, i, 0)),
            *halves_specs(half, width, block),
            whole(spread.shape),
            whole(unpack.shape),
            whole(w_out.shape),
            rows(wide),
            whole((8, wide)),
        ],
        [rows(wide)] * 4,
        flops=2 * seq * wide * 4 * wide,
        moved=22_000_000,
        prefetch=1,
    )(place, o, own, other, spread, unpack, w_out, xp, gain)


def ffn_body(turn, place_ref, b_ref, df_ref, *refs):
    gates, ups, downs, refs = refs[:4], refs[4:8], refs[8:24], refs[24:]
    before, refs = refs[: 4 * turn], refs[4 * turn :]
    out_ref, db_ref, gu_ref, d_send, d_keep, wg_ref, wu_ref, wd_ref, down_sem, *carry = refs
    s = pl.program_id(0)
    core, z_me, y_me, x_me = (place_ref[n] for n in range(4))
    chunk = wg_ref.shape[1]
    half = core if turn else 1 - core
    rows = wd_ref.shape[0] // 8

    def carried(n):
        return pltpu.make_async_copy(before[2 + n], carry[n], carry[2 + n])

    def down_copies():
        for swapped in range(2):
            for q in range(2):
                for near in range(4):
                    for up_z in range(2):
                        k = lax.rem(z_me + 4 - (2 * half + up_z), 4)
                        block = up_z * 4 + (y_me ^ (near // 2)) * 2 + (x_me ^ (near % 2))
                        row = pl.multiple_of(rows * block, 16)
                        col = pl.multiple_of(2 * chunk * (core ^ swapped) + chunk * q, chunk)
                        ref = downs[8 * swapped + 4 * q + near]
                        yield pltpu.make_async_copy(
                            ref.at[k, pl.ds(ref.shape[1] - rows, rows), :],
                            wd_ref.at[pl.ds(row, rows), pl.ds(col, chunk)],
                            down_sem.at[16 * swapped + 8 * q + 2 * near + up_z],
                        )

    @pl.when(s == 0)
    def _():
        for copy in down_copies():
            copy.start()
        if turn:
            carried(0).start()
            carried(1).start()

    for near in range(4):
        for k in range(4):
            block = lax.rem(z_me + 4 - k, 4) * 4 + (y_me ^ (near // 2)) * 2 + (x_me ^ (near % 2))
            row = pl.multiple_of(block * 64, 64)
            wg_ref[pl.ds(row, 64), :] = gates[near][k]
            wu_ref[pl.ds(row, 64), :] = ups[near][k]

    b, df = b_ref[...], df_ref[...]
    wg, wu = wg_ref[...], wu_ref[...]
    gate = mm(b, wg)
    upper = mm(b, wu)

    @pl.when(s == 0)
    def _():
        for copy in down_copies():
            copy.wait()

    wd = wd_ref[pl.ds(pl.multiple_of(chunk * s, chunk), chunk), :]
    sig = jax.nn.sigmoid(gate)
    act = gate * sig
    z = (act * upper).astype(BF16)
    dz = mm_nt(df, wd)
    dg = (dz * upper * (sig + act * (1.0 - sig))).astype(BF16)
    du = (dz * act).astype(BF16)

    @pl.when(s == 0)
    def _():
        out_ref[...] = mm(z, wd)
        db_ref[...] = mm_nt(dg, wg) + mm_nt(du, wu)

    @pl.when(s > 0)
    def _():
        out_ref[...] += mm(z, wd)
        db_ref[...] += mm_nt(dg, wg) + mm_nt(du, wu)

    if turn:

        @pl.when(s == pl.num_programs(0) - 1)
        def _():
            carried(0).wait()
            carried(1).wait()
            out_ref[...] += carry[0][...]
            db_ref[...] += carry[1][...]

    gu_ref[:, :64] = mm_tn(b, dg).astype(BF16).reshape(gu_ref.shape[0], 64, chunk)
    gu_ref[:, 64:] = mm_tn(b, du).astype(BF16).reshape(gu_ref.shape[0], 64, chunk)
    side = df.shape[1] // 2
    for ref, j in ((d_send, 1 - core), (d_keep, core)):
        dwd = mm_tn(z, df_ref[:, pl.ds(pl.multiple_of(side * j, side), side)]).astype(BF16)
        ref[0] = dwd[:, :chunk]
        ref[1] = dwd[:, chunk:]


def feed_forward(place, b, df, mine, other, turn, before=()):
    seq, wide = b.shape
    blocks, chunks, chunk = 16, 5, 256
    columns = mine if turn else other
    any_spec = pl.BlockSpec(memory_space=pl.ANY)
    half_of = lambda place: place[0] if turn else 1 - place[0]
    d_shape = jax.ShapeDtypeStruct((2, 2 * chunks * chunk, chunk), BF16)
    d_spec = pl.BlockSpec((2, chunk, chunk), lambda s, place: (0, half_of(place) * chunks + s, 0))
    return call(
        functools.partial(ffn_body, turn),
        [
            jax.ShapeDtypeStruct((seq, wide), F32),
            jax.ShapeDtypeStruct((seq, wide), F32),
            jax.ShapeDtypeStruct((blocks, 128 * chunks, chunk), BF16),
            d_shape,
            d_shape,
        ],
        (chunks,),
        [whole(b.shape), whole(df.shape)]
        + [pl.BlockSpec((4, 64, chunk), lambda s, place: (0, s, 0))] * 8
        + [any_spec] * (16 + len(before)),
        [
            whole((seq, wide)),
            whole((seq, wide)),
            pl.BlockSpec((blocks, 128, chunk), lambda s, place: (0, s, 0)),
            d_spec,
            d_spec,
        ],
        scratch=[
            pltpu.VMEM((wide, chunk), BF16),
            pltpu.VMEM((wide, chunk), BF16),
            pltpu.VMEM((chunks * chunk, wide), BF16),
            pltpu.SemaphoreType.DMA((32,)),
        ]
        + turn * [pltpu.VMEM((seq, wide), F32)] * 2
        + turn * [pltpu.SemaphoreType.DMA] * 2,
        flops=18 * seq * wide * chunks * chunk,
        moved=40_000_000,
        prefetch=1,
        alias={27: 3, 28: 4} if before else None,
    )(place, b, df, *columns, *mine, *other, *before)


def token_block(steps):
    def at(i, place):
        return jnp.where(i < steps // 2, (1 - place[0]) * (steps // 2) + i, place[0] * (steps // 2) + i - steps // 2)

    return at


def token_specs(steps, block, width):
    half = steps // 2
    return [
        pl.BlockSpec((width, block), lambda i, place: (0, jnp.minimum(i, half - 1))),
        pl.BlockSpec((1, width, block), lambda i, place: (place[0], 0, jnp.maximum(i - half, 0))),
    ]


def put_tokens(send_ref, keep_ref, value):
    early = pl.program_id(0) < pl.num_programs(0) // 2

    @pl.when(early)
    def _():
        send_ref[...] = value.astype(send_ref.dtype)

    @pl.when(jnp.logical_not(early))
    def _():
        keep_ref[0] = value.astype(keep_ref.dtype)


def post_body(width, place_ref, m_ref, acc_ref, db_ref, df_ref, gain_ref, e_ref, u_ref,
              sum_ref, wo_ref, op_ref,
              send_ref, keep_ref, em_ref, do_ref, dwo_send, dwo_keep, dgain_ref, da_ref):
    i = pl.program_id(0)
    m, db = m_ref[...], db_ref[...]
    out = (m + acc_ref[...]).astype(BF16)
    put_tokens(send_ref, keep_ref, mm_nt(e_ref[:width, :], out))
    scale = lax.rsqrt(jnp.sum(m * m, axis=-1, keepdims=True) / width + EPSILON)
    n = m * scale
    c = db * gain_ref[1:2]
    mean = jnp.sum(c * n, axis=-1, keepdims=True) / width
    em = df_ref[...].astype(F32) + scale * (c - n * mean)
    em_ref[...] = em
    da = em.astype(BF16)
    dgain = jnp.sum(db * n, axis=0, keepdims=True)
    block = m.shape[0]
    late = pl.num_programs(0) // 2
    at = jnp.where(i < late, (1 - place_ref[0]) * late + i, place_ref[0] * late + i - late)
    rows = pl.ds(pl.multiple_of(block * at, block), block)
    da_ref[rows, :] = da

    @pl.when(i == 0)
    def _():
        dgain_ref[...] = dgain

    @pl.when(i > 0)
    def _():
        dgain_ref[...] += dgain

    do = mm_nt(da, wo_ref[...]).astype(BF16)
    product = do.astype(F32) * op_ref[rows, :].astype(F32)
    high = product.astype(BF16)
    low = (product - high.astype(F32)).astype(BF16)
    delta = mm(high, sum_ref[...]) + mm(low, sum_ref[...])
    full = jnp.concatenate([do] + [t.astype(BF16) for t in three_terms(delta)], axis=1)
    do = mm(full, u_ref[...]).astype(BF16)
    for head in range(HEADS):
        do_ref[head] = do[:, LANES * head : LANES * (head + 1)]

    @pl.when(i == pl.num_programs(0) - 1)
    def _():
        half = da_ref.shape[1] // 2
        for ref, j in ((dwo_send, 1 - place_ref[0]), (dwo_keep, place_ref[0])):
            dwo = mm_tn(op_ref[...], da_ref[:, pl.ds(pl.multiple_of(half * j, half), half)]).astype(BF16)
            for q in range(2):
                ref[q] = dwo[:, 256 * q : 256 * (q + 1)].reshape(ref.shape[1:])


def after(place, m, acc, db, df, gain, spread, unpack, delta_sum, w_out, op, width, block=512):
    seq, wide = m.shape
    blocks = 16
    steps = seq // block
    at = token_block(steps)
    rows = lambda n: pl.BlockSpec((block, n), lambda i, place: (at(i, place), 0))
    heads = pl.BlockSpec((HEADS, block, LANES), lambda i, place: (0, at(i, place), 0))
    dwo_shape = (2, blocks, wide // blocks, 256)
    consts = (gain, spread, unpack, delta_sum, w_out, op)
    return call(
        functools.partial(post_body, width),
        [
            jax.ShapeDtypeStruct((width, seq // 2), BF16),
            jax.ShapeDtypeStruct((2, width, seq // 2), BF16),
            jax.ShapeDtypeStruct((seq, wide), F32),
            jax.ShapeDtypeStruct((HEADS, seq, LANES), BF16),
            jax.ShapeDtypeStruct(dwo_shape, BF16),
            jax.ShapeDtypeStruct(dwo_shape, BF16),
            jax.ShapeDtypeStruct((1, wide), F32),
        ],
        (steps,),
        [rows(wide)] * 4 + [whole(t.shape) for t in consts],
        token_specs(steps, block, width)
        + [rows(wide), heads, whole(dwo_shape), whole(dwo_shape), whole((1, wide))],
        scratch=[pltpu.VMEM((seq, wide), BF16)],
        flops=2 * seq * wide * 6 * wide,
        moved=40_000_000,
        prefetch=1,
    )(place, m, acc, db, df, *consts)


def weights_body(place_ref, dq_ref, dk_ref, dv_ref, a_ref, w_ref, gain_ref,
                 dgain_ref, flat_ref, send_ref, keep_ref, dw_acc, part_ref, all_ref):
    i = pl.program_id(0)
    heads = HEADS + KV_HEADS

    pairs_to(flat_ref, lambda h: dq_ref[h] if h < HEADS else dk_ref[h - HEADS], heads)
    pairs_to(flat_ref, lambda h: dv_ref[h], KV_HEADS, heads * HEAD)
    block = flat_ref.shape[0]
    all_ref[pl.ds(pl.multiple_of(block * i, block), block), :] = flat_ref[...]

    @pl.when(i == pl.num_programs(0) - 1)
    def _():
        wide = dw_acc.shape[0]
        dw_acc[...] = mm_tn(a_ref[...], all_ref[...])
        total = jnp.sum(dw_acc[...] * w_ref[...].astype(F32), axis=-1, keepdims=True)
        column = lambda row: jnp.broadcast_to(row, (LANES, wide)).T
        gain = column(gain_ref[:1])
        attn = jnp.broadcast_to(total, (wide, LANES)) / jnp.where(gain == 0.0, 1.0, gain)
        lane = lane_of(wide)
        gains = jnp.where(lane == 32, attn, 0.0) + jnp.where(lane == 33, column(dgain_ref[...]), 0.0)
        n_q, n_k = HEADS * HEAD // 2, KV_HEADS * HEAD // 2
        for j in range(2):
            part_ref[:, 768:] = gains.astype(BF16)
            part_ref[:, :n_q] = dw_acc[:, n_q * j : n_q * (j + 1)].astype(BF16)
            for part in range(2):
                at, to = 2 * n_q + n_k * (2 * part + j), n_q + n_k * part
                part_ref[:, to : to + n_k] = dw_acc[:, at : at + n_k].astype(BF16)
            for ref, here in ((keep_ref, place_ref[0] == j), (send_ref, place_ref[0] != j)):

                @pl.when(here)
                def _():
                    ref[...] = part_ref[...].reshape(ref.shape)


def projections_back(place, parts, a, w_qkv, gain, dgain_ffn, block=256):
    seq, wide = a.shape
    blocks = 16
    rows = lambda n: pl.BlockSpec((block, n), lambda i, *_: (i, 0))
    heads = lambda t: pl.BlockSpec((t.shape[0], block, LANES), lambda i, *_: (0, i, 0))
    shape = (blocks, wide // blocks, 896)
    return call(
        weights_body,
        [
            jax.ShapeDtypeStruct((seq, QKV_PAD), BF16),
            jax.ShapeDtypeStruct(shape, BF16),
            jax.ShapeDtypeStruct(shape, BF16),
        ],
        (seq // block,),
        [heads(t) for t in parts] + [whole(a.shape), whole(w_qkv.shape), whole((8, wide)), whole((1, wide))],
        [rows(QKV_PAD), whole(shape), whole(shape)],
        scratch=[
            pltpu.VMEM((wide, QKV_PAD), F32),
            pltpu.VMEM((wide, 896), BF16),
            pltpu.VMEM((seq, QKV_PAD), BF16),
        ],
        flops=2 * seq * wide * QKV_PAD,
        moved=20_000_000,
        prefetch=1,
    )(place, *parts, a, w_qkv, gain, dgain_ffn)


def input_body(width, place_ref, flat_ref, w_ref, xp_ref, em_ref, gain_ref, e_ref, send_ref, keep_ref):
    da = mm_nt(flat_ref[...], w_ref[...])
    xp = xp_ref[...].astype(F32)
    scale = lax.rsqrt(jnp.sum(xp * xp, axis=-1, keepdims=True) / width + EPSILON)
    n = xp * scale
    c = da * gain_ref[:1]
    mean = jnp.sum(c * n, axis=-1, keepdims=True) / width
    grad = em_ref[...] + scale * (c - n * mean)
    put_tokens(send_ref, keep_ref, mm_nt(e_ref[:width, :], grad.astype(BF16)))


def input_back(place, flat, w_qkv, xp, em, gain, spread, width, block=512):
    seq, wide = xp.shape
    steps = seq // block
    at = token_block(steps)
    rows = lambda n: pl.BlockSpec((block, n), lambda i, place: (at(i, place), 0))
    return call(
        functools.partial(input_body, width),
        [
            jax.ShapeDtypeStruct((width, seq // 2), BF16),
            jax.ShapeDtypeStruct((2, width, seq // 2), F32),
        ],
        (steps,),
        [rows(QKV_PAD), whole(w_qkv.shape), rows(wide), rows(wide), whole((8, wide)), whole(spread.shape)],
        token_specs(steps, block, width),
        flops=2 * seq * wide * (QKV_PAD + 2 * width),
        moved=20_000_000,
        prefetch=1,
    )(place, flat, w_qkv, xp, em, gain, spread)


def begin_body(reader, n_in, place_ref, *refs):
    ins, outs = refs[:n_in], refs[n_in:]
    _, _, y, x = (place_ref[n] for n in range(4))
    for side in range(2):
        mine = y if side else x
        for other in range(2):
            for ref, bit in ((outs[2 * side], 1 - mine), (outs[2 * side + 1], mine)):
                block = 2 * bit + other if side else 2 * other + bit
                for row, keep, got in reader(ins, side, block):
                    ref[other, row : row + keep.shape[0]] = add(keep, got)


def begin(place, arrays, reader, rows, count=4):
    n = arrays[0].shape[-1]

    def spec(t):
        lead = t.shape[:-3]
        return pl.BlockSpec((*lead, 4, *t.shape[-2:]), lambda i, place: (0,) * len(lead) + (i, 0, 0))

    shape = jax.ShapeDtypeStruct((2 * count, rows, n), BF16)
    return call(
        functools.partial(begin_body, reader, len(arrays)),
        [shape] * 4,
        (count,),
        [spec(t) for t in arrays],
        [pl.BlockSpec((2, rows, n), lambda i, place: (i, 0, 0))] * 4,
        flops=1,
        moved=16 * count * rows * n * 6,
        prefetch=1,
        vmem=VMEM_SMALL,
    )(place, *arrays)


def turn_body(place_ref, *refs):
    y, x = place_ref[2], place_ref[3]
    for side in range(2):
        keep, got = refs[2 * side : 2 * side + 2]
        mine = x if side else y
        for ref, bit in ((refs[4 + 2 * side], 1 - mine), (refs[5 + 2 * side], mine)):
            ref[0] = add(keep[bit], got[bit])


def turn(place, keeps, gots):
    blocks, rows, n = keeps[0].shape
    shape = jax.ShapeDtypeStruct((blocks // 2, rows, n), BF16)
    return call(
        turn_body,
        [shape] * 4,
        (blocks // 2,),
        [pl.BlockSpec((2, rows, n), lambda i, place: (i, 0, 0))] * 4,
        [pl.BlockSpec((1, rows, n), lambda i, place: (i, 0, 0))] * 4,
        flops=1,
        moved=blocks * rows * n * 12,
        prefetch=1,
        vmem=VMEM_SMALL,
    )(place, keeps[0], gots[0], keeps[1], gots[1])


def climb_body(place_ref, a_keep, a_got, b_keep, b_got, total_ref, *sent):
    for step in range(4):
        block = lax.rem(place_ref[1] + step, 4)
        for side, (keep, got) in enumerate(((a_keep, a_got), (b_keep, b_got))):
            value = keep[block].astype(F32) + got[block].astype(F32)
            if step:
                sent[step - 1][side] = value.astype(BF16)
            else:
                total_ref[side] = value


def climb(place, keeps, gots):
    _, rows, n = keeps[0].shape
    return call(
        climb_body,
        [jax.ShapeDtypeStruct((2, rows, n), F32)] + [jax.ShapeDtypeStruct((2, rows, n), BF16)] * 3,
        (1,),
        [whole(keeps[0].shape)] * 4,
        [whole((2, rows, n))] * 4,
        flops=1,
        moved=rows * n * 50,
        prefetch=1,
        vmem=VMEM_SMALL,
    )(place, keeps[0], gots[0], keeps[1], gots[1])


def unpack_matrix(width, blocks, wide):
    per, step = width // blocks, wide // blocks
    col = jnp.arange(WIDE_HEADS, dtype=jnp.int32)
    feature = col // LANES * HEAD + col % LANES
    place = jnp.where(col % LANES < HEAD, feature // per * step + feature % per, -1)
    term = col % LANES - HEAD
    place = jnp.where((term >= 0) & (term < 3), wide + term * LANES + col // LANES, place)
    return (jnp.arange(wide + 3 * LANES, dtype=jnp.int32)[:, None] == place[None, :]).astype(BF16)


def delta_matrix(width, blocks, wide):
    per, step = width // blocks, wide // blocks
    row = jnp.arange(wide, dtype=jnp.int32)
    head = jnp.where(row % step < per, (row // step * per + row % step) // HEAD, -1)
    return (head[:, None] == jnp.arange(LANES, dtype=jnp.int32)[None, :]).astype(BF16)


def spread_matrix(width, blocks, wide):
    row = jnp.arange(wide, dtype=jnp.int32)
    per, step = width // blocks, wide // blocks
    place = (row // per) * step + row % per
    hit = (place[:, None] == jnp.arange(wide, dtype=jnp.int32)[None, :]) & (row < width)[:, None]
    return hit.astype(BF16)


def tables(positions, segments):
    lane = jnp.arange(LANES, dtype=jnp.int32)
    frequency = 10000.0 ** (-((lane % 32).astype(F32) * 2.0 / HEAD))
    angles = positions.astype(F32)[:, None] * frequency[None, :]
    cos, sin = jnp.cos(angles), jnp.sin(angles)
    high = (lane % HEAD >= 32)[None, :]
    sa = jnp.where(high, sin, 0.0)
    sb = jnp.where(high, 0.0, -sin)
    doc = (lane - HEAD)[None, :]
    mine = segments[:, None] == doc
    in_doc = (doc >= 0) & (doc < DOCS)
    aq = jnp.where(mine & in_doc, MASKED, 0.0)
    ak = jnp.where(in_doc & ~mine, 1.0, 0.0)
    ak = jnp.where((doc >= DOCS) & (doc < DOCS + 3), -1.0, ak)
    return cos, sa, sb, aq, ak


def pad_rows(w, blocks, step=64):
    per = w.shape[0] // blocks
    return jnp.pad(w.reshape(blocks, per, w.shape[1]), ((0, 0), (0, step - per), (0, 0)))


def pad_cols(w, blocks, step=64):
    per = w.shape[1] // blocks
    w = jnp.pad(w.reshape(w.shape[0], blocks, per), ((0, 0), (0, 0), (0, step - per)))
    return w.reshape(w.shape[0], blocks * step)


def cut_rows(w, per):
    return w[:, :per].reshape(w.shape[0] * per, w.shape[2])


def cut_cols(w, per, step=64):
    blocks = w.shape[1] // step
    return w.reshape(w.shape[0], blocks, step)[:, :, :per].reshape(w.shape[0], blocks * per)


def chunked(w, chunk=256):
    blocks, rows, cols = w.shape
    w = w.reshape(blocks, rows, cols // chunk, chunk).transpose(0, 2, 1, 3)
    return w.reshape(blocks, cols // chunk * rows, chunk)


def joined(w, rows):
    blocks, total, chunk = w.shape
    w = w.reshape(blocks, total // rows, rows, chunk).transpose(0, 2, 1, 3)
    return w.reshape(blocks, rows, total // rows * chunk)


def pack_half(w_gate, w_up, w_down, blocks, groups):
    down = pad_cols(w_down, groups)
    down = down.reshape(blocks, w_down.shape[0] // blocks, down.shape[1])
    gate, upper = chunked(pad_rows(w_gate, blocks)), chunked(pad_rows(w_up, blocks))
    return jnp.concatenate([gate, down[:, :, :256], upper, down[:, :, 256:]], axis=1)


def add(left, right):
    return (left.astype(F32) + right.astype(F32)).astype(BF16)


def swap(x):
    return lax.ppermute(x, "ctx", [(0, 1), (1, 0)])


def across(x, bit, count):
    return lax.ppermute(x, "dp", [(i, i ^ (1 << bit)) for i in range(count)])


def pick(x, index, axis=0):
    return lax.dynamic_index_in_dim(x, index, axis, keepdims=False)


def tie(value, *others):
    return lax.optimization_barrier((value, *others))[0]


def tie_all(values, *others):
    return lax.optimization_barrier((*values, *others))[: len(values)]


def along_z(x, step, count):
    return lax.ppermute(x, "dp", [(i, (i + 4 * step) % count) for i in range(count)])


def rise(x, count):
    return [x] + [along_z(x, k, count) for k in (1, 2, 3)]


def spread_first(stack, count):
    half = stack.shape[1] // 2
    first, second = stack[:, :half], stack[:, half:]
    return first, across(first, 0, count), second, across(second, 1, count)


def spread_second(first, first_got, second, second_got, count):
    first, second = jnp.concatenate([first, first_got]), jnp.concatenate([second, second_got])
    return first, across(first, 1, count), second, across(second, 0, count)


def pieces_of(whole_one):
    n = whole_one.shape[1] // 2
    cube = whole_one.reshape(4, 2, 2, 2 * n, -1)
    cube = jnp.stack([cube[(4 - k) % 4] for k in range(4)])
    first, second = cube[:, :, :, :n], cube[:, :, :, n:]
    first, second = first.transpose(1, 2, 0, 3, 4), second.transpose(2, 1, 0, 3, 4)
    flat = lambda t: t.reshape(8, n, -1)
    return flat(first[0]), flat(first[1]), flat(second[0]), flat(second[1])


def fine_pieces_of(whole_one):
    n = whole_one.shape[1] // 2
    cube = whole_one.reshape(4, 2, 2, 2 * n, -1)
    cube = jnp.stack([cube[(4 - k) % 4] for k in range(4)])
    near = [cube[:, dy, dx] for dy in range(2) for dx in range(2)]
    return [t[:, :n] for t in near] + [t[:, n:] for t in near]


class RowSum:
    def __init__(self, place, count, arrays, reader, rows):
        self.place, self.count = place, count
        a_sent, a_kept, b_sent, b_kept = begin(place, arrays, reader, rows)
        self.sent, self.kept = [a_sent, b_sent], [a_kept, b_kept]

    def move(self):
        self.got = [across(self.sent[0], 0, self.count), across(self.sent[1], 1, self.count)]

    def wait(self, other):
        self.got = list(lax.optimization_barrier((*self.got, other))[:-1])

    def turn(self, other):
        self.wait(other)
        a_sent, a_kept, b_sent, b_kept = turn(self.place, self.kept, self.got)
        self.sent, self.kept = [a_sent, b_sent], [a_kept, b_kept]

    def move_again(self):
        self.got = [across(self.sent[0], 1, self.count), across(self.sent[1], 0, self.count)]

    def climb(self, other):
        self.wait(other)
        self.kept, *self.sent = climb(self.place, self.kept, self.got)

    def start_up(self):
        return along_z(self.sent[1], 1, self.count)

    def start_down(self):
        return along_z(self.sent[2], 3, self.count)

    def go_up(self, got):
        return along_z(add(self.sent[0], got), 1, self.count)

    def move_up(self):
        return [along_z(self.sent[k - 1], k, self.count) for k in (1, 2, 3)]

    def total(self, *gots):
        total = self.kept
        for got in gots:
            total = total + got.astype(F32)
        return total


def read_rows(ins, side, block):
    half = ins[0].shape[1] // 2
    rows = slice(half * side, half * (side + 1))
    return [(0, ins[0][block, rows], ins[1][block, rows])]


def read_quarters(ins, side, block):
    first = ins[0].shape[2]
    return [(0, ins[0][side, block], ins[1][side, block]), (first, ins[2][side, block], ins[3][side, block])]


def put_other(both, got, core):
    return lax.dynamic_update_slice(both, got[None], (1 - core, 0, 0))


def shards_of_two(inputs, segment_ids, positions, w_query, w_key, w_value, w_out, w_gate, w_up,
                  w_down, gain_attn, gain_ffn, cotangent):
    count = lax.axis_size("dp")
    me, core = lax.axis_index("dp"), lax.axis_index("ctx")
    place = (core, me // 4, (me >> 1) & 1, me & 1)
    place_of = jnp.stack(place).astype(jnp.int32)
    per = gain_attn.shape[0]
    width = per * count
    groups = w_out.shape[1] // per
    hidden = w_down.shape[0]
    n_q, n_k = w_query.shape[1], w_key.shape[1]
    n_qkv = n_q + 2 * n_k

    shard = jnp.concatenate(
        [w_query, w_key, w_value, gain_attn[:, None], gain_ffn[:, None]], axis=1
    )
    shard = jnp.pad(shard, ((0, 0), (0, 896 - n_qkv - 2)))
    shard = jnp.concatenate([shard, pad_cols(w_out, groups)], axis=1)
    shard = jnp.pad(shard, ((0, 64 - per), (0, 0)))
    packed = pack_half(w_gate, w_up, w_down, 1, groups)[0]
    wide = count * 64
    spread, unpack = spread_matrix(width, count, wide), unpack_matrix(width, count, wide)
    delta_sum = delta_matrix(width, count, wide)
    table = tables(pick(positions[:, 0], core), pick(segment_ids[:, 0], core))

    level = rise(shard, count)
    stack = tie(jnp.stack(level), spread, unpack, delta_sum, *table)
    part = spread_first(stack, count)
    packed = tie(packed, stack)
    up = along_z(packed, 1, count)
    part = tie_all(part, up)
    near_far = spread_second(*part, count)
    up = tie(up, part[0])
    up_two, down = along_z(up, 1, count), along_z(packed, 3, count)
    near_far = tie_all(near_far, up_two, down)
    pieces = near_far + tuple(swap(t) for t in near_far)
    packs = jnp.stack(tie_all((packed, up, up_two, down), near_far[0]))
    half = packs.shape[1] // 2
    a00, b00 = packs[:, :half], packs[:, half:]
    a01, b10 = across(a00, 0, count), across(b00, 1, count)

    def halves(x):
        x = jnp.swapaxes(x[:, 0], 1, 2)
        return pick(x, core), swap(pick(x, 1 - core))

    x_own, x_other = halves(inputs)
    ct_own, ct_other = halves(cotangent)
    pieces = tie_all(pieces, a00, b00)
    xp, a, q, k, v, w_qkv, w_o, gains = pre_attention(place_of, x_own, x_other, spread, pieces, *table)
    a01, b10, ct_other, a00, b00 = tie_all((a01, b10, ct_other, a00, b00), q)
    a10, b01 = across(a00, 1, count), across(b00, 0, count)
    got = [swap(a00), swap(b00), swap(a01)]
    q = tie(q, a01, b10, ct_other)
    o, q2 = attend(q, k, v)
    a10, b01, *got = tie_all((a10, b01, *got), o)
    a11, b11 = across(tie(a01, a10), 1, count), across(tie(b10, a10), 0, count)
    got += [swap(b10), swap(a10), swap(b01)]
    op, m, b, df = middle(
        place_of, tie(o, a10, b01, *got[:3]), ct_own, ct_other, spread, unpack, w_o, xp, gains
    )
    a11, b11, *got = tie_all((a11, b11, *got), b)
    mine = [a00, a01, a10, a11, b00, b01, b10, b11]
    other = [got[0], got[2], got[4], swap(a11), got[1], got[5], got[3], swap(b11)]

    acc0, db0, gu_send, d_send, d_keep = feed_forward(place_of, b, df, mine, other, 0)
    gu_got = swap(gu_send)
    acc, db, gu_keep, d_send, d_keep = feed_forward(
        place_of, tie(b, gu_send), df, mine, other, 1, (d_send, d_keep, acc0, db0)
    )
    one = RowSum(place_of, count, (gu_keep, tie(gu_got, acc)), read_rows, 320)
    one.move()
    blocked = lambda t: t.reshape(2, count, hidden, 256)
    d_got = swap(d_send)
    m = tie(m, *one.sent, d_send)
    out_send, outs, em, do, o_send, o_keep, dgf = after(
        place_of, m, acc, db, df, gains, spread, unpack, delta_sum, w_o, op, width
    )
    o_got = swap(o_send)
    one.turn(em)
    one.move_again()
    two = RowSum(
        place_of, count, (blocked(d_keep), blocked(tie(d_got, em)), o_keep, o_got), read_quarters, 224
    )
    two.move()
    do = tie(do, *one.sent, *two.sent)
    parts = attend_back(q2, k, v, do, *table[:3], 0, KV_HEADS)
    outs = put_other(outs, tie(swap(out_send), parts[0]), core)
    one.climb(parts[0])
    up, down = one.start_up(), one.start_down()
    two.turn(parts[0])
    two.move_again()
    a = tie(a, *one.sent, *two.sent)
    flat, p_send, p_keep = projections_back(place_of, parts, a, w_qkv, gains, dgf)
    up, down, *two.got = tie_all((up, down, *two.got), flat)
    p_got = swap(tie(p_send, up))
    two.climb(flat)
    one_up, one_down, two_up = one.go_up(up), down, two.start_up()
    three = RowSum(place_of, count, (p_keep, p_got), read_rows, 32)
    three.move()
    flat = tie(flat, *two.sent, *three.sent)
    gi_send, gis = input_back(place_of, flat, w_qkv, xp, em, gains, spread, width)
    *three.got, one_up, two_up = tie_all((*three.got, one_up, two_up), gis)
    gi_got = swap(tie(gi_send, one_up))
    three.turn(one_up)
    three.move_again()
    two_up, two_down = two.go_up(two_up), two.start_down()
    gis = put_other(gis, gi_got.astype(F32), core)
    first = one.total(one_up, one_down)
    three.climb(first)
    last_got = three.move_up()
    second, third = two.total(two_up, two_down), three.total(*last_got)
    third = third.reshape(64, 896)[:per]
    gu = first.reshape(5, 2, 64, 256)
    wide_of = lambda t: t.transpose(1, 0, 2).reshape(t.shape[1], -1)
    tokens = lambda t: jnp.swapaxes(t, 1, 2)[:, None]
    return (
        tokens(outs),
        tokens(gis),
        third[:, :n_q],
        third[:, n_q : n_q + n_k],
        third[:, n_q + n_k : n_qkv],
        cut_cols(wide_of(second[:, 160:])[:per], per),
        wide_of(gu[:, 0])[:per],
        wide_of(gu[:, 1])[:per],
        cut_cols(wide_of(second[:, :160]), per),
        third[:, n_qkv],
        third[:, n_qkv + 1],
    )


def shards_of_many(inputs, segment_ids, positions, w_query, w_key, w_value, w_out, w_gate, w_up,
                   w_down, gain_attn, gain_ffn, cotangent):
    count, cores = lax.axis_size("dp"), lax.axis_size("ctx")
    core = lax.axis_index("ctx")
    share = cores // MICRO
    per = gain_attn.shape[0]
    width = per * count

    def gathered(w):
        return lax.all_gather(lax.all_gather(w, "dp", axis=0, tiled=True), "ctx", axis=1, tiled=True)

    full = [gathered(w) for w in (w_query, w_key, w_value, w_out, w_gate, w_up, w_down)]
    gain_pair = lax.all_gather(jnp.stack([gain_attn, gain_ffn]), "dp", axis=1, tiled=True)
    w_o, w_g, w_u, w_d = full[3:]
    half = lambda w, j: w[:, w.shape[1] // 2 * j : w.shape[1] // 2 * (j + 1)]
    packs = [pack_half(half(w_g, j), half(w_u, j), half(w_d, j), count, count // 2) for j in range(2)]
    mine, other = (fine_pieces_of(p) for p in packs)
    pieces = []
    for j in range(2):
        parts = [half(w, j) for w in full[:3]] + [gain_pair.T]
        part = jnp.concatenate(parts, axis=1)
        part = jnp.pad(part, ((0, 0), (0, 896 - part.shape[1])))
        part = jnp.concatenate([part, pad_cols(half(w_o, j), count // 2)], axis=1)
        pieces += pieces_of(pad_rows(part, count))
    which = core // share

    def sequence(x):
        whole_one = pick(lax.all_gather(x[:, 0], "ctx", axis=1, tiled=True), which).T
        return whole_one[:, : whole_one.shape[1] // 2], whole_one[:, whole_one.shape[1] // 2 :]

    place = jnp.zeros((4,), jnp.int32)
    wide = count * 64
    spread, unpack = spread_matrix(width, count, wide), unpack_matrix(width, count, wide)
    delta_sum = delta_matrix(width, count, wide)
    cos, sa, sb, aq, ak = tables(pick(positions[:, 0], which), pick(segment_ids[:, 0], which))
    xp, a, q, k, v, w_qkv, w_o, gains = pre_attention(
        place, *sequence(inputs), spread, pieces, cos, sa, sb, aq, ak
    )
    o, q2 = attend(q, k, v)
    op, m, b, df = middle(place, o, *sequence(cotangent), spread, unpack, w_o, xp, gains)
    acc0, db0, gu_send, d_send, d_keep = feed_forward(place, b, df, mine, other, 0)
    acc, db, gu_keep, d_send, d_keep = feed_forward(
        place, b, df, mine, other, 1, (d_send, d_keep, acc0, db0)
    )
    out_send, outs, em, do, o_send, o_keep, dgf = after(
        place, m, acc, db, df, gains, spread, unpack, delta_sum, w_o, op, width
    )
    parts = attend_back(q2, k, v, do, cos, sa, sb, 0, KV_HEADS)
    flat, p_send, p_keep = projections_back(place, parts, a, w_qkv, gains, dgf)
    gi_send, gis = input_back(place, flat, w_qkv, xp, em, gains, spread, width)

    parts = [cut_rows(p, per) for p in (p_keep, p_send)]
    n_q, n_k = HEADS * HEAD // 2, KV_HEADS * HEAD // 2
    both = lambda at, n: jnp.concatenate([p[:, at : at + n] for p in parts], axis=1)
    side = lambda t: jnp.concatenate([t[0], t[1]], axis=-1)

    def wide_of(index):
        every = []
        for t in (gu_keep, gu_send):
            t = t.reshape(count, 5, 2, 64, 256)[:, :, index]
            every.append(cut_rows(t.transpose(0, 2, 1, 3).reshape(count, 64, -1), per))
        return jnp.concatenate(every, axis=1)

    grads = [
        both(0, n_q),
        both(n_q * 1, n_k),
        both(n_q + n_k, n_k),
        cut_cols(cut_rows(jnp.concatenate([side(o_keep), side(o_send)], axis=-1), per), per),
        wide_of(0),
        wide_of(1),
        cut_cols(
            jnp.concatenate([side(d_keep), side(d_send)], axis=-1),
            per,
        ),
    ]

    def summed(g):
        g = lax.psum_scatter(g * (1.0 / share), "dp", scatter_dimension=0, tiled=True)
        return lax.psum_scatter(g, "ctx", scatter_dimension=1, tiled=True).astype(F32)

    sums = [summed(g.astype(BF16)) for g in grads]
    dgain = parts[0][:, 2 * n_k + n_q : 2 * n_k + n_q + 2].astype(F32).T * (1.0 / share)
    dgain = lax.psum_scatter(lax.psum(dgain, "ctx"), "dp", scatter_dimension=1, tiled=True)

    def tokens(seq):
        rows = seq.shape[0] // cores
        every = lax.all_gather(seq, "ctx", axis=0, tiled=False)
        return lax.dynamic_slice_in_dim(every[::share], core * rows, rows, axis=1)[:, None]

    out = jnp.concatenate([outs[0], out_send], axis=1).T
    gi = jnp.concatenate([gis[0], gi_send.astype(F32)], axis=1).T
    return (tokens(out), tokens(gi), *sums, dgain[0], dgain[1])


def solution(mesh):
    two = mesh.shape["ctx"] == MICRO and mesh.shape["dp"] == 16
    matrices = (P("dp", "ctx"),) * 7 + (P("dp"), P("dp"))
    tokens = P(None, "dp", "ctx", None)
    return jax.shard_map(
        shards_of_two if two else shards_of_many,
        mesh=mesh,
        in_specs=(tokens, P(None, "dp", None), P(None, "dp", None)) + matrices + (tokens,),
        out_specs=(tokens, tokens) + matrices,
        check_vma=False,
    )
```

profile of v0, /device:TPU:0, one launch (start us, length us, event | category | flops | bytes accessed | tf_op | source)
XLA Modules:
  0.0 409.8 jit_solution(8494656808274764931)
XLA Ops:
  4.5 4.1 %collective-permute-start.2 = (bf16[64,1408]{1,0:T(8,128)(2,1)S(1)}, bf16[64,1408]{1,0:T(8,128)(2,1)S(1)}, u32[]{:S(2)}, u32[]{:S(2)}) collective-permute-start(bf16[64,1408]{1,0:T(8,128)(2,1)S(1)} %get-tuple-element.348), channel_id=1, source_target_pairs={{0,16},{2,18},{4,20},{6,22},{8,24},{10,26},{12,28},{14,30},{16,0},... | collective-permute-start | bytes 540680 | tf_op jit(solution)/shard_map/ppermute | solution.py:871
  14.6 4.7 %fusion.u_ref = bf16[1408,1920]{1,0:T(8,128)(2,1)} fusion(s32[1920]{0:T(1024)S(1)} %fusion.20), kind=kLoop, calls=%fused_computation.1 | loop fusion | flops 5406720 | bytes 5414400 | tf_op jit(solution)/shard_map/convert_element_type | solution.py:772
  21.3 3.2 fusion.5
  30.0 6.3 %collective-permute-done.5 = bf16[4,32,1408]{2,1,0:T(8,128)(2,1)S(1)} collective-permute-done((bf16[4,32,1408]{2,1,0:T(8,128)(2,1)S(1)}, bf16[4,32,1408]{2,1,0:T(8,128)(2,1)S(1)}, u32[]{:S(2)}, u32[]{:S(2)}) %collective-permute-start.5) | collective-permute-done | bytes 360480 | tf_op jit(solution)/shard_map/ppermute | solution.py:855
  37.6 3.2 collective-permute-done.6
  49.4 10.2 %collective-permute-done.10 = bf16[960,256]{1,0:T(8,128)(2,1)S(1)} collective-permute-done((bf16[960,256]{1,0:T(8,128)(2,1)S(1)}, bf16[960,256]{1,0:T(8,128)(2,1)S(1)}, u32[]{:S(2)}, u32[]{:S(2)}) %collective-permute-start.10) | collective-permute-done | bytes 491552 | tf_op jit(solution)/shard_map/ppermute | solution.py:871
  59.6 9.1 %collective-permute-done.9 = bf16[960,256]{1,0:T(8,128)(2,1)} collective-permute-done((bf16[960,256]{1,0:T(8,128)(2,1)S(1)}, bf16[960,256]{1,0:T(8,128)(2,1)}, u32[]{:S(2)}, u32[]{:S(2)}) %collective-permute-start.9) | collective-permute-done | bytes 491552 | tf_op jit(solution)/shard_map/ppermute | solution.py:871
  77.7 18.2 %shard_map.212 = (bf16[1024,1024]{1,0:T(8,128)(2,1)}, bf16[1024,1024]{1,0:T(8,128)(2,1)}, bf16[15,1024,128]{2,1,0:T(8,128)(2,1)}, bf16[5,1024,128]{2,1,0:T(8,128...) custom-call(s32[4]{0:T(128)} %pad_add_fusion.place_ref, ...), custom_call_target="tpu_custom_call" | custom-call | flops 5502926848 | bytes 20000000 | tf_op jit(solution)/shard_map/pallas_call | solution.py:166
  95.9 4.4 %collective-permute-done.16.refs_14_.refs_6_ = bf16[4,480,256]{2,1,0:T(8,128)(2,1)} collective-permute-done((bf16[4,480,256]{2,1,0:T(8,128)(2,1)S(1)}, bf16[4,480,256]{2,1,0:T(8,128)(2,1)}, u32[]{:S(2)}, u32[]{:S(2)}) %collective-permute-start.16) | collective-permute-done | bytes 983072 | tf_op jit(solution)/shard_map/ppermute | solution.py:855
  103.0 24.9 %shard_map.213 = (bf16[15,1024,128]{2,1,0:T(8,128)(2,1)}, bf16[15,1024,128]{2,1,0:T(8,128)(2,1)}) custom-call(bf16[15,1024,128]{2,1,0:T(8,128)(2,1)} %get-tuple-element.188.q_ref, bf16[5,1024,128]{2,1,0:T(8,128)(2,1)} %get-tuple-element.189.k_ref, bf16[5,1024,128]{2,1,0:T(8,128)(2,1)} %get-tuple-element.190.v_ref), custom_call_target="tpu_custom_call" | custom-call | flops 8053063680 | bytes 15000000 | tf_op jit(solution)/shard_map/pallas_call | solution.py:224
  131.1 16.7 %shard_map.214 = (bf16[1024,1024]{1,0:T(8,128)(2,1)}, f32[1024,1024]{1,0:T(8,128)}, bf16[1024,1024]{1,0:T(8,128)(2,1)}, bf16[1024,1024]{1,0:T(8,128)(2,1)}) custom-call(s32[4]{0:T(128)} %pad_add_fusion.place_ref, bf16[15,1024,128]{2,1,0:T(8,128)(2,1)} %get-tuple-element.199.o_ref, bf16[960,512]{1,0:T(8,128)(2,1)} %get-tuple-element.335.own_ref, ...), custom_call_target="tpu_custom_call" | custom-call | flops 8589934592 | bytes 22000000 | tf_op jit(solution)/shard_map/pallas_call | solution.py:325
  147.9 4.6 %collective-permute-done.23.refs_11_.refs_3_ = bf16[4,480,256]{2,1,0:T(8,128)(2,1)S(1)} collective-permute-done((bf16[4,480,256]{2,1,0:T(8,128)(2,1)}, bf16[4,480,256]{2,1,0:T(8,128)(2,1)S(1)}, u32[]{:S(2)}, u32[]{:S(2)}) %collective-permute-start.23) | collective-permute-done | bytes 983072 | tf_op jit(solution)/shard_map/ppermute | solution.py:855
  158.0 41.5 %shard_map.215 = (f32[1024,1024]{1,0:T(8,128)}, f32[1024,1024]{1,0:T(8,128)}, bf16[16,640,256]{2,1,0:T(8,128)(2,1)}, bf16[2,2560,256]{2,1,0:T(8,128)(2,1)}, bf16[2,2560,256]{2,1,0:T(8,128)(2,1)}) custom-call(s32[4]{0:T(128)} %pad_add_fusion.place_ref, bf16[1024,1024]{1,0:T(8,128)(2,1)} %get-tuple-element.217.b_ref, ...), custom_call_target="tpu_custom_call" | custom-call | flops 24159191040 | bytes 40000000 | tf_op jit(solution)/shard_map/pallas_call | solution.py:448
  199.7 42.8 %shard_map.216 = (f32[1024,1024]{1,0:T(8,128)}, f32[1024,1024]{1,0:T(8,128)}, bf16[16,640,256]{2,1,0:T(8,128)(2,1)}, bf16[2,2560,256]{2,1,0:T(8,128)(2,1)}, bf16[2,2560,256]{2,1,0:T(8,128)(2,1)}) custom-call(s32[4]{0:T(128)} %pad_add_fusion.place_ref, bf16[1024,1024]{1,0:T(8,128)(2,1)} %get-tuple-element.217.b_ref, ...), custom_call_target="tpu_custom_call", output_to_operand_aliasing={{3}: (27, {}), {4}: (28, {})} | custom-call | flops 24159191040 | bytes 40000000 | tf_op jit(solution)/shard_map/pallas_call | solution.py:448
  245.4 3.1 shard_map.217
  253.7 31.1 %shard_map.218 = (bf16[960,512]{1,0:T(8,128)(2,1)}, bf16[2,960,512]{2,1,0:T(8,128)(2,1)}, f32[1024,1024]{1,0:T(8,128)}, bf16[15,1024,128]{2,1,0:T(8,128)(2,1)}, ...) custom-call(s32[4]{0:T(128)} %pad_add_fusion.place_ref, ...), custom_call_target="tpu_custom_call" | custom-call | flops 12884901888 | bytes 40000000 | tf_op jit(solution)/shard_map/pallas_call | solution.py:567
  288.9 3.0 shard_map.220
  299.2 35.8 %shard_map.221 = (bf16[15,1024,128]{2,1,0:T(8,128)(2,1)}, bf16[5,1024,128]{2,1,0:T(8,128)(2,1)}, bf16[5,1024,128]{2,1,0:T(8,128)(2,1)}) custom-call(bf16[15,1024,128]{2,1,0:T(8,128)(2,1)} %get-tuple-element.233.q_ref, bf16[5,1024,128]{2,1,0:T(8,128)(2,1)} %get-tuple-element.189.k_ref, bf16[5,1024,128]{2,1,0:T(8,128)(2,1)} %get-tuple-element.190.v_ref, ...), custom_call_target="tpu_custom_call" | custom-call | flops 20132659200 | bytes 20000000 | tf_op jit(solution)/shard_map/pallas_call | solution.py:283
  339.9 3.2 collective-permute-start.41
  343.0 14.6 %shard_map.224 = (bf16[1024,1664]{1,0:T(8,128)(2,1)}, bf16[16,64,896]{2,1,0:T(8,128)(2,1)}, bf16[16,64,896]{2,1,0:T(8,128)(2,1)}) custom-call(s32[4]{0:T(128)} %pad_add_fusion.place_ref, bf16[15,1024,128]{2,1,0:T(8,128)(2,1)} %get-tuple-element.249.dq_ref, bf16[5,1024,128]{2,1,0:T(8,128)(2,1)} %get-tuple-element.251.dk_ref, ...), custom_call_target="tpu_custom_call" | custom-call | flops 3489660928 | bytes 20000000 | tf_op jit(solution)/shard_map/pallas_call | solution.py:629
  358.2 4.9 %collective-permute-done.31 = bf16[960,512]{1,0:T(8,128)(2,1)S(1)} collective-permute-done((bf16[960,512]{1,0:T(8,128)(2,1)}, bf16[960,512]{1,0:T(8,128)(2,1)S(1)}, u32[]{:S(2)}, u32[]{:S(2)}) %collective-permute-start.31) | collective-permute-done | bytes 983072 | tf_op jit(solution)/shard_map/ppermute | solution.py:851
  364.5 3.4 collective-permute-start.56
  372.2 14.2 %shard_map.227 = (bf16[960,512]{1,0:T(8,128)(2,1)}, f32[2,960,512]{2,1,0:T(8,128)}) custom-call(s32[4]{0:T(128)} %pad_add_fusion.place_ref, bf16[1024,1664]{1,0:T(8,128)(2,1)} %get-tuple-element.286.flat_ref, bf16[1024,1664]{1,0:T(8,128)(2,1)} %get-tuple-element.268.w_ref, bf16[1024,1024]{1,0:T(8,128)(2,1)} %get-tuple-element.201.xp_ref, ...), custom_call_target="tpu_custom_call" | custom-call | flops 7516192768 | bytes 20000000 | tf_op jit(solution)/shard_map/pallas_call | solution.py:666
  395.3 3.7 collective-permute-start.53
  (259 shorter events, 97.5 us)
Async XLA Ops:
  4.5 22.2 %collective-permute-start.2 = (bf16[64,1408]{1,0:T(8,128)(2,1)S(1)}, bf16[64,1408]{1,0:T(8,128)(2,1)S(1)}, u32[]{:S(2)}, u32[]{:S(2)}) collective-permute-start(bf16[64,1408]{1,0:T(8,128)(2,1)S(1)} %get-tuple-element.348), channel_id=1, source_target_pairs={{0,16},{2,18},{4,20},{6,22},{8,24},{10,26},{12,28},{14,30},{16,0},... | collective-permute-start | bytes 540680 | tf_op jit(solution)/shard_map/ppermute | solution.py:871
  43.2 25.5 %collective-permute-start.7 = (bf16[8,32,1408]{2,1,0:T(8,128)(2,1)}, bf16[8,32,1408]{2,1,0:T(8,128)(2,1)}, u32[]{:S(2)}, u32[]{:S(2)}) collective-permute-start(bf16[8,32,1408]{2,1,0:T(8,128)(2,1)} %constant_dynamic-update-slice_fusion.refs_0_), channel_id=1, source_target_pairs={{0,4},{2,6},{4,0},{6,2},{8,12},{10,14},{12,8},{14,10},{16,20},{18,... | collective-permute-start | bytes 2162696 | tf_op jit(solution)/shard_map/ppermute | solution.py:855
  45.5 23.2 %collective-permute-start.8 = (bf16[8,32,1408]{2,1,0:T(8,128)(2,1)}, bf16[8,32,1408]{2,1,0:T(8,128)(2,1)}, u32[]{:S(2)}, u32[]{:S(2)}) collective-permute-start(bf16[8,32,1408]{2,1,0:T(8,128)(2,1)} %constant_dynamic-update-slice_fusion.2.refs_2_), channel_id=1, source_target_pairs={{0,2},{2,0},{4,6},{6,4},{8,10},{10,8},{12,14},{14,12},{16,18},{18,... | collective-permute-start | bytes 2162696 | tf_op jit(solution)/shard_map/ppermute | solution.py:855
  76.0 24.2 %collective-permute-start.16 = (bf16[4,480,256]{2,1,0:T(8,128)(2,1)S(1)}, bf16[4,480,256]{2,1,0:T(8,128)(2,1)}, u32[]{:S(2)}, u32[]{:S(2)}) collective-permute-start(bf16[4,480,256]{2,1,0:T(8,128)(2,1)S(1)} %get-tuple-element.193.refs_12_.refs_4_), channel_id=1, source_target_pairs={{0,4},{2,6},{4,0},{6,2},{8,12},{10,14},{12,8},{14,10},{16,20},{18,... | collective-permute-start | bytes 2949128 | tf_op jit(solution)/shard_map/ppermute | solution.py:855
  76.6 24.1 %collective-permute-start.15 = (bf16[4,480,256]{2,1,0:T(8,128)(2,1)}, bf16[4,480,256]{2,1,0:T(8,128)(2,1)}, u32[]{:S(2)}, u32[]{:S(2)}) collective-permute-start(bf16[4,480,256]{2,1,0:T(8,128)(2,1)} %get-tuple-element.192.refs_8_.refs_0_), channel_id=1, source_target_pairs={{0,2},{2,0},{4,6},{6,4},{8,10},{10,8},{12,14},{14,12},{16,18},{18,... | collective-permute-start | bytes 2949128 | tf_op jit(solution)/shard_map/ppermute | solution.py:855
  100.7 27.2 %collective-permute-start.20 = (bf16[4,480,256]{2,1,0:T(8,128)(2,1)}, bf16[4,480,256]{2,1,0:T(8,128)(2,1)S(1)}, u32[]{:S(2)}, u32[]{:S(2)}) collective-permute-start(bf16[4,480,256]{2,1,0:T(8,128)(2,1)} %get-tuple-element.192.refs_8_.refs_0_), channel_id=1, source_target_pairs={{0,1},{1,0},{2,3},{3,2},{4,5},{5,4},{6,7},{7,6},{8,9},{9,8},{10,11... | collective-permute-start | bytes 2949128 | tf_op jit(solution)/shard_map/ppermute | solution.py:851
  100.7 27.8 %collective-permute-start.18 = (bf16[4,480,256]{2,1,0:T(8,128)(2,1)}, bf16[4,480,256]{2,1,0:T(8,128)(2,1)S(1)}, u32[]{:S(2)}, u32[]{:S(2)}) collective-permute-start(bf16[4,480,256]{2,1,0:T(8,128)(2,1)} %get-tuple-element.192.refs_8_.refs_0_), channel_id=1, source_target_pairs={{0,4},{2,6},{4,0},{6,2},{8,12},{10,14},{12,8},{14,10},{16,20},{18,... | collective-permute-start | bytes 2949128 | tf_op jit(solution)/shard_map/ppermute | solution.py:855
  102.2 26.3 %collective-permute-start.21 = (bf16[4,480,256]{2,1,0:T(8,128)(2,1)S(1)}, bf16[4,480,256]{2,1,0:T(8,128)(2,1)S(1)}, u32[]{:S(2)}, u32[]{:S(2)}) collective-permute-start(bf16[4,480,256]{2,1,0:T(8,128)(2,1)S(1)} %get-tuple-element.193.refs_12_.refs_4_), channel_id=1, source_target_pairs={{0,1},{1,0},{2,3},{3,2},{4,5},{5,4},{6,7},{7,6},{8,9},{9,8},{10,11... | collective-permute-start | bytes 2949128 | tf_op jit(solution)/shard_map/ppermute | solution.py:851
  102.4 26.1 %collective-permute-start.19 = (bf16[4,480,256]{2,1,0:T(8,128)(2,1)S(1)}, bf16[4,480,256]{2,1,0:T(8,128)(2,1)S(1)}, u32[]{:S(2)}, u32[]{:S(2)}) collective-permute-start(bf16[4,480,256]{2,1,0:T(8,128)(2,1)S(1)} %get-tuple-element.193.refs_12_.refs_4_), channel_id=1, source_target_pairs={{0,2},{2,0},{4,6},{6,4},{8,10},{10,8},{12,14},{14,12},{16,18},{18,... | collective-permute-start | bytes 2949128 | tf_op jit(solution)/shard_map/ppermute | solution.py:855
  103.0 25.6 %collective-permute-start.22 = (bf16[4,480,256]{2,1,0:T(8,128)(2,1)}, bf16[4,480,256]{2,1,0:T(8,128)(2,1)S(1)}, u32[]{:S(2)}, u32[]{:S(2)}) collective-permute-start(bf16[4,480,256]{2,1,0:T(8,128)(2,1)} %collective-permute-done.15.refs_9_.refs_1_), channel_id=1, source_target_pairs={{0,1},{1,0},{2,3},{3,2},{4,5},{5,4},{6,7},{7,6},{8,9},{9,8},{10,11... | collective-permute-start | bytes 2949128 | tf_op jit(solution)/shard_map/ppermute | solution.py:851
  128.6 24.0 %collective-permute-start.23 = (bf16[4,480,256]{2,1,0:T(8,128)(2,1)}, bf16[4,480,256]{2,1,0:T(8,128)(2,1)S(1)}, u32[]{:S(2)}, u32[]{:S(2)}) collective-permute-start(bf16[4,480,256]{2,1,0:T(8,128)(2,1)} %collective-permute-done.15.refs_9_.refs_1_), channel_id=1, source_target_pairs={{0,4},{2,6},{4,0},{6,2},{8,12},{10,14},{12,8},{14,10},{16,20},{18,... | collective-permute-start | bytes 2949128 | tf_op jit(solution)/shard_map/ppermute | solution.py:855
  129.1 23.7 %collective-permute-start.24 = (bf16[4,480,256]{2,1,0:T(8,128)(2,1)}, bf16[4,480,256]{2,1,0:T(8,128)(2,1)}, u32[]{:S(2)}, u32[]{:S(2)}) collective-permute-start(bf16[4,480,256]{2,1,0:T(8,128)(2,1)} %collective-permute-done.16.refs_14_.refs_6_), channel_id=1, source_target_pairs={{0,2},{2,0},{4,6},{6,4},{8,10},{10,8},{12,14},{14,12},{16,18},{18,... | collective-permute-start | bytes 2949128 | tf_op jit(solution)/shard_map/ppermute | solution.py:855
  130.6 22.2 %collective-permute-start.27 = (bf16[4,480,256]{2,1,0:T(8,128)(2,1)S(1)}, bf16[4,480,256]{2,1,0:T(8,128)(2,1)}, u32[]{:S(2)}, u32[]{:S(2)}) collective-permute-start(bf16[4,480,256]{2,1,0:T(8,128)(2,1)S(1)} %collective-permute-done.19.refs_13_.refs_5_), channel_id=1, source_target_pairs={{0,1},{1,0},{2,3},{3,2},{4,5},{5,4},{6,7},{7,6},{8,9},{9,8},{10,11... | collective-permute-start | bytes 2949128 | tf_op jit(solution)/shard_map/ppermute | solution.py:851
  130.6 22.2 %collective-permute-start.26 = (bf16[4,480,256]{2,1,0:T(8,128)(2,1)S(1)}, bf16[4,480,256]{2,1,0:T(8,128)(2,1)}, u32[]{:S(2)}, u32[]{:S(2)}) collective-permute-start(bf16[4,480,256]{2,1,0:T(8,128)(2,1)S(1)} %collective-permute-done.18.refs_10_.refs_2_), channel_id=1, source_target_pairs={{0,1},{1,0},{2,3},{3,2},{4,5},{5,4},{6,7},{7,6},{8,9},{9,8},{10,11... | collective-permute-start | bytes 2949128 | tf_op jit(solution)/shard_map/ppermute | solution.py:851
  199.5 43.4 %collective-permute-start.30 = (bf16[16,640,256]{2,1,0:T(8,128)(2,1)}, bf16[16,640,256]{2,1,0:T(8,128)(2,1)S(1)}, u32[]{:S(2)}, u32[]{:S(2)}) collective-permute-start(bf16[16,640,256]{2,1,0:T(8,128)(2,1)} %get-tuple-element.216), channel_id=1, source_target_pairs={{0,1},{1,0},{2,3},{3,2},{4,5},{5,4},{6,7},{7,6},{8,9},{9,8},{10,11... | collective-permute-start | bytes 15728648 | tf_op jit(solution)/shard_map/ppermute | solution.py:851
  242.5 42.3 %collective-permute-start.34 = (bf16[2,2560,256]{2,1,0:T(8,128)(2,1)}, bf16[2,2560,256]{2,1,0:T(8,128)(2,1)S(1)}, u32[]{:S(2)}, u32[]{:S(2)}) collective-permute-start(bf16[2,2560,256]{2,1,0:T(8,128)(2,1)} %get-tuple-element.227), channel_id=1, source_target_pairs={{0,1},{1,0},{2,3},{3,2},{4,5},{5,4},{6,7},{7,6},{8,9},{9,8},{10,11... | collective-permute-start | bytes 7864328 | tf_op jit(solution)/shard_map/ppermute | solution.py:851
  250.6 43.2 %collective-permute-start.32 = (bf16[8,320,256]{2,1,0:T(8,128)(2,1)}, bf16[8,320,256]{2,1,0:T(8,128)(2,1)S(1)}, u32[]{:S(2)}, u32[]{:S(2)}) collective-permute-start(bf16[8,320,256]{2,1,0:T(8,128)(2,1)} %get-tuple-element.225), channel_id=1, source_target_pairs={{0,2},{2,0},{4,6},{6,4},{8,10},{10,8},{12,14},{14,12},{16,18},{18,... | collective-permute-start | bytes 3932168 | tf_op jit(solution)/shard_map/ppermute | solution.py:855
  252.1 41.7 %collective-permute-start.33 = (bf16[8,320,256]{2,1,0:T(8,128)(2,1)}, bf16[8,320,256]{2,1,0:T(8,128)(2,1)S(1)}, u32[]{:S(2)}, u32[]{:S(2)}) collective-permute-start(bf16[8,320,256]{2,1,0:T(8,128)(2,1)} %get-tuple-element.226), channel_id=1, source_target_pairs={{0,4},{2,6},{4,0},{6,2},{8,12},{10,14},{12,8},{14,10},{16,20},{18,... | collective-permute-start | bytes 3932168 | tf_op jit(solution)/shard_map/ppermute | solution.py:855
  292.8 42.3 %collective-permute-start.38 = (bf16[8,224,256]{2,1,0:T(8,128)(2,1)}, bf16[8,224,256]{2,1,0:T(8,128)(2,1)S(1)}, u32[]{:S(2)}, u32[]{:S(2)}) collective-permute-start(bf16[8,224,256]{2,1,0:T(8,128)(2,1)} %get-tuple-element.246), channel_id=1, source_target_pairs={{0,2},{2,0},{4,6},{6,4},{8,10},{10,8},{12,14},{14,12},{16,18},{18,... | collective-permute-start | bytes 2752520 | tf_op jit(solution)/shard_map/ppermute | solution.py:855
  293.3 41.7 %collective-permute-start.39 = (bf16[8,224,256]{2,1,0:T(8,128)(2,1)}, bf16[8,224,256]{2,1,0:T(8,128)(2,1)S(1)}, u32[]{:S(2)}, u32[]{:S(2)}) collective-permute-start(bf16[8,224,256]{2,1,0:T(8,128)(2,1)} %get-tuple-element.247), channel_id=1, source_target_pairs={{0,4},{2,6},{4,0},{6,2},{8,12},{10,14},{12,8},{14,10},{16,20},{18,... | collective-permute-start | bytes 2752520 | tf_op jit(solution)/shard_map/ppermute | solution.py:855
  296.2 42.1 %collective-permute-start.36 = (bf16[4,320,256]{2,1,0:T(8,128)(2,1)}, bf16[4,320,256]{2,1,0:T(8,128)(2,1)S(1)}, u32[]{:S(2)}, u32[]{:S(2)}) collective-permute-start(bf16[4,320,256]{2,1,0:T(8,128)(2,1)} %get-tuple-element.240), channel_id=1, source_target_pairs={{0,4},{2,6},{4,0},{6,2},{8,12},{10,14},{12,8},{14,10},{16,20},{18,... | collective-permute-start | bytes 1966088 | tf_op jit(solution)/shard_map/ppermute | solution.py:855
  297.7 40.6 %collective-permute-start.37 = (bf16[4,320,256]{2,1,0:T(8,128)(2,1)}, bf16[4,320,256]{2,1,0:T(8,128)(2,1)S(1)}, u32[]{:S(2)}, u32[]{:S(2)}) collective-permute-start(bf16[4,320,256]{2,1,0:T(8,128)(2,1)} %get-tuple-element.241), channel_id=1, source_target_pairs={{0,2},{2,0},{4,6},{6,4},{8,10},{10,8},{12,14},{14,12},{16,18},{18,... | collective-permute-start | bytes 1966088 | tf_op jit(solution)/shard_map/ppermute | solution.py:855
  364.0 22.4 %collective-permute-start.48 = (bf16[2,224,256]{2,1,0:T(8,128)(2,1)S(1)}, bf16[2,224,256]{2,1,0:T(8,128)(2,1)S(1)}, u32[]{:S(2)}, u32[]{:S(2)}) collective-permute-start(bf16[2,224,256]{2,1,0:T(8,128)(2,1)S(1)} %get-tuple-element.278), channel_id=1, source_target_pairs={{0,8},{2,10},{4,12},{6,14},{8,16},{10,18},{12,20},{14,22},{16,24},... | collective-permute-start | bytes 688136 | tf_op jit(solution)/shard_map/ppermute | solution.py:871
  364.5 34.5 %collective-permute-start.56 = (bf16[2,224,256]{2,1,0:T(8,128)(2,1)S(1)}, bf16[2,224,256]{2,1,0:T(8,128)(2,1)S(1)}, u32[]{:S(2)}, u32[]{:S(2)}) collective-permute-start(bf16[2,224,256]{2,1,0:T(8,128)(2,1)S(1)} %get-tuple-element.279), channel_id=1, source_target_pairs={{0,24},{2,26},{4,28},{6,30},{8,0},{10,2},{12,4},{14,6},{16,8},{18,... | collective-permute-start | bytes 688136 | tf_op jit(solution)/shard_map/ppermute | solution.py:871
  (73 other events, 933.8 us)
where the time goes:
time: 415 us; the launch traced here: 410 us
  Pallas kernels  254 us (61%)
  waiting for transfers between devices  58 us (14%)
  starting transfers between devices  50.9 us (12%)
  local copies, waits for them, and re-layouts  28.9 us (7%)
  other arithmetic  16 us (4%)
    pallas_call x2, Pallas kernels, feed_forward(): call(functools.partial(ffn_body, turn), [jax.ShapeDtypeStruct((seq, wide)...  84.3 us
    pallas_call x1, Pallas kernels, attend_back(): call(functools.partial(attend_back_body, block), [jax.ShapeDtypeStruct((G...  35.8 us
    pallas_call x1, Pallas kernels, after(): call(functools.partial(post_body, width), [jax.ShapeDtypeStruct((width, s...  31.1 us
    ppermute x15, waiting for transfers between devices, along_z(): lax.ppermute(x, 'dp', [(i, (i + 4 * step) % count) for i in range(count)])  26.6 us
    pallas_call x1, Pallas kernels, attend(): call(functools.partial(attend_body, block), [shape, shape], (KV_HEADS,),...  24.9 us
    ppermute x22, starting transfers between devices, across(): return lax.ppermute(x, 'dp', [(i, i ^ 1 << bit) for i in range(count)])  24.6 us
    ppermute x15, starting transfers between devices, along_z(): lax.ppermute(x, 'dp', [(i, (i + 4 * step) % count) for i in range(count)])  21.7 us
    ppermute x22, waiting for transfers between devices, across(): return lax.ppermute(x, 'dp', [(i, i ^ 1 << bit) for i in range(count)])  20 us
  transfers between devices with their start and end apart: 57, of which 17 were waited for; matrix products, arithmetic and copies ran while one was open for 7% of the time, Pallas kernels for 52%

commit v1 on v0

--- a/solution.py
+++ b/solution.py
@@ -232,7 +232,7 @@
     )(q, k, v)
 
 
-def attend_back_body(block, q_ref, k_ref, v_ref, do_ref, cos_ref, sa_ref, sb_ref,
+def attend_back_body(block, q_ref, k_ref, v_ref, do_ref, delta_ref, cos_ref, sa_ref, sb_ref,
                      dq_ref, dk_ref, dv_ref, acc_ref):
     seq = k_ref.shape[1]
     above = lax.broadcasted_iota(jnp.int32, (block, block), 0) <= lax.broadcasted_iota(
@@ -262,7 +262,7 @@
             p = jnp.exp(mm_nt(k, q))
             inner = jnp.where(above, p[:, :block], 0.0)
             p = inner if p.shape[1] == block else jnp.concatenate([inner, p[:, block:]], axis=1)
-            ds = (p * mm_nt(v, do)).astype(BF16)
+            ds = (p * (mm_nt(v, do) - delta_ref[g : g + 1, block * j :])).astype(BF16)
             dv = dv + mm(p.astype(BF16), do)
             dk = dk + mm(ds, q)
             dq = mm_tn(ds, k)
@@ -276,7 +276,7 @@
         dq_ref[g] = unrotate(acc_ref[g] * HEAD ** -0.5, slice(0, seq))
 
 
-def attend_back(q, k, v, do, cos, sa, sb, first, count, block=256):
+def attend_back(q, k, v, do, delta, cos, sa, sb, first, count, block=256):
     seq = q.shape[1]
     group = lambda at: pl.BlockSpec((GROUP, seq, LANES), lambda n: (n + at, 0, 0))
     one = lambda at: pl.BlockSpec((1, seq, LANES), lambda n: (n + at, 0, 0))
@@ -288,12 +288,14 @@
             jax.ShapeDtypeStruct((count, seq, LANES), BF16),
         ],
         (count,),
-        [group(first), one(first), one(first), group(first)] + [whole((seq, LANES))] * 3,
+        [group(first), one(first), one(first), group(first)]
+        + [pl.BlockSpec((8, seq), lambda n: (n + first, 0))]
+        + [whole((seq, LANES))] * 3,
         [group(0), one(0), one(0)],
         scratch=[pltpu.VMEM((GROUP, seq, LANES), F32)],
         flops=10 * GROUP * count * seq * seq * LANES,
         moved=4_000_000 * count,
-    )(q, k, v, do, cos, sa, sb)
+    )(q, k, v, do, delta, cos, sa, sb)
 
 
 def pairs_to(ref, get, heads, first=0):
@@ -308,7 +310,7 @@
 def mid_body(width, place_ref, o_ref, own_ref, other_ref, e_ref, u_ref, wo_ref, xp_ref, gain_ref,
              op_ref, m_ref, b_ref, df_ref):
     flat = jnp.concatenate([o_ref[head] for head in range(HEADS)], axis=1)
-    op = mm_nt(flat, u_ref[: wo_ref.shape[0], :]).astype(BF16)
+    op = mm_nt(flat, u_ref[...]).astype(BF16)
     op_ref[...] = op
     m = xp_ref[...].astype(F32) + mm(op, wo_ref[...])
     m_ref[...] = m
@@ -380,6 +382,8 @@
     def _():
         for copy in down_copies():
             copy.start()
+        out_ref[...] = jnp.zeros_like(out_ref)
+        db_ref[...] = jnp.zeros_like(db_ref)
         if turn:
             carried(0).start()
             carried(1).start()
@@ -391,17 +395,16 @@
             wg_ref[pl.ds(row, 64), :] = gates[near][k]
             wu_ref[pl.ds(row, 64), :] = ups[near][k]
 
-    b, df = b_ref[...], df_ref[...]
-    wg, wu = wg_ref[...], wu_ref[...]
-    gate = mm(b, wg)
-    upper = mm(b, wu)
-
     @pl.when(s == 0)
     def _():
         for copy in down_copies():
             copy.wait()
 
+    b, df = b_ref[...], df_ref[...]
+    wg, wu = wg_ref[...], wu_ref[...]
     wd = wd_ref[pl.ds(pl.multiple_of(chunk * s, chunk), chunk), :]
+    gate = mm(b, wg)
+    upper = mm(b, wu)
     sig = jax.nn.sigmoid(gate)
     act = gate * sig
     z = (act * upper).astype(BF16)
@@ -409,15 +412,8 @@
     dg = (dz * upper * (sig + act * (1.0 - sig))).astype(BF16)
     du = (dz * act).astype(BF16)
 
-    @pl.when(s == 0)
-    def _():
-        out_ref[...] = mm(z, wd)
-        db_ref[...] = mm_nt(dg, wg) + mm_nt(du, wu)
-
-    @pl.when(s > 0)
-    def _():
-        out_ref[...] += mm(z, wd)
-        db_ref[...] += mm_nt(dg, wg) + mm_nt(du, wu)
+    out_ref[...] += mm(z, wd)
+    db_ref[...] += mm_nt(dg, wg) + mm_nt(du, wu)
 
     if turn:
 
@@ -507,13 +503,11 @@
         keep_ref[0] = value.astype(keep_ref.dtype)
 
 
-def post_body(width, place_ref, m_ref, acc_ref, db_ref, df_ref, gain_ref, e_ref, u_ref,
+def post_body(width, place_ref, m_ref, db_ref, df_ref, gain_ref, u_ref,
               sum_ref, wo_ref, op_ref,
-              send_ref, keep_ref, em_ref, do_ref, dwo_send, dwo_keep, dgain_ref, da_ref):
+              em_ref, do_ref, delta_ref, dwo_send, dwo_keep, dgain_ref, da_ref):
     i = pl.program_id(0)
     m, db = m_ref[...], db_ref[...]
-    out = (m + acc_ref[...]).astype(BF16)
-    put_tokens(send_ref, keep_ref, mm_nt(e_ref[:width, :], out))
     scale = lax.rsqrt(jnp.sum(m * m, axis=-1, keepdims=True) / width + EPSILON)
     n = m * scale
     c = db * gain_ref[1:2]
@@ -523,9 +517,7 @@
     da = em.astype(BF16)
     dgain = jnp.sum(db * n, axis=0, keepdims=True)
     block = m.shape[0]
-    late = pl.num_programs(0) // 2
-    at = jnp.where(i < late, (1 - place_ref[0]) * late + i, place_ref[0] * late + i - late)
-    rows = pl.ds(pl.multiple_of(block * at, block), block)
+    rows = pl.ds(pl.multiple_of(block * i, block), block)
     da_ref[rows, :] = da
 
     @pl.when(i == 0)
@@ -540,9 +532,8 @@
     product = do.astype(F32) * op_ref[rows, :].astype(F32)
     high = product.astype(BF16)
     low = (product - high.astype(F32)).astype(BF16)
-    delta = mm(high, sum_ref[...]) + mm(low, sum_ref[...])
-    full = jnp.concatenate([do] + [t.astype(BF16) for t in three_terms(delta)], axis=1)
-    do = mm(full, u_ref[...]).astype(BF16)
+    delta_ref[...] = mm_nt(sum_ref[...], high) + mm_nt(sum_ref[...], low)
+    do = mm(do, u_ref[...]).astype(BF16)
     for head in range(HEADS):
         do_ref[head] = do[:, LANES * head : LANES * (head + 1)]
 
@@ -555,35 +546,64 @@
                 ref[q] = dwo[:, 256 * q : 256 * (q + 1)].reshape(ref.shape[1:])
 
 
-def after(place, m, acc, db, df, gain, spread, unpack, delta_sum, w_out, op, width, block=512):
+def after(place, m, db, df, gain, unpack, delta_sum, w_out, op, width, block=512):
     seq, wide = m.shape
     blocks = 16
     steps = seq // block
-    at = token_block(steps)
-    rows = lambda n: pl.BlockSpec((block, n), lambda i, place: (at(i, place), 0))
-    heads = pl.BlockSpec((HEADS, block, LANES), lambda i, place: (0, at(i, place), 0))
+    rows = lambda n: pl.BlockSpec((block, n), lambda i, place: (i, 0))
+    heads = pl.BlockSpec((HEADS, block, LANES), lambda i, place: (0, i, 0))
     dwo_shape = (2, blocks, wide // blocks, 256)
-    consts = (gain, spread, unpack, delta_sum, w_out, op)
+    consts = (gain, unpack, delta_sum, w_out, op)
     return call(
         functools.partial(post_body, width),
         [
-            jax.ShapeDtypeStruct((width, seq // 2), BF16),
-            jax.ShapeDtypeStruct((2, width, seq // 2), BF16),
             jax.ShapeDtypeStruct((seq, wide), F32),
             jax.ShapeDtypeStruct((HEADS, seq, LANES), BF16),
+            jax.ShapeDtypeStruct((8 * KV_HEADS, seq), F32),
             jax.ShapeDtypeStruct(dwo_shape, BF16),
             jax.ShapeDtypeStruct(dwo_shape, BF16),
             jax.ShapeDtypeStruct((1, wide), F32),
         ],
         (steps,),
-        [rows(wide)] * 4 + [whole(t.shape) for t in consts],
-        token_specs(steps, block, width)
-        + [rows(wide), heads, whole(dwo_shape), whole(dwo_shape), whole((1, wide))],
+        [rows(wide)] * 3 + [whole(t.shape) for t in consts],
+        [
+            rows(wide),
+            heads,
+            pl.BlockSpec((8 * KV_HEADS, block), lambda i, place: (0, i)),
+            whole(dwo_shape),
+            whole(dwo_shape),
+            whole((1, wide)),
+        ],
         scratch=[pltpu.VMEM((seq, wide), BF16)],
         flops=2 * seq * wide * 6 * wide,
         moved=40_000_000,
         prefetch=1,
-    )(place, m, acc, db, df, *consts)
+    )(place, m, db, df, *consts)
+
+
+def finish_body(width, place_ref, m_ref, acc_ref, e_ref, send_ref, keep_ref):
+    out = (m_ref[...] + acc_ref[...]).astype(BF16)
+    put_tokens(send_ref, keep_ref, mm_nt(e_ref[:width, :], out))
+
+
+def finish(place, m, acc, spread, width, block=256):
+    seq, wide = m.shape
+    steps = seq // block
+    at = token_block(steps)
+    rows = lambda n: pl.BlockSpec((block, n), lambda i, place: (at(i, place), 0))
+    return call(
+        functools.partial(finish_body, width),
+        [
+            jax.ShapeDtypeStruct((width, seq // 2), BF16),
+            jax.ShapeDtypeStruct((2, width, seq // 2), BF16),
+        ],
+        (steps,),
+        [rows(wide), rows(wide), whole(spread.shape)],
+        token_specs(steps, block, width),
+        flops=2 * seq * wide * wide,
+        moved=16_000_000,
+        prefetch=1,
+    )(place, m, acc, spread)
 
 
 def weights_body(place_ref, dq_ref, dk_ref, dv_ref, a_ref, w_ref, gain_ref,
@@ -647,35 +667,60 @@
     )(place, *parts, a, w_qkv, gain, dgain_ffn)
 
 
-def input_body(width, place_ref, flat_ref, w_ref, xp_ref, em_ref, gain_ref, e_ref, send_ref, keep_ref):
-    da = mm_nt(flat_ref[...], w_ref[...])
-    xp = xp_ref[...].astype(F32)
-    scale = lax.rsqrt(jnp.sum(xp * xp, axis=-1, keepdims=True) / width + EPSILON)
-    n = xp * scale
-    c = da * gain_ref[:1]
-    mean = jnp.sum(c * n, axis=-1, keepdims=True) / width
-    grad = em_ref[...] + scale * (c - n * mean)
-    put_tokens(send_ref, keep_ref, mm_nt(e_ref[:width, :], grad.astype(BF16)))
-
-
-def input_back(place, flat, w_qkv, xp, em, gain, spread, width, block=512):
+def input_body(width, keep, place_ref, flat_ref, w_ref, xp_ref, em_ref, gain_ref, e_ref, *refs):
+    got_ref, to_ref = refs if keep else (None, refs[0])
+    i = pl.program_id(0)
+    steps = pl.num_programs(0) // (2 if keep else 1)
+
+    def work():
+        da = mm_nt(flat_ref[...], w_ref[...])
+        xp = xp_ref[...].astype(F32)
+        scale = lax.rsqrt(jnp.sum(xp * xp, axis=-1, keepdims=True) / width + EPSILON)
+        n = xp * scale
+        c = da * gain_ref[:1]
+        mean = jnp.sum(c * n, axis=-1, keepdims=True) / width
+        grad = em_ref[...] + scale * (c - n * mean)
+        return mm_nt(e_ref[:width, :], grad.astype(BF16))
+
+    if keep:
+
+        @pl.when(i < steps)
+        def _():
+            to_ref[0] = work()
+
+        @pl.when(i >= steps)
+        def _():
+            to_ref[0] = got_ref[...].astype(F32)
+
+    else:
+        to_ref[...] = work().astype(BF16)
+
+
+def input_back(place, flat, w_qkv, xp, em, gain, spread, width, got=None, block=256):
     seq, wide = xp.shape
-    steps = seq // block
-    at = token_block(steps)
-    rows = lambda n: pl.BlockSpec((block, n), lambda i, place: (at(i, place), 0))
+    steps = seq // 2 // block
+    keep = got is not None
+    token = lambda i, place: (place[0] if keep else 1 - place[0]) * steps + jnp.minimum(i, steps - 1)
+    rows = lambda n: pl.BlockSpec((block, n), lambda i, place: (token(i, place), 0))
+    ins = [rows(QKV_PAD), whole(w_qkv.shape), rows(wide), rows(wide), whole((8, wide)), whole(spread.shape)]
+    if keep:
+        ins.append(pl.BlockSpec((width, block), lambda i, place: (0, jnp.maximum(i - steps, 0))))
+        shape = jax.ShapeDtypeStruct((2, width, seq // 2), F32)
+        half = lambda i, place: jnp.where(i < steps, place[0], 1 - place[0])
+        out = pl.BlockSpec((1, width, block), lambda i, place: (half(i, place), 0, lax.rem(i, steps)))
+    else:
+        shape = jax.ShapeDtypeStruct((width, seq // 2), BF16)
+        out = pl.BlockSpec((width, block), lambda i, place: (0, i))
     return call(
-        functools.partial(input_body, width),
-        [
-            jax.ShapeDtypeStruct((width, seq // 2), BF16),
-            jax.ShapeDtypeStruct((2, width, seq // 2), F32),
-        ],
-        (steps,),
-        [rows(QKV_PAD), whole(w_qkv.shape), rows(wide), rows(wide), whole((8, wide)), whole(spread.shape)],
-        token_specs(steps, block, width),
-        flops=2 * seq * wide * (QKV_PAD + 2 * width),
-        moved=20_000_000,
+        functools.partial(input_body, width, keep),
+        [shape],
+        (steps * (2 if keep else 1),),
+        ins,
+        [out],
+        flops=seq * wide * (QKV_PAD + width),
+        moved=10_000_000,
         prefetch=1,
-    )(place, flat, w_qkv, xp, em, gain, spread)
+    )(place, flat, w_qkv, xp, em, gain, spread, *([got] if keep else []))[0]
 
 
 def begin_body(reader, n_in, place_ref, *refs):
@@ -767,16 +812,16 @@
     col = jnp.arange(WIDE_HEADS, dtype=jnp.int32)
     feature = col // LANES * HEAD + col % LANES
     place = jnp.where(col % LANES < HEAD, feature // per * step + feature % per, -1)
-    term = col % LANES - HEAD
-    place = jnp.where((term >= 0) & (term < 3), wide + term * LANES + col // LANES, place)
-    return (jnp.arange(wide + 3 * LANES, dtype=jnp.int32)[:, None] == place[None, :]).astype(BF16)
+    return (jnp.arange(wide, dtype=jnp.int32)[:, None] == place[None, :]).astype(BF16)
 
 
 def delta_matrix(width, blocks, wide):
     per, step = width // blocks, wide // blocks
-    row = jnp.arange(wide, dtype=jnp.int32)
-    head = jnp.where(row % step < per, (row // step * per + row % step) // HEAD, -1)
-    return (head[:, None] == jnp.arange(LANES, dtype=jnp.int32)[None, :]).astype(BF16)
+    col = jnp.arange(wide, dtype=jnp.int32)
+    head = jnp.where(col % step < per, (col // step * per + col % step) // HEAD, -1)
+    row = jnp.arange(8 * KV_HEADS, dtype=jnp.int32)
+    mine = jnp.where(row % 8 < GROUP, row // 8 * GROUP + row % 8, -2)
+    return (mine[:, None] == head[None, :]).astype(BF16)
 
 
 def spread_matrix(width, blocks, wide):
@@ -982,20 +1027,26 @@
     shard = jnp.concatenate([shard, pad_cols(w_out, groups)], axis=1)
     shard = jnp.pad(shard, ((0, 64 - per), (0, 0)))
     packed = pack_half(w_gate, w_up, w_down, 1, groups)[0]
+
+    def halves(x):
+        x = jnp.swapaxes(x[:, 0], 1, 2)
+        return pick(x, core), swap(pick(x, 1 - core))
+
     wide = count * 64
     spread, unpack = spread_matrix(width, count, wide), unpack_matrix(width, count, wide)
     delta_sum = delta_matrix(width, count, wide)
     table = tables(pick(positions[:, 0], core), pick(segment_ids[:, 0], core))
 
     level = rise(shard, count)
-    stack = tie(jnp.stack(level), spread, unpack, delta_sum, *table)
+    x_own, x_other = halves(inputs)
+    ct_own, ct_other = halves(cotangent)
+    stack = tie(jnp.stack(level), spread, delta_sum, *table, x_other, ct_other)
     part = spread_first(stack, count)
     packed = tie(packed, stack)
-    up = along_z(packed, 1, count)
-    part = tie_all(part, up)
-    near_far = spread_second(*part, count)
-    up = tie(up, part[0])
-    up_two, down = along_z(up, 1, count), along_z(packed, 3, count)
+    up, down = along_z(packed, 1, count), along_z(packed, 3, count)
+    near_far = spread_second(*tie_all(part, unpack), count)
+    up, down = tie_all((up, down), part[0])
+    up_two = along_z(up, 1, count)
     near_far = tie_all(near_far, up_two, down)
     pieces = near_far + tuple(swap(t) for t in near_far)
     packs = jnp.stack(tie_all((packed, up, up_two, down), near_far[0]))
@@ -1003,18 +1054,12 @@
     a00, b00 = packs[:, :half], packs[:, half:]
     a01, b10 = across(a00, 0, count), across(b00, 1, count)
 
-    def halves(x):
-        x = jnp.swapaxes(x[:, 0], 1, 2)
-        return pick(x, core), swap(pick(x, 1 - core))
-
-    x_own, x_other = halves(inputs)
-    ct_own, ct_other = halves(cotangent)
     pieces = tie_all(pieces, a00, b00)
     xp, a, q, k, v, w_qkv, w_o, gains = pre_attention(place_of, x_own, x_other, spread, pieces, *table)
-    a01, b10, ct_other, a00, b00 = tie_all((a01, b10, ct_other, a00, b00), q)
+    a01, b10, a00, b00 = tie_all((a01, b10, a00, b00), q)
     a10, b01 = across(a00, 1, count), across(b00, 0, count)
     got = [swap(a00), swap(b00), swap(a01)]
-    q = tie(q, a01, b10, ct_other)
+    q = tie(q, a01, b10)
     o, q2 = attend(q, k, v)
     a10, b01, *got = tie_all((a10, b01, *got), o)
     a11, b11 = across(tie(a01, a10), 1, count), across(tie(b10, a10), 0, count)
@@ -1036,9 +1081,7 @@
     blocked = lambda t: t.reshape(2, count, hidden, 256)
     d_got = swap(d_send)
     m = tie(m, *one.sent, d_send)
-    out_send, outs, em, do, o_send, o_keep, dgf = after(
-        place_of, m, acc, db, df, gains, spread, unpack, delta_sum, w_o, op, width
-    )
+    em, do, delta, o_send, o_keep, dgf = after(place_of, m, db, df, gains, unpack, delta_sum, w_o, op, width)
     o_got = swap(o_send)
     one.turn(em)
     one.move_again()
@@ -1047,8 +1090,7 @@
     )
     two.move()
     do = tie(do, *one.sent, *two.sent)
-    parts = attend_back(q2, k, v, do, *table[:3], 0, KV_HEADS)
-    outs = put_other(outs, tie(swap(out_send), parts[0]), core)
+    parts = attend_back(q2, k, v, do, delta, *table[:3], 0, KV_HEADS)
     one.climb(parts[0])
     up, down = one.start_up(), one.start_down()
     two.turn(parts[0])
@@ -1062,16 +1104,21 @@
     three = RowSum(place_of, count, (p_keep, p_got), read_rows, 32)
     three.move()
     flat = tie(flat, *two.sent, *three.sent)
-    gi_send, gis = input_back(place_of, flat, w_qkv, xp, em, gains, spread, width)
-    *three.got, one_up, two_up = tie_all((*three.got, one_up, two_up), gis)
+    gi_send = input_back(place_of, flat, w_qkv, xp, em, gains, spread, width)
+    *three.got, one_up, two_up = tie_all((*three.got, one_up, two_up), gi_send)
     gi_got = swap(tie(gi_send, one_up))
     three.turn(one_up)
     three.move_again()
     two_up, two_down = two.go_up(two_up), two.start_down()
-    gis = put_other(gis, gi_got.astype(F32), core)
+    out_send, outs = finish(place_of, tie(m, *three.sent), acc, spread, width)
+    *three.got, gi_got = tie_all((*three.got, gi_got), outs)
+    three.climb(gi_got)
+    last_got = three.move_up()
+    out_got = swap(out_send)
+    gis = input_back(place_of, tie(flat, *three.sent, out_send), w_qkv, xp, em, gains, spread, width, gi_got)
+    last_got = tie_all(last_got, gis)
+    outs = put_other(outs, tie(out_got, gis), core)
     first = one.total(one_up, one_down)
-    three.climb(first)
-    last_got = three.move_up()
     second, third = two.total(two_up, two_down), three.total(*last_got)
     third = third.reshape(64, 896)[:per]
     gu = first.reshape(5, 2, 64, 256)
@@ -1136,12 +1183,12 @@
     acc, db, gu_keep, d_send, d_keep = feed_forward(
         place, b, df, mine, other, 1, (d_send, d_keep, acc0, db0)
     )
-    out_send, outs, em, do, o_send, o_keep, dgf = after(
-        place, m, acc, db, df, gains, spread, unpack, delta_sum, w_o, op, width
-    )
-    parts = attend_back(q2, k, v, do, cos, sa, sb, 0, KV_HEADS)
+    em, do, delta, o_send, o_keep, dgf = after(place, m, db, df, gains, unpack, delta_sum, w_o, op, width)
+    out_send, outs = finish(place, m, acc, spread, width)
+    parts = attend_back(q2, k, v, do, delta, cos, sa, sb, 0, KV_HEADS)
     flat, p_send, p_keep = projections_back(place, parts, a, w_qkv, gains, dgf)
-    gi_send, gis = input_back(place, flat, w_qkv, xp, em, gains, spread, width)
+    gi_send = input_back(place, flat, w_qkv, xp, em, gains, spread, width)
+    gis = input_back(place, flat, w_qkv, xp, em, gains, spread, width, gi_send)
 
     parts = [cut_rows(p, per) for p in (p_keep, p_send)]
     n_q, n_k = HEADS * HEAD // 2, KV_HEADS * HEAD // 2

time: 415 us -> 403 us (0.971)
  Pallas kernels: 254 us -> 245 us
    pallas_call x2, Pallas kernels: 84.3 us -> 69.6 us  [feed_forward(): call(functools.partial(ffn_body, turn), [jax.ShapeDtypeStruct((seq, wide)...]
    ppermute x22, waiting for transfers between devices: 20 us -> 11.6 us  [across(): return lax.ppermute(x, 'dp', [(i, i ^ 1 << bit) for i in range(count)])]
    ppermute x15, waiting for transfers between devices: 26.6 us -> 31.9 us  [along_z(): lax.ppermute(x, 'dp', [(i, (i + 4 * step) % count) for i in range(count)])]
    pallas_call x2 -> x4, Pallas kernels: 45.2 us -> 50.5 us  [the longest x1 22.3 us: after(): call(functools.partial(post_body, width), [jax.ShapeDtypeStruct((seq, wid...]
    unnamed x88 -> x94, local copies, waits for them, and re-layouts: 13.3 us -> 13.9 us
  transfers between devices with their start and end apart: 57 -> 57, of which waited for: 17 -> 17; matrix products, arithmetic and copies ran while one was open for 7% -> 7% of each run, Pallas kernels for 52% -> 53%
where the time goes in v1:
time: 403 us; the launch traced here: 398 us
  Pallas kernels  245 us (61%)
  waiting for transfers between devices  55.4 us (14%)
  starting transfers between devices  49.3 us (12%)
  local copies, waits for them, and re-layouts  31 us (8%)
  other arithmetic  15 us (4%)
    pallas_call x2, Pallas kernels, feed_forward(): call(functools.partial(ffn_body, turn), [jax.ShapeDtypeStruct((seq, wide)...  69.6 us
    pallas_call x1, Pallas kernels, attend_back(): call(functools.partial(attend_back_body, block), [jax.ShapeDtypeStruct((G...  36.3 us
    ppermute x15, waiting for transfers between devices, along_z(): lax.ppermute(x, 'dp', [(i, (i + 4 * step) % count) for i in range(count)])  31.9 us
    pallas_call x1, Pallas kernels, attend(): call(functools.partial(attend_body, block), [shape, shape], (KV_HEADS,),...  24.9 us
    ppermute x22, starting transfers between devices, across(): return lax.ppermute(x, 'dp', [(i, i ^ 1 << bit) for i in range(count)])  22.7 us
    ppermute x15, starting transfers between devices, along_z(): lax.ppermute(x, 'dp', [(i, (i + 4 * step) % count) for i in range(count)])  22.4 us
    pallas_call x1, Pallas kernels, after(): call(functools.partial(post_body, width), [jax.ShapeDtypeStruct((seq, wid...  22.3 us
    pallas_call x2, Pallas kernels, input_back(): call(functools.partial(input_body, width, keep), [shape], (steps * (2 if...  20.1 us
  transfers between devices with their start and end apart: 57, of which 17 were waited for; matrix products, arithmetic and copies ran while one was open for 7% of the time, Pallas kernels for 53%

profile of v1, /device:TPU:0, one launch (start us, length us, event | category | flops | bytes accessed | tf_op | source)
XLA Modules:
  0.0 397.7 jit_solution(7929333837100656841)
XLA Ops:
  4.4 4.1 %collective-permute-start.2 = (bf16[64,1408]{1,0:T(8,128)(2,1)S(1)}, bf16[64,1408]{1,0:T(8,128)(2,1)S(1)}, u32[]{:S(2)}, u32[]{:S(2)}) collective-permute-start(bf16[64,1408]{1,0:T(8,128)(2,1)S(1)} %get-tuple-element.362), channel_id=1, source_target_pairs={{0,16},{2,18},{4,20},{6,22},{8,24},{10,26},{12,28},{14,30},{16,0},... | collective-permute-start | bytes 540680 | tf_op jit(solution)/shard_map/ppermute | solution.py:916
  19.1 3.2 fusion.5
  30.7 3.5 fusion.u_ref
  42.9 4.9 %collective-permute-done.10 = bf16[960,256]{1,0:T(8,128)(2,1)S(1)} collective-permute-done((bf16[960,256]{1,0:T(8,128)(2,1)S(1)}, bf16[960,256]{1,0:T(8,128)(2,1)S(1)}, u32[]{:S(2)}, u32[]{:S(2)}) %collective-permute-start.10) | collective-permute-done | bytes 491552 | tf_op jit(solution)/shard_map/ppermute | solution.py:916
  47.8 9.9 %collective-permute-done.9 = bf16[960,256]{1,0:T(8,128)(2,1)S(1)} collective-permute-done((bf16[960,256]{1,0:T(8,128)(2,1)S(1)}, bf16[960,256]{1,0:T(8,128)(2,1)S(1)}, u32[]{:S(2)}, u32[]{:S(2)}) %collective-permute-start.9) | collective-permute-done | bytes 491552 | tf_op jit(solution)/shard_map/ppermute | solution.py:916
  57.9 13.4 %collective-permute-done.11 = bf16[960,256]{1,0:T(8,128)(2,1)S(1)} collective-permute-done((bf16[960,256]{1,0:T(8,128)(2,1)S(1)}, bf16[960,256]{1,0:T(8,128)(2,1)S(1)}, u32[]{:S(2)}, u32[]{:S(2)}) %collective-permute-start.11) | collective-permute-done | bytes 491552 | tf_op jit(solution)/shard_map/ppermute | solution.py:916
  77.0 18.2 %shard_map.212 = (bf16[1024,1024]{1,0:T(8,128)(2,1)}, bf16[1024,1024]{1,0:T(8,128)(2,1)}, bf16[15,1024,128]{2,1,0:T(8,128)(2,1)}, bf16[5,1024,128]{2,1,0:T(8,128...) custom-call(s32[4]{0:T(128)} %pad_add_fusion.place_ref, ...), custom_call_target="tpu_custom_call" | custom-call | flops 5502926848 | bytes 20000000 | tf_op jit(solution)/shard_map/pallas_call | solution.py:166
  100.2 24.9 %shard_map.213 = (bf16[15,1024,128]{2,1,0:T(8,128)(2,1)}, bf16[15,1024,128]{2,1,0:T(8,128)(2,1)}) custom-call(bf16[15,1024,128]{2,1,0:T(8,128)(2,1)} %get-tuple-element.195.q_ref, bf16[5,1024,128]{2,1,0:T(8,128)(2,1)} %get-tuple-element.196.k_ref, bf16[5,1024,128]{2,1,0:T(8,128)(2,1)} %get-tuple-element.197.v_ref), custom_call_target="tpu_custom_call" | custom-call | flops 8053063680 | bytes 15000000 | tf_op jit(solution)/shard_map/pallas_call | solution.py:224
  129.1 16.4 %shard_map.214 = (bf16[1024,1024]{1,0:T(8,128)(2,1)}, f32[1024,1024]{1,0:T(8,128)}, bf16[1024,1024]{1,0:T(8,128)(2,1)}, bf16[1024,1024]{1,0:T(8,128)(2,1)}) custom-call(s32[4]{0:T(128)} %pad_add_fusion.place_ref, bf16[15,1024,128]{2,1,0:T(8,128)(2,1)} %get-tuple-element.206.o_ref, bf16[960,512]{1,0:T(8,128)(2,1)} %get-tuple-element.349.own_ref, ...), custom_call_target="tpu_custom_call" | custom-call | flops 8589934592 | bytes 22000000 | tf_op jit(solution)/shard_map/pallas_call | solution.py:327
  145.5 4.2 %collective-permute-done.23.refs_11_.refs_3_ = bf16[4,480,256]{2,1,0:T(8,128)(2,1)S(1)} collective-permute-done((bf16[4,480,256]{2,1,0:T(8,128)(2,1)}, bf16[4,480,256]{2,1,0:T(8,128)(2,1)S(1)}, u32[]{:S(2)}, u32[]{:S(2)}) %collective-permute-start.23) | collective-permute-done | bytes 983072 | tf_op jit(solution)/shard_map/ppermute | solution.py:900
  155.7 33.3 %shard_map.215 = (f32[1024,1024]{1,0:T(8,128)}, f32[1024,1024]{1,0:T(8,128)}, bf16[16,640,256]{2,1,0:T(8,128)(2,1)}, bf16[2,2560,256]{2,1,0:T(8,128)(2,1)}, bf16[2,2560,256]{2,1,0:T(8,128)(2,1)}) custom-call(s32[4]{0:T(128)} %pad_add_fusion.place_ref, bf16[1024,1024]{1,0:T(8,128)(2,1)} %get-tuple-element.224.b_ref, ...), custom_call_target="tpu_custom_call" | custom-call | flops 24159191040 | bytes 40000000 | tf_op jit(solution)/shard_map/pallas_call | solution.py:444
  189.3 36.3 %shard_map.216 = (f32[1024,1024]{1,0:T(8,128)}, f32[1024,1024]{1,0:T(8,128)}, bf16[16,640,256]{2,1,0:T(8,128)(2,1)}, bf16[2,2560,256]{2,1,0:T(8,128)(2,1)}, bf16[2,2560,256]{2,1,0:T(8,128)(2,1)}) custom-call(s32[4]{0:T(128)} %pad_add_fusion.place_ref, bf16[1024,1024]{1,0:T(8,128)(2,1)} %get-tuple-element.224.b_ref, ...), custom_call_target="tpu_custom_call", output_to_operand_aliasing={{3}: (27, {}), {4}: (28, {})} | custom-call | flops 24159191040 | bytes 40000000 | tf_op jit(solution)/shard_map/pallas_call | solution.py:444
  228.5 3.1 shard_map.217
  236.0 22.3 %shard_map.218 = (f32[1024,1024]{1,0:T(8,128)}, bf16[15,1024,128]{2,1,0:T(8,128)(2,1)}, f32[40,1024]{1,0:T(8,128)}, bf16[2,16,64,256]{3,2,1,0:T(8,128)(2,1)}, bf...) custom-call(s32[4]{0:T(128)} %pad_add_fusion.place_ref, f32[1024,1024]{1,0:T(8,128)} %get-tuple-element.301.m_ref, ...), custom_call_target="tpu_custom_call" | custom-call | flops 12884901888 | bytes 40000000 | tf_op jit(solution)/shard_map/pallas_call | solution.py:557
  272.8 36.3 %shard_map.221 = (bf16[15,1024,128]{2,1,0:T(8,128)(2,1)}, bf16[5,1024,128]{2,1,0:T(8,128)(2,1)}, bf16[5,1024,128]{2,1,0:T(8,128)(2,1)}) custom-call(bf16[15,1024,128]{2,1,0:T(8,128)(2,1)} %get-tuple-element.236.q_ref, bf16[5,1024,128]{2,1,0:T(8,128)(2,1)} %get-tuple-element.196.k_ref, bf16[5,1024,128]{2,1,0:T(8,128)(2,1)} %get-tuple-element.197.v_ref, ...), custom_call_target="tpu_custom_call" | custom-call | flops 20132659200 | bytes 20000000 | tf_op jit(solution)/shard_map/pallas_call | solution.py:283
  314.0 3.8 collective-permute-start.40
  317.8 14.6 %shard_map.224 = (bf16[1024,1664]{1,0:T(8,128)(2,1)}, bf16[16,64,896]{2,1,0:T(8,128)(2,1)}, bf16[16,64,896]{2,1,0:T(8,128)(2,1)}) custom-call(s32[4]{0:T(128)} %pad_add_fusion.place_ref, bf16[15,1024,128]{2,1,0:T(8,128)(2,1)} %get-tuple-element.255.dq_ref, bf16[5,1024,128]{2,1,0:T(8,128)(2,1)} %get-tuple-element.256.dk_ref, ...), custom_call_target="tpu_custom_call" | custom-call | flops 3489660928 | bytes 20000000 | tf_op jit(solution)/shard_map/pallas_call | solution.py:649
  332.5 4.0 %collective-permute-done.43.refs_1_ = bf16[16,64,896]{2,1,0:T(8,128)(2,1)S(1)} collective-permute-done((bf16[16,64,896]{2,1,0:T(8,128)(2,1)}, bf16[16,64,896]{2,1,0:T(8,128)(2,1)S(1)}, u32[]{:S(2)}, u32[]{:S(2)}) %collective-permute-start.43) | collective-permute-done | bytes 1835040 | tf_op jit(solution)/shard_map/ppermute | solution.py:896
  342.4 3.9 collective-permute-start.56
  346.3 9.1 %shard_map.227 = bf16[960,512]{1,0:T(8,128)(2,1)} custom-call(s32[4]{0:T(128)} %pad_add_fusion.place_ref, bf16[1024,1664]{1,0:T(8,128)(2,1)} %get-tuple-element.315.flat_ref, bf16[1024,1664]{1,0:T(8,128)(2,1)} %get-tuple-element.273.w_ref, bf16[1024,1024]{1,0:T(8,128)(2,1)} %get-tuple-element.208.xp_ref, f32[1024,1024]{1,0:T(8,128)} %get-tuple-element.241.em_ref, ...), custom_call_target="tpu_custom_call" | custom-call | flops 2751463424 | bytes 10000000 | tf_op jit(solution)/shard_map/pallas_call | solution.py:714
  355.4 3.6 collective-permute-done.47
  365.8 8.0 %shard_map.229 = (bf16[960,512]{1,0:T(8,128)(2,1)}, bf16[2,960,512]{2,1,0:T(8,128)(2,1)}) custom-call(s32[4]{0:T(128)} %pad_add_fusion.place_ref, f32[1024,1024]{1,0:T(8,128)} %get-tuple-element.301.m_ref, f32[1024,1024]{1,0:T(8,128)} %get-tuple-element.230.acc_ref, bf16[1024,1024]{1,0:T(8,128)(2,1)} %fusion.2.e_ref), custom_call_target="tpu_custom_call" | custom-call | flops 2147483648 | bytes 16000000 | tf_op jit(solution)/shard_map/pallas_call | solution.py:594
  378.4 4.4 %collective-permute-start.53 = (bf16[2,32,896]{2,1,0:T(8,128)(2,1)S(1)}, bf16[2,32,896]{2,1,0:T(8,128)(2,1)S(1)}, u32[]{:S(2)}, u32[]{:S(2)}) collective-permute-start(bf16[2,32,896]{2,1,0:T(8,128)(2,1)S(1)} %get-tuple-element.313), channel_id=1, source_target_pairs={{0,16},{2,18},{4,20},{6,22},{8,24},{10,26},{12,28},{14,30},{16,0},... | collective-permute-start | bytes 344072 | tf_op jit(solution)/shard_map/ppermute | solution.py:916
  382.8 11.0 %shard_map.231 = f32[2,960,512]{2,1,0:T(8,128)} custom-call(s32[4]{0:T(128)} %pad_add_fusion.place_ref, bf16[1024,1664]{1,0:T(8,128)(2,1)} %get-tuple-element.315.flat_ref, bf16[1024,1664]{1,0:T(8,128)(2,1)} %get-tuple-element.273.w_ref, bf16[1024,1024]{1,0:T(8,128)(2,1)} %get-tuple-element.208.xp_ref, f32[1024,1024]{1,0:T(8,128)} %get-tuple-element.241.em_ref, ...), custom_call_target="tpu_custom_call" | custom-call | flops 2751463424 | bytes 10000000 | tf_op jit(solution)/shard_map/pallas_call | solution.py:714
  (267 shorter events, 99.4 us)
Async XLA Ops:
  4.4 22.0 %collective-permute-start.2 = (bf16[64,1408]{1,0:T(8,128)(2,1)S(1)}, bf16[64,1408]{1,0:T(8,128)(2,1)S(1)}, u32[]{:S(2)}, u32[]{:S(2)}) collective-permute-start(bf16[64,1408]{1,0:T(8,128)(2,1)S(1)} %get-tuple-element.362), channel_id=1, source_target_pairs={{0,16},{2,18},{4,20},{6,22},{8,24},{10,26},{12,28},{14,30},{16,0},... | collective-permute-start | bytes 540680 | tf_op jit(solution)/shard_map/ppermute | solution.py:916
  34.1 23.6 %collective-permute-start.9 = (bf16[960,256]{1,0:T(8,128)(2,1)S(1)}, bf16[960,256]{1,0:T(8,128)(2,1)S(1)}, u32[]{:S(2)}, u32[]{:S(2)}) collective-permute-start(bf16[960,256]{1,0:T(8,128)(2,1)S(1)} %maximum_bitcast_fusion), channel_id=1, source_target_pairs={{0,8},{2,10},{4,12},{6,14},{8,16},{10,18},{12,20},{14,22},{16,24},... | collective-permute-start | bytes 1474568 | tf_op jit(solution)/shard_map/ppermute | solution.py:916
  40.8 30.5 %collective-permute-start.8 = (bf16[8,32,1408]{2,1,0:T(8,128)(2,1)}, bf16[8,32,1408]{2,1,0:T(8,128)(2,1)}, u32[]{:S(2)}, u32[]{:S(2)}) collective-permute-start(bf16[8,32,1408]{2,1,0:T(8,128)(2,1)} %constant_dynamic-update-slice_fusion.2.refs_2_), channel_id=1, source_target_pairs={{0,2},{2,0},{4,6},{6,4},{8,10},{10,8},{12,14},{14,12},{16,18},{18,... | collective-permute-start | bytes 2162696 | tf_op jit(solution)/shard_map/ppermute | solution.py:900
  42.3 29.0 %collective-permute-start.7 = (bf16[8,32,1408]{2,1,0:T(8,128)(2,1)S(1)}, bf16[8,32,1408]{2,1,0:T(8,128)(2,1)S(1)}, u32[]{:S(2)}, u32[]{:S(2)}) collective-permute-start(bf16[8,32,1408]{2,1,0:T(8,128)(2,1)S(1)} %constant_dynamic-update-slice_fusion.refs_0_), channel_id=1, source_target_pairs={{0,4},{2,6},{4,0},{6,2},{8,12},{10,14},{12,8},{14,10},{16,20},{18,... | collective-permute-start | bytes 2162696 | tf_op jit(solution)/shard_map/ppermute | solution.py:900
  72.8 23.9 %collective-permute-start.17 = (bf16[4,480,256]{2,1,0:T(8,128)(2,1)S(1)}, bf16[4,480,256]{2,1,0:T(8,128)(2,1)}, u32[]{:S(2)}, u32[]{:S(2)}) collective-permute-start(bf16[4,480,256]{2,1,0:T(8,128)(2,1)S(1)} %get-tuple-element.200.refs_12_.refs_4_), channel_id=1, source_target_pairs={{0,4},{2,6},{4,0},{6,2},{8,12},{10,14},{12,8},{14,10},{16,20},{18,... | collective-permute-start | bytes 2949128 | tf_op jit(solution)/shard_map/ppermute | solution.py:900
  74.7 23.9 %collective-permute-start.16 = (bf16[4,480,256]{2,1,0:T(8,128)(2,1)S(1)}, bf16[4,480,256]{2,1,0:T(8,128)(2,1)}, u32[]{:S(2)}, u32[]{:S(2)}) collective-permute-start(bf16[4,480,256]{2,1,0:T(8,128)(2,1)S(1)} %get-tuple-element.199.refs_8_.refs_0_), channel_id=1, source_target_pairs={{0,2},{2,0},{4,6},{6,4},{8,10},{10,8},{12,14},{14,12},{16,18},{18,... | collective-permute-start | bytes 2949128 | tf_op jit(solution)/shard_map/ppermute | solution.py:900
  98.6 26.5 %collective-permute-start.20 = (bf16[4,480,256]{2,1,0:T(8,128)(2,1)S(1)}, bf16[4,480,256]{2,1,0:T(8,128)(2,1)S(1)}, u32[]{:S(2)}, u32[]{:S(2)}) collective-permute-start(bf16[4,480,256]{2,1,0:T(8,128)(2,1)S(1)} %get-tuple-element.199.refs_8_.refs_0_), channel_id=1, source_target_pairs={{0,1},{1,0},{2,3},{3,2},{4,5},{5,4},{6,7},{7,6},{8,9},{9,8},{10,11... | collective-permute-start | bytes 2949128 | tf_op jit(solution)/shard_map/ppermute | solution.py:896
  98.6 27.0 %collective-permute-start.18 = (bf16[4,480,256]{2,1,0:T(8,128)(2,1)S(1)}, bf16[4,480,256]{2,1,0:T(8,128)(2,1)S(1)}, u32[]{:S(2)}, u32[]{:S(2)}) collective-permute-start(bf16[4,480,256]{2,1,0:T(8,128)(2,1)S(1)} %get-tuple-element.199.refs_8_.refs_0_), channel_id=1, source_target_pairs={{0,4},{2,6},{4,0},{6,2},{8,12},{10,14},{12,8},{14,10},{16,20},{18,... | collective-permute-start | bytes 2949128 | tf_op jit(solution)/shard_map/ppermute | solution.py:900
  99.4 26.3 %collective-permute-start.21 = (bf16[4,480,256]{2,1,0:T(8,128)(2,1)S(1)}, bf16[4,480,256]{2,1,0:T(8,128)(2,1)S(1)}, u32[]{:S(2)}, u32[]{:S(2)}) collective-permute-start(bf16[4,480,256]{2,1,0:T(8,128)(2,1)S(1)} %get-tuple-element.200.refs_12_.refs_4_), channel_id=1, source_target_pairs={{0,1},{1,0},{2,3},{3,2},{4,5},{5,4},{6,7},{7,6},{8,9},{9,8},{10,11... | collective-permute-start | bytes 2949128 | tf_op jit(solution)/shard_map/ppermute | solution.py:896
  99.6 26.1 %collective-permute-start.19 = (bf16[4,480,256]{2,1,0:T(8,128)(2,1)S(1)}, bf16[4,480,256]{2,1,0:T(8,128)(2,1)S(1)}, u32[]{:S(2)}, u32[]{:S(2)}) collective-permute-start(bf16[4,480,256]{2,1,0:T(8,128)(2,1)S(1)} %get-tuple-element.200.refs_12_.refs_4_), channel_id=1, source_target_pairs={{0,2},{2,0},{4,6},{6,4},{8,10},{10,8},{12,14},{14,12},{16,18},{18,... | collective-permute-start | bytes 2949128 | tf_op jit(solution)/shard_map/ppermute | solution.py:900
  100.2 25.5 %collective-permute-start.22 = (bf16[4,480,256]{2,1,0:T(8,128)(2,1)}, bf16[4,480,256]{2,1,0:T(8,128)(2,1)S(1)}, u32[]{:S(2)}, u32[]{:S(2)}) collective-permute-start(bf16[4,480,256]{2,1,0:T(8,128)(2,1)} %collective-permute-done.16.refs_9_.refs_1_), channel_id=1, source_target_pairs={{0,1},{1,0},{2,3},{3,2},{4,5},{5,4},{6,7},{7,6},{8,9},{9,8},{10,11... | collective-permute-start | bytes 2949128 | tf_op jit(solution)/shard_map/ppermute | solution.py:896
  125.7 24.0 %collective-permute-start.23 = (bf16[4,480,256]{2,1,0:T(8,128)(2,1)}, bf16[4,480,256]{2,1,0:T(8,128)(2,1)S(1)}, u32[]{:S(2)}, u32[]{:S(2)}) collective-permute-start(bf16[4,480,256]{2,1,0:T(8,128)(2,1)} %collective-permute-done.16.refs_9_.refs_1_), channel_id=1, source_target_pairs={{0,4},{2,6},{4,0},{6,2},{8,12},{10,14},{12,8},{14,10},{16,20},{18,... | collective-permute-start | bytes 2949128 | tf_op jit(solution)/shard_map/ppermute | solution.py:900
  127.0 23.6 %collective-permute-start.24 = (bf16[4,480,256]{2,1,0:T(8,128)(2,1)}, bf16[4,480,256]{2,1,0:T(8,128)(2,1)S(1)}, u32[]{:S(2)}, u32[]{:S(2)}) collective-permute-start(bf16[4,480,256]{2,1,0:T(8,128)(2,1)} %collective-permute-done.17.refs_14_.refs_6_), channel_id=1, source_target_pairs={{0,2},{2,0},{4,6},{6,4},{8,10},{10,8},{12,14},{14,12},{16,18},{18,... | collective-permute-start | bytes 2949128 | tf_op jit(solution)/shard_map/ppermute | solution.py:900
  128.5 22.1 %collective-permute-start.27 = (bf16[4,480,256]{2,1,0:T(8,128)(2,1)S(1)}, bf16[4,480,256]{2,1,0:T(8,128)(2,1)}, u32[]{:S(2)}, u32[]{:S(2)}) collective-permute-start(bf16[4,480,256]{2,1,0:T(8,128)(2,1)S(1)} %collective-permute-done.19.refs_13_.refs_5_), channel_id=1, source_target_pairs={{0,1},{1,0},{2,3},{3,2},{4,5},{5,4},{6,7},{7,6},{8,9},{9,8},{10,11... | collective-permute-start | bytes 2949128 | tf_op jit(solution)/shard_map/ppermute | solution.py:896
  128.5 22.1 %collective-permute-start.26 = (bf16[4,480,256]{2,1,0:T(8,128)(2,1)S(1)}, bf16[4,480,256]{2,1,0:T(8,128)(2,1)}, u32[]{:S(2)}, u32[]{:S(2)}) collective-permute-start(bf16[4,480,256]{2,1,0:T(8,128)(2,1)S(1)} %collective-permute-done.18.refs_10_.refs_2_), channel_id=1, source_target_pairs={{0,1},{1,0},{2,3},{3,2},{4,5},{5,4},{6,7},{7,6},{8,9},{9,8},{10,11... | collective-permute-start | bytes 2949128 | tf_op jit(solution)/shard_map/ppermute | solution.py:896
  189.0 37.0 %collective-permute-start.30 = (bf16[16,640,256]{2,1,0:T(8,128)(2,1)}, bf16[16,640,256]{2,1,0:T(8,128)(2,1)S(1)}, u32[]{:S(2)}, u32[]{:S(2)}) collective-permute-start(bf16[16,640,256]{2,1,0:T(8,128)(2,1)} %get-tuple-element.223), channel_id=1, source_target_pairs={{0,1},{1,0},{2,3},{3,2},{4,5},{5,4},{6,7},{7,6},{8,9},{9,8},{10,11... | collective-permute-start | bytes 15728648 | tf_op jit(solution)/shard_map/ppermute | solution.py:896
  225.6 32.8 %collective-permute-start.33 = (bf16[2,2560,256]{2,1,0:T(8,128)(2,1)}, bf16[2,2560,256]{2,1,0:T(8,128)(2,1)S(1)}, u32[]{:S(2)}, u32[]{:S(2)}) collective-permute-start(bf16[2,2560,256]{2,1,0:T(8,128)(2,1)} %get-tuple-element.234), channel_id=1, source_target_pairs={{0,1},{1,0},{2,3},{3,2},{4,5},{5,4},{6,7},{7,6},{8,9},{9,8},{10,11... | collective-permute-start | bytes 7864328 | tf_op jit(solution)/shard_map/ppermute | solution.py:896
  233.7 34.4 %collective-permute-start.31 = (bf16[8,320,256]{2,1,0:T(8,128)(2,1)}, bf16[8,320,256]{2,1,0:T(8,128)(2,1)S(1)}, u32[]{:S(2)}, u32[]{:S(2)}) collective-permute-start(bf16[8,320,256]{2,1,0:T(8,128)(2,1)} %get-tuple-element.232), channel_id=1, source_target_pairs={{0,2},{2,0},{4,6},{6,4},{8,10},{10,8},{12,14},{14,12},{16,18},{18,... | collective-permute-start | bytes 3932168 | tf_op jit(solution)/shard_map/ppermute | solution.py:900
  235.2 32.9 %collective-permute-start.32 = (bf16[8,320,256]{2,1,0:T(8,128)(2,1)}, bf16[8,320,256]{2,1,0:T(8,128)(2,1)S(1)}, u32[]{:S(2)}, u32[]{:S(2)}) collective-permute-start(bf16[8,320,256]{2,1,0:T(8,128)(2,1)} %get-tuple-element.233), channel_id=1, source_target_pairs={{0,4},{2,6},{4,0},{6,2},{8,12},{10,14},{12,8},{14,10},{16,20},{18,... | collective-permute-start | bytes 3932168 | tf_op jit(solution)/shard_map/ppermute | solution.py:900
  266.3 42.8 %collective-permute-start.37 = (bf16[8,224,256]{2,1,0:T(8,128)(2,1)}, bf16[8,224,256]{2,1,0:T(8,128)(2,1)S(1)}, u32[]{:S(2)}, u32[]{:S(2)}) collective-permute-start(bf16[8,224,256]{2,1,0:T(8,128)(2,1)} %get-tuple-element.251), channel_id=1, source_target_pairs={{0,2},{2,0},{4,6},{6,4},{8,10},{10,8},{12,14},{14,12},{16,18},{18,... | collective-permute-start | bytes 2752520 | tf_op jit(solution)/shard_map/ppermute | solution.py:900
  266.9 42.2 %collective-permute-start.38 = (bf16[8,224,256]{2,1,0:T(8,128)(2,1)}, bf16[8,224,256]{2,1,0:T(8,128)(2,1)S(1)}, u32[]{:S(2)}, u32[]{:S(2)}) collective-permute-start(bf16[8,224,256]{2,1,0:T(8,128)(2,1)} %get-tuple-element.252), channel_id=1, source_target_pairs={{0,4},{2,6},{4,0},{6,2},{8,12},{10,14},{12,8},{14,10},{16,20},{18,... | collective-permute-start | bytes 2752520 | tf_op jit(solution)/shard_map/ppermute | solution.py:900
  270.5 42.6 %collective-permute-start.35 = (bf16[4,320,256]{2,1,0:T(8,128)(2,1)}, bf16[4,320,256]{2,1,0:T(8,128)(2,1)S(1)}, u32[]{:S(2)}, u32[]{:S(2)}) collective-permute-start(bf16[4,320,256]{2,1,0:T(8,128)(2,1)} %get-tuple-element.245), channel_id=1, source_target_pairs={{0,4},{2,6},{4,0},{6,2},{8,12},{10,14},{12,8},{14,10},{16,20},{18,... | collective-permute-start | bytes 1966088 | tf_op jit(solution)/shard_map/ppermute | solution.py:900
  271.3 41.8 %collective-permute-start.36 = (bf16[4,320,256]{2,1,0:T(8,128)(2,1)}, bf16[4,320,256]{2,1,0:T(8,128)(2,1)S(1)}, u32[]{:S(2)}, u32[]{:S(2)}) collective-permute-start(bf16[4,320,256]{2,1,0:T(8,128)(2,1)} %get-tuple-element.246), channel_id=1, source_target_pairs={{0,2},{2,0},{4,6},{6,4},{8,10},{10,8},{12,14},{14,12},{16,18},{18,... | collective-permute-start | bytes 1966088 | tf_op jit(solution)/shard_map/ppermute | solution.py:900
  342.4 31.4 %collective-permute-start.56 = (bf16[2,224,256]{2,1,0:T(8,128)(2,1)S(1)}, bf16[2,224,256]{2,1,0:T(8,128)(2,1)}, u32[]{:S(2)}, u32[]{:S(2)}) collective-permute-start(bf16[2,224,256]{2,1,0:T(8,128)(2,1)S(1)} %get-tuple-element.291), channel_id=1, source_target_pairs={{0,24},{2,26},{4,28},{6,30},{8,0},{10,2},{12,4},{14,6},{16,8},{18,... | collective-permute-start | bytes 688136 | tf_op jit(solution)/shard_map/ppermute | solution.py:916
  (76 other events, 907.5 us)

commit v2 on v1

--- a/solution.py
+++ b/solution.py
@@ -19,9 +19,8 @@
 LANES = 128
 QKV = (HEADS + 2 * KV_HEADS) * HEAD
 QKV_PAD = 1664
-VMEM_LIMIT = 56 * 1024 * 1024
 PACK = 1408
-VMEM_SMALL = 24 * 1024 * 1024
+MIB = 1024 * 1024
 WIDE_HEADS = HEADS * LANES
 F32 = jnp.float32
 BF16 = jnp.bfloat16
@@ -44,7 +43,7 @@
 
 
 def call(body, out_shape, grid, in_specs, out_specs, scratch=(), flops=0, moved=0, prefetch=0, alias=None,
-         vmem=VMEM_LIMIT):
+         vmem=8):
     return pl.pallas_call(
         body,
         out_shape=out_shape,
@@ -56,7 +55,7 @@
             scratch_shapes=scratch,
         ),
         input_output_aliases=alias or {},
-        compiler_params=pltpu.CompilerParams(vmem_limit_bytes=vmem),
+        compiler_params=pltpu.CompilerParams(vmem_limit_bytes=vmem * MIB),
         cost_estimate=pl.CostEstimate(flops=flops, bytes_accessed=moved, transcendentals=0),
     )
 
@@ -185,6 +184,7 @@
         scratch=[pltpu.VMEM((2, wide, PACK), BF16)],
         flops=2 * seq * wide * (width + QKV_PAD),
         moved=20_000_000,
+        vmem=56,
         prefetch=1,
     )(place, own, other, spread, *pieces, cos, sa, sb, aq, ak)
 
@@ -229,6 +229,7 @@
         [group, group],
         flops=4 * HEADS * seq * seq * LANES,
         moved=15_000_000,
+        vmem=56,
     )(q, k, v)
 
 
@@ -295,6 +296,7 @@
         scratch=[pltpu.VMEM((GROUP, seq, LANES), F32)],
         flops=10 * GROUP * count * seq * seq * LANES,
         moved=4_000_000 * count,
+        vmem=12,
     )(q, k, v, do, delta, cos, sa, sb)
 
 
@@ -345,6 +347,7 @@
         [rows(wide)] * 4,
         flops=2 * seq * wide * 4 * wide,
         moved=22_000_000,
+        vmem=56,
         prefetch=1,
     )(place, o, own, other, spread, unpack, w_out, xp, gain)
 
@@ -437,7 +440,7 @@
     seq, wide = b.shape
     blocks, chunks, chunk = 16, 5, 256
     columns = mine if turn else other
-    any_spec = pl.BlockSpec(memory_space=pl.ANY)
+    any_spec = pl.BlockSpec(memory_space=pltpu.HBM)
     half_of = lambda place: place[0] if turn else 1 - place[0]
     d_shape = jax.ShapeDtypeStruct((2, 2 * chunks * chunk, chunk), BF16)
     d_spec = pl.BlockSpec((2, chunk, chunk), lambda s, place: (0, half_of(place) * chunks + s, 0))
@@ -471,6 +474,7 @@
         + turn * [pltpu.SemaphoreType.DMA] * 2,
         flops=18 * seq * wide * chunks * chunk,
         moved=40_000_000,
+        vmem=56,
         prefetch=1,
         alias={27: 3, 28: 4} if before else None,
     )(place, b, df, *columns, *mine, *other, *before)
@@ -577,6 +581,7 @@
         scratch=[pltpu.VMEM((seq, wide), BF16)],
         flops=2 * seq * wide * 6 * wide,
         moved=40_000_000,
+        vmem=56,
         prefetch=1,
     )(place, m, db, df, *consts)
 
@@ -602,6 +607,7 @@
         token_specs(steps, block, width),
         flops=2 * seq * wide * wide,
         moved=16_000_000,
+        vmem=8,
         prefetch=1,
     )(place, m, acc, spread)
 
@@ -663,6 +669,7 @@
         ],
         flops=2 * seq * wide * QKV_PAD,
         moved=20_000_000,
+        vmem=28,
         prefetch=1,
     )(place, *parts, a, w_qkv, gain, dgain_ffn)
 
@@ -719,6 +726,7 @@
         [out],
         flops=seq * wide * (QKV_PAD + width),
         moved=10_000_000,
+        vmem=56 if keep else 8,
         prefetch=1,
     )(place, flat, w_qkv, xp, em, gain, spread, *([got] if keep else []))[0]
 
@@ -751,8 +759,8 @@
         [pl.BlockSpec((2, rows, n), lambda i, place: (i, 0, 0))] * 4,
         flops=1,
         moved=16 * count * rows * n * 6,
+        vmem=24,
         prefetch=1,
-        vmem=VMEM_SMALL,
     )(place, *arrays)
 
 
@@ -776,8 +784,8 @@
         [pl.BlockSpec((1, rows, n), lambda i, place: (i, 0, 0))] * 4,
         flops=1,
         moved=blocks * rows * n * 12,
+        vmem=24,
         prefetch=1,
-        vmem=VMEM_SMALL,
     )(place, keeps[0], gots[0], keeps[1], gots[1])
 
 
@@ -802,8 +810,8 @@
         [whole((2, rows, n))] * 4,
         flops=1,
         moved=rows * n * 50,
+        vmem=24,
         prefetch=1,
-        vmem=VMEM_SMALL,
     )(place, keeps[0], gots[0], keeps[1], gots[1])
 
 
@@ -1040,14 +1048,14 @@
     level = rise(shard, count)
     x_own, x_other = halves(inputs)
     ct_own, ct_other = halves(cotangent)
-    stack = tie(jnp.stack(level), spread, delta_sum, *table, x_other, ct_other)
+    stack = tie(jnp.stack(level), packed, x_other, ct_other)
     part = spread_first(stack, count)
     packed = tie(packed, stack)
     up, down = along_z(packed, 1, count), along_z(packed, 3, count)
-    near_far = spread_second(*tie_all(part, unpack), count)
+    near_far = spread_second(*part, count)
     up, down = tie_all((up, down), part[0])
     up_two = along_z(up, 1, count)
-    near_far = tie_all(near_far, up_two, down)
+    near_far = tie_all(near_far, up_two, down, spread, delta_sum, unpack, *table)
     pieces = near_far + tuple(swap(t) for t in near_far)
     packs = jnp.stack(tie_all((packed, up, up_two, down), near_far[0]))
     half = packs.shape[1] // 2
@@ -1106,19 +1114,21 @@
     flat = tie(flat, *two.sent, *three.sent)
     gi_send = input_back(place_of, flat, w_qkv, xp, em, gains, spread, width)
     *three.got, one_up, two_up = tie_all((*three.got, one_up, two_up), gi_send)
-    gi_got = swap(tie(gi_send, one_up))
-    three.turn(one_up)
+    three.turn(gi_send)
     three.move_again()
-    two_up, two_down = two.go_up(two_up), two.start_down()
+    gi_got = swap(tie(gi_send, *three.sent))
+    two_up = two.go_up(tie(two_up, *three.sent))
+    two.sent[2] = tie(two.sent[2], *three.sent)
+    two_down = two.start_down()
     out_send, outs = finish(place_of, tie(m, *three.sent), acc, spread, width)
-    *three.got, gi_got = tie_all((*three.got, gi_got), outs)
+    first = tie(one.total(one_up, one_down), outs)
+    *three.got, gi_got, two_up = tie_all((*three.got, gi_got, two_up), outs)
     three.climb(gi_got)
     last_got = three.move_up()
     out_got = swap(out_send)
     gis = input_back(place_of, tie(flat, *three.sent, out_send), w_qkv, xp, em, gains, spread, width, gi_got)
     last_got = tie_all(last_got, gis)
     outs = put_other(outs, tie(out_got, gis), core)
-    first = one.total(one_up, one_down)
     second, third = two.total(two_up, two_down), three.total(*last_got)
     third = third.reshape(64, 896)[:per]
     gu = first.reshape(5, 2, 64, 256)

time: 403 us -> 393 us (0.975)
  Pallas kernels: 245 us -> 226 us
  waiting for transfers between devices: 55.4 us -> 68.5 us
    ppermute x15, waiting for transfers between devices: 31.9 us -> 43.2 us  [along_z(): lax.ppermute(x, 'dp', [(i, (i + 4 * step) % count) for i in range(count)])]
    pallas_call x1, Pallas kernels: 14.6 us -> 7.85 us  [projections_back(): call(weights_body, [jax.ShapeDtypeStruct((seq, QKV_PAD), BF16), jax.Shape...]
    pallas_call x2, Pallas kernels: 20.1 us -> 15.7 us  [input_back(): call(functools.partial(input_body, width, keep), [shape], (steps * (2 if...]
    unnamed x94 -> x106, local copies, waits for them, and re-layouts: 13.9 us -> 13 us
  transfers between devices with their start and end apart: 57 -> 57, of which waited for: 17 -> 20; matrix products, arithmetic and copies ran while one was open for 7% -> 7% of each run, Pallas kernels for 53% -> 49%
where the time goes in v2:
time: 393 us; the launch traced here: 387 us
  Pallas kernels  226 us (58%)
  waiting for transfers between devices  68.5 us (17%)
  starting transfers between devices  48.1 us (12%)
  local copies, waits for them, and re-layouts  27.9 us (7%)
  other arithmetic  15.2 us (4%)
    pallas_call x2, Pallas kernels, feed_forward(): call(functools.partial(ffn_body, turn), [jax.ShapeDtypeStruct((seq, wide)...  69.6 us
    ppermute x15, waiting for transfers between devices, along_z(): lax.ppermute(x, 'dp', [(i, (i + 4 * step) % count) for i in range(count)])  43.2 us
    pallas_call x1, Pallas kernels, attend_back(): call(functools.partial(attend_back_body, block), [jax.ShapeDtypeStruct((G...  34.2 us
    pallas_call x1, Pallas kernels, attend(): call(functools.partial(attend_body, block), [shape, shape], (KV_HEADS,),...  24.9 us
    ppermute x22, starting transfers between devices, across(): return lax.ppermute(x, 'dp', [(i, i ^ 1 << bit) for i in range(count)])  22.4 us
    pallas_call x1, Pallas kernels, after(): call(functools.partial(post_body, width), [jax.ShapeDtypeStruct((seq, wid...  22.3 us
    ppermute x15, starting transfers between devices, along_z(): lax.ppermute(x, 'dp', [(i, (i + 4 * step) % count) for i in range(count)])  21.4 us
    pallas_call x1, Pallas kernels, pre_attention(): call(functools.partial(pre_body, width), [jax.ShapeDtypeStruct((seq, wide...  18.4 us
  transfers between devices with their start and end apart: 57, of which 20 were waited for; matrix products, arithmetic and copies ran while one was open for 7% of the time, Pallas kernels for 49%

profile of v2, /device:TPU:0, one launch (start us, length us, event | category | flops | bytes accessed | tf_op | source)
XLA Modules:
  0.0 387.2 jit_solution(13075049767619156052)
XLA Ops:
  4.4 4.1 %collective-permute-start.2 = (bf16[64,1408]{1,0:T(8,128)(2,1)S(1)}, bf16[64,1408]{1,0:T(8,128)(2,1)S(1)}, u32[]{:S(2)}, u32[]{:S(2)}) collective-permute-start(bf16[64,1408]{1,0:T(8,128)(2,1)S(1)} %get-tuple-element.362), channel_id=1, source_target_pairs={{0,16},{2,18},{4,20},{6,22},{8,24},{10,26},{12,28},{14,30},{16,0},... | collective-permute-start | bytes 540680 | tf_op jit(solution)/shard_map/ppermute | solution.py:924
  18.6 3.2 fusion.5
  32.0 4.0 %collective-permute-done.5 = bf16[4,32,1408]{2,1,0:T(8,128)(2,1)S(1)} collective-permute-done((bf16[4,32,1408]{2,1,0:T(8,128)(2,1)S(1)}, bf16[4,32,1408]{2,1,0:T(8,128)(2,1)S(1)}, u32[]{:S(2)}, u32[]{:S(2)}) %collective-permute-start.5) | collective-permute-done | bytes 360480 | tf_op jit(solution)/shard_map/ppermute | solution.py:908
  42.6 13.0 %collective-permute-done.9 = bf16[960,256]{1,0:T(8,128)(2,1)S(1)} collective-permute-done((bf16[960,256]{1,0:T(8,128)(2,1)S(1)}, bf16[960,256]{1,0:T(8,128)(2,1)S(1)}, u32[]{:S(2)}, u32[]{:S(2)}) %collective-permute-start.9) | collective-permute-done | bytes 491552 | tf_op jit(solution)/shard_map/ppermute | solution.py:924
  55.6 3.5 fusion.u_ref
  59.0 10.0 %collective-permute-done.11 = bf16[960,256]{1,0:T(8,128)(2,1)S(1)} collective-permute-done((bf16[960,256]{1,0:T(8,128)(2,1)S(1)}, bf16[960,256]{1,0:T(8,128)(2,1)S(1)}, u32[]{:S(2)}, u32[]{:S(2)}) %collective-permute-start.11) | collective-permute-done | bytes 491552 | tf_op jit(solution)/shard_map/ppermute | solution.py:924
  74.7 18.4 %shard_map.212 = (bf16[1024,1024]{1,0:T(8,128)(2,1)}, bf16[1024,1024]{1,0:T(8,128)(2,1)}, bf16[15,1024,128]{2,1,0:T(8,128)(2,1)}, bf16[5,1024,128]{2,1,0:T(8,128...) custom-call(s32[4]{0:T(128)} %pad_add_fusion.place_ref, ...), custom_call_target="tpu_custom_call" | custom-call | flops 5502926848 | bytes 20000000 | tf_op jit(solution)/shard_map/pallas_call | solution.py:165
  97.9 24.9 %shard_map.213 = (bf16[15,1024,128]{2,1,0:T(8,128)(2,1)}, bf16[15,1024,128]{2,1,0:T(8,128)(2,1)}) custom-call(bf16[15,1024,128]{2,1,0:T(8,128)(2,1)} %get-tuple-element.191.q_ref, bf16[5,1024,128]{2,1,0:T(8,128)(2,1)} %get-tuple-element.192.k_ref, bf16[5,1024,128]{2,1,0:T(8,128)(2,1)} %get-tuple-element.193.v_ref), custom_call_target="tpu_custom_call" | custom-call | flops 8053063680 | bytes 15000000 | tf_op jit(solution)/shard_map/pallas_call | solution.py:224
  126.6 16.4 %shard_map.214 = (bf16[1024,1024]{1,0:T(8,128)(2,1)}, f32[1024,1024]{1,0:T(8,128)}, bf16[1024,1024]{1,0:T(8,128)(2,1)}, bf16[1024,1024]{1,0:T(8,128)(2,1)}) custom-call(s32[4]{0:T(128)} %pad_add_fusion.place_ref, bf16[15,1024,128]{2,1,0:T(8,128)(2,1)} %get-tuple-element.202.o_ref, bf16[960,512]{1,0:T(8,128)(2,1)} %get-tuple-element.349.own_ref, ...), custom_call_target="tpu_custom_call" | custom-call | flops 8589934592 | bytes 22000000 | tf_op jit(solution)/shard_map/pallas_call | solution.py:329
  143.1 4.3 %collective-permute-done.23.refs_11_.refs_3_ = bf16[4,480,256]{2,1,0:T(8,128)(2,1)S(1)} collective-permute-done((bf16[4,480,256]{2,1,0:T(8,128)(2,1)}, bf16[4,480,256]{2,1,0:T(8,128)(2,1)S(1)}, u32[]{:S(2)}, u32[]{:S(2)}) %collective-permute-start.23) | collective-permute-done | bytes 983072 | tf_op jit(solution)/shard_map/ppermute | solution.py:908
  153.3 33.4 %shard_map.215 = (f32[1024,1024]{1,0:T(8,128)}, f32[1024,1024]{1,0:T(8,128)}, bf16[16,640,256]{2,1,0:T(8,128)(2,1)}, bf16[2,2560,256]{2,1,0:T(8,128)(2,1)}, bf16[2,2560,256]{2,1,0:T(8,128)(2,1)}) custom-call(s32[4]{0:T(128)} %pad_add_fusion.place_ref, bf16[1024,1024]{1,0:T(8,128)(2,1)} %get-tuple-element.220.b_ref, ...), custom_call_target="tpu_custom_call" | custom-call | flops 24159191040 | bytes 40000000 | tf_op jit(solution)/shard_map/pallas_call | solution.py:447
  186.9 36.3 %shard_map.216 = (f32[1024,1024]{1,0:T(8,128)}, f32[1024,1024]{1,0:T(8,128)}, bf16[16,640,256]{2,1,0:T(8,128)(2,1)}, bf16[2,2560,256]{2,1,0:T(8,128)(2,1)}, bf16[2,2560,256]{2,1,0:T(8,128)(2,1)}) custom-call(s32[4]{0:T(128)} %pad_add_fusion.place_ref, bf16[1024,1024]{1,0:T(8,128)(2,1)} %get-tuple-element.220.b_ref, ...), custom_call_target="tpu_custom_call", output_to_operand_aliasing={{3}: (27, {}), {4}: (28, {})} | custom-call | flops 24159191040 | bytes 40000000 | tf_op jit(solution)/shard_map/pallas_call | solution.py:447
  226.1 3.0 shard_map.217
  233.6 22.3 %shard_map.218 = (f32[1024,1024]{1,0:T(8,128)}, bf16[15,1024,128]{2,1,0:T(8,128)(2,1)}, f32[40,1024]{1,0:T(8,128)}, bf16[2,16,64,256]{3,2,1,0:T(8,128)(2,1)}, bf...) custom-call(s32[4]{0:T(128)} %pad_add_fusion.place_ref, f32[1024,1024]{1,0:T(8,128)} %get-tuple-element.296.m_ref, ...), custom_call_target="tpu_custom_call" | custom-call | flops 12884901888 | bytes 40000000 | tf_op jit(solution)/shard_map/pallas_call | solution.py:561
  269.8 34.2 %shard_map.221 = (bf16[15,1024,128]{2,1,0:T(8,128)(2,1)S(1)}, bf16[5,1024,128]{2,1,0:T(8,128)(2,1)S(1)}, bf16[5,1024,128]{2,1,0:T(8,128)(2,1)S(1)}) custom-call(bf16[15,1024,128]{2,1,0:T(8,128)(2,1)S(1)} %copy-done.23, bf16[5,1024,128]{2,1,0:T(8,128)(2,1)S(1)} %copy-done.21, bf16[5,1024,128]{2,1,0:T(8,128)(2,1)S(1)} %copy-done.22, ...), custom_call_target="tpu_custom_call" | custom-call | flops 20132659200 | bytes 20000000 | tf_op jit(solution)/shard_map/pallas_call | solution.py:284
  307.8 3.8 collective-permute-start.40
  311.6 7.9 %shard_map.224 = (bf16[1024,1664]{1,0:T(8,128)(2,1)S(1)}, bf16[16,64,896]{2,1,0:T(8,128)(2,1)S(1)}, bf16[16,64,896]{2,1,0:T(8,128)(2,1)S(1)}) custom-call(s32[4]{0:T(128)S(1)} %copy-done.19, bf16[15,1024,128]{2,1,0:T(8,128)(2,1)S(1)} %get-tuple-element.251.dq_ref, bf16[5,1024,128]{2,1,0:T(8,128)(2,1)S(1)} %get-tuple-element.252.dk_ref, ...), custom_call_target="tpu_custom_call" | custom-call | flops 3489660928 | bytes 20000000 | tf_op jit(solution)/shard_map/pallas_call | solution.py:655
  323.0 3.8 collective-permute-done.43.refs_1_
  331.2 2.9 collective-permute-start.47
  334.1 4.6 %shard_map.227 = bf16[960,512]{1,0:T(8,128)(2,1)S(1)} custom-call(s32[4]{0:T(128)S(1)} %copy-done.19, bf16[1024,1664]{1,0:T(8,128)(2,1)S(1)} %get-tuple-element.312.flat_ref, bf16[1024,1664]{1,0:T(8,128)(2,1)S(1)} %copy-done.2, bf16[1024,1024]{1,0:T(8,128)(2,1)S(1)} %copy-done.4, f32[1024,1024]{1,0:T(8,128)S(1)} %copy-done.1, f32[8,1024]{1,0:T(8,128)S(1)} %copy-done.17, ...), custom_call_target="tpu_custom_call" | custom-call | flops 2751463424 | bytes 10000000 | tf_op jit(solution)/shard_map/pallas_call | solution.py:721
  338.7 7.6 %collective-permute-done.47 = bf16[2,224,256]{2,1,0:T(8,128)(2,1)S(1)} collective-permute-done((bf16[2,224,256]{2,1,0:T(8,128)(2,1)S(1)}, bf16[2,224,256]{2,1,0:T(8,128)(2,1)S(1)}, u32[]{:S(2)}, u32[]{:S(2)}) %collective-permute-start.47) | collective-permute-done | bytes 229408 | tf_op jit(solution)/shard_map/ppermute | solution.py:924
  349.0 4.7 %shard_map.229 = (bf16[960,512]{1,0:T(8,128)(2,1)S(1)}, bf16[2,960,512]{2,1,0:T(8,128)(2,1)}) custom-call(s32[4]{0:T(128)S(1)} %copy-done.19, f32[1024,1024]{1,0:T(8,128)S(1)} %copy-done.6, f32[1024,1024]{1,0:T(8,128)S(1)} %copy-done.7, bf16[1024,1024]{1,0:T(8,128)(2,1)S(1)} %copy-done), custom_call_target="tpu_custom_call" | custom-call | flops 2147483648 | bytes 16000000 | tf_op jit(solution)/shard_map/pallas_call | solution.py:599
  356.3 7.5 %collective-permute-done.52 = bf16[2,224,256]{2,1,0:T(8,128)(2,1)S(1)} collective-permute-done((bf16[2,224,256]{2,1,0:T(8,128)(2,1)S(1)}, bf16[2,224,256]{2,1,0:T(8,128)(2,1)S(1)}, u32[]{:S(2)}, u32[]{:S(2)}) %collective-permute-start.52) | collective-permute-done | bytes 229408 | tf_op jit(solution)/shard_map/ppermute | solution.py:924
  369.0 11.1 %shard_map.231 = f32[2,960,512]{2,1,0:T(8,128)} custom-call(s32[4]{0:T(128)} %pad_add_fusion.place_ref, bf16[1024,1664]{1,0:T(8,128)(2,1)} %copy-done.3, bf16[1024,1664]{1,0:T(8,128)(2,1)} %get-tuple-element.269.w_ref, bf16[1024,1024]{1,0:T(8,128)(2,1)} %get-tuple-element.204.xp_ref, f32[1024,1024]{1,0:T(8,128)} %get-tuple-element.237.em_ref, ...), custom_call_target="tpu_custom_call" | custom-call | flops 2751463424 | bytes 10000000 | tf_op jit(solution)/shard_map/pallas_call | solution.py:721
  (279 shorter events, 100.6 us)
Async XLA Ops:
  30.2 25.4 %collective-permute-start.9 = (bf16[960,256]{1,0:T(8,128)(2,1)S(1)}, bf16[960,256]{1,0:T(8,128)(2,1)S(1)}, u32[]{:S(2)}, u32[]{:S(2)}) collective-permute-start(bf16[960,256]{1,0:T(8,128)(2,1)S(1)} %maximum_bitcast_fusion), channel_id=1, source_target_pairs={{0,8},{2,10},{4,12},{6,14},{8,16},{10,18},{12,20},{14,22},{16,24},... | collective-permute-start | bytes 1474568 | tf_op jit(solution)/shard_map/ppermute | solution.py:924
  36.1 32.9 %collective-permute-start.6 = (bf16[8,32,1408]{2,1,0:T(8,128)(2,1)S(1)}, bf16[8,32,1408]{2,1,0:T(8,128)(2,1)S(1)}, u32[]{:S(2)}, u32[]{:S(2)}) collective-permute-start(bf16[8,32,1408]{2,1,0:T(8,128)(2,1)S(1)} %pad_maximum_fusion.2.refs_0_), channel_id=1, source_target_pairs={{0,4},{2,6},{4,0},{6,2},{8,12},{10,14},{12,8},{14,10},{16,20},{18,... | collective-permute-start | bytes 2162696 | tf_op jit(solution)/shard_map/ppermute | solution.py:908
  40.0 29.0 %collective-permute-start.8 = (bf16[8,32,1408]{2,1,0:T(8,128)(2,1)}, bf16[8,32,1408]{2,1,0:T(8,128)(2,1)}, u32[]{:S(2)}, u32[]{:S(2)}) collective-permute-start(bf16[8,32,1408]{2,1,0:T(8,128)(2,1)} %pad_maximum_fusion.3.refs_2_), channel_id=1, source_target_pairs={{0,2},{2,0},{4,6},{6,4},{8,10},{10,8},{12,14},{14,12},{16,18},{18,... | collective-permute-start | bytes 2162696 | tf_op jit(solution)/shard_map/ppermute | solution.py:908
  70.5 23.9 %collective-permute-start.17 = (bf16[4,480,256]{2,1,0:T(8,128)(2,1)S(1)}, bf16[4,480,256]{2,1,0:T(8,128)(2,1)}, u32[]{:S(2)}, u32[]{:S(2)}) collective-permute-start(bf16[4,480,256]{2,1,0:T(8,128)(2,1)S(1)} %get-tuple-element.196.refs_12_.refs_4_), channel_id=1, source_target_pairs={{0,4},{2,6},{4,0},{6,2},{8,12},{10,14},{12,8},{14,10},{16,20},{18,... | collective-permute-start | bytes 2949128 | tf_op jit(solution)/shard_map/ppermute | solution.py:908
  72.3 23.9 %collective-permute-start.16 = (bf16[4,480,256]{2,1,0:T(8,128)(2,1)S(1)}, bf16[4,480,256]{2,1,0:T(8,128)(2,1)}, u32[]{:S(2)}, u32[]{:S(2)}) collective-permute-start(bf16[4,480,256]{2,1,0:T(8,128)(2,1)S(1)} %get-tuple-element.195.refs_8_.refs_0_), channel_id=1, source_target_pairs={{0,2},{2,0},{4,6},{6,4},{8,10},{10,8},{12,14},{14,12},{16,18},{18,... | collective-permute-start | bytes 2949128 | tf_op jit(solution)/shard_map/ppermute | solution.py:908
  96.2 26.5 %collective-permute-start.20 = (bf16[4,480,256]{2,1,0:T(8,128)(2,1)S(1)}, bf16[4,480,256]{2,1,0:T(8,128)(2,1)S(1)}, u32[]{:S(2)}, u32[]{:S(2)}) collective-permute-start(bf16[4,480,256]{2,1,0:T(8,128)(2,1)S(1)} %get-tuple-element.195.refs_8_.refs_0_), channel_id=1, source_target_pairs={{0,1},{1,0},{2,3},{3,2},{4,5},{5,4},{6,7},{7,6},{8,9},{9,8},{10,11... | collective-permute-start | bytes 2949128 | tf_op jit(solution)/shard_map/ppermute | solution.py:904
  96.2 27.1 %collective-permute-start.18 = (bf16[4,480,256]{2,1,0:T(8,128)(2,1)S(1)}, bf16[4,480,256]{2,1,0:T(8,128)(2,1)S(1)}, u32[]{:S(2)}, u32[]{:S(2)}) collective-permute-start(bf16[4,480,256]{2,1,0:T(8,128)(2,1)S(1)} %get-tuple-element.195.refs_8_.refs_0_), channel_id=1, source_target_pairs={{0,4},{2,6},{4,0},{6,2},{8,12},{10,14},{12,8},{14,10},{16,20},{18,... | collective-permute-start | bytes 2949128 | tf_op jit(solution)/shard_map/ppermute | solution.py:908
  97.1 26.2 %collective-permute-start.21 = (bf16[4,480,256]{2,1,0:T(8,128)(2,1)S(1)}, bf16[4,480,256]{2,1,0:T(8,128)(2,1)S(1)}, u32[]{:S(2)}, u32[]{:S(2)}) collective-permute-start(bf16[4,480,256]{2,1,0:T(8,128)(2,1)S(1)} %get-tuple-element.196.refs_12_.refs_4_), channel_id=1, source_target_pairs={{0,1},{1,0},{2,3},{3,2},{4,5},{5,4},{6,7},{7,6},{8,9},{9,8},{10,11... | collective-permute-start | bytes 2949128 | tf_op jit(solution)/shard_map/ppermute | solution.py:904
  97.3 26.0 %collective-permute-start.19 = (bf16[4,480,256]{2,1,0:T(8,128)(2,1)S(1)}, bf16[4,480,256]{2,1,0:T(8,128)(2,1)S(1)}, u32[]{:S(2)}, u32[]{:S(2)}) collective-permute-start(bf16[4,480,256]{2,1,0:T(8,128)(2,1)S(1)} %get-tuple-element.196.refs_12_.refs_4_), channel_id=1, source_target_pairs={{0,2},{2,0},{4,6},{6,4},{8,10},{10,8},{12,14},{14,12},{16,18},{18,... | collective-permute-start | bytes 2949128 | tf_op jit(solution)/shard_map/ppermute | solution.py:908
  97.9 25.5 %collective-permute-start.22 = (bf16[4,480,256]{2,1,0:T(8,128)(2,1)}, bf16[4,480,256]{2,1,0:T(8,128)(2,1)S(1)}, u32[]{:S(2)}, u32[]{:S(2)}) collective-permute-start(bf16[4,480,256]{2,1,0:T(8,128)(2,1)} %collective-permute-done.16.refs_9_.refs_1_), channel_id=1, source_target_pairs={{0,1},{1,0},{2,3},{3,2},{4,5},{5,4},{6,7},{7,6},{8,9},{9,8},{10,11... | collective-permute-start | bytes 2949128 | tf_op jit(solution)/shard_map/ppermute | solution.py:904
  122.8 20.3 %collective-permute-start.25 = (bf16[4,480,256]{2,1,0:T(8,128)(2,1)}, bf16[4,480,256]{2,1,0:T(8,128)(2,1)S(1)}, u32[]{:S(2)}, u32[]{:S(2)}) collective-permute-start(bf16[4,480,256]{2,1,0:T(8,128)(2,1)} %collective-permute-done.17.refs_14_.refs_6_), channel_id=1, source_target_pairs={{0,1},{1,0},{2,3},{3,2},{4,5},{5,4},{6,7},{7,6},{8,9},{9,8},{10,11... | collective-permute-start | bytes 2949128 | tf_op jit(solution)/shard_map/ppermute | solution.py:904
  123.4 24.0 %collective-permute-start.23 = (bf16[4,480,256]{2,1,0:T(8,128)(2,1)}, bf16[4,480,256]{2,1,0:T(8,128)(2,1)S(1)}, u32[]{:S(2)}, u32[]{:S(2)}) collective-permute-start(bf16[4,480,256]{2,1,0:T(8,128)(2,1)} %collective-permute-done.16.refs_9_.refs_1_), channel_id=1, source_target_pairs={{0,4},{2,6},{4,0},{6,2},{8,12},{10,14},{12,8},{14,10},{16,20},{18,... | collective-permute-start | bytes 2949128 | tf_op jit(solution)/shard_map/ppermute | solution.py:908
  124.6 23.6 %collective-permute-start.24 = (bf16[4,480,256]{2,1,0:T(8,128)(2,1)}, bf16[4,480,256]{2,1,0:T(8,128)(2,1)S(1)}, u32[]{:S(2)}, u32[]{:S(2)}) collective-permute-start(bf16[4,480,256]{2,1,0:T(8,128)(2,1)} %collective-permute-done.17.refs_14_.refs_6_), channel_id=1, source_target_pairs={{0,2},{2,0},{4,6},{6,4},{8,10},{10,8},{12,14},{14,12},{16,18},{18,... | collective-permute-start | bytes 2949128 | tf_op jit(solution)/shard_map/ppermute | solution.py:908
  126.1 22.1 %collective-permute-start.27 = (bf16[4,480,256]{2,1,0:T(8,128)(2,1)S(1)}, bf16[4,480,256]{2,1,0:T(8,128)(2,1)}, u32[]{:S(2)}, u32[]{:S(2)}) collective-permute-start(bf16[4,480,256]{2,1,0:T(8,128)(2,1)S(1)} %collective-permute-done.19.refs_13_.refs_5_), channel_id=1, source_target_pairs={{0,1},{1,0},{2,3},{3,2},{4,5},{5,4},{6,7},{7,6},{8,9},{9,8},{10,11... | collective-permute-start | bytes 2949128 | tf_op jit(solution)/shard_map/ppermute | solution.py:904
  126.1 22.1 %collective-permute-start.26 = (bf16[4,480,256]{2,1,0:T(8,128)(2,1)S(1)}, bf16[4,480,256]{2,1,0:T(8,128)(2,1)}, u32[]{:S(2)}, u32[]{:S(2)}) collective-permute-start(bf16[4,480,256]{2,1,0:T(8,128)(2,1)S(1)} %collective-permute-done.18.refs_10_.refs_2_), channel_id=1, source_target_pairs={{0,1},{1,0},{2,3},{3,2},{4,5},{5,4},{6,7},{7,6},{8,9},{9,8},{10,11... | collective-permute-start | bytes 2949128 | tf_op jit(solution)/shard_map/ppermute | solution.py:904
  186.7 36.9 %collective-permute-start.30 = (bf16[16,640,256]{2,1,0:T(8,128)(2,1)}, bf16[16,640,256]{2,1,0:T(8,128)(2,1)S(1)}, u32[]{:S(2)}, u32[]{:S(2)}) collective-permute-start(bf16[16,640,256]{2,1,0:T(8,128)(2,1)} %get-tuple-element.219), channel_id=1, source_target_pairs={{0,1},{1,0},{2,3},{3,2},{4,5},{5,4},{6,7},{7,6},{8,9},{9,8},{10,11... | collective-permute-start | bytes 15728648 | tf_op jit(solution)/shard_map/ppermute | solution.py:904
  223.1 32.9 %collective-permute-start.33 = (bf16[2,2560,256]{2,1,0:T(8,128)(2,1)}, bf16[2,2560,256]{2,1,0:T(8,128)(2,1)S(1)}, u32[]{:S(2)}, u32[]{:S(2)}) collective-permute-start(bf16[2,2560,256]{2,1,0:T(8,128)(2,1)} %get-tuple-element.230), channel_id=1, source_target_pairs={{0,1},{1,0},{2,3},{3,2},{4,5},{5,4},{6,7},{7,6},{8,9},{9,8},{10,11... | collective-permute-start | bytes 7864328 | tf_op jit(solution)/shard_map/ppermute | solution.py:904
  231.3 32.6 %collective-permute-start.31 = (bf16[8,320,256]{2,1,0:T(8,128)(2,1)}, bf16[8,320,256]{2,1,0:T(8,128)(2,1)S(1)}, u32[]{:S(2)}, u32[]{:S(2)}) collective-permute-start(bf16[8,320,256]{2,1,0:T(8,128)(2,1)} %get-tuple-element.228), channel_id=1, source_target_pairs={{0,2},{2,0},{4,6},{6,4},{8,10},{10,8},{12,14},{14,12},{16,18},{18,... | collective-permute-start | bytes 3932168 | tf_op jit(solution)/shard_map/ppermute | solution.py:908
  232.8 31.1 %collective-permute-start.32 = (bf16[8,320,256]{2,1,0:T(8,128)(2,1)}, bf16[8,320,256]{2,1,0:T(8,128)(2,1)S(1)}, u32[]{:S(2)}, u32[]{:S(2)}) collective-permute-start(bf16[8,320,256]{2,1,0:T(8,128)(2,1)} %get-tuple-element.229), channel_id=1, source_target_pairs={{0,4},{2,6},{4,0},{6,2},{8,12},{10,14},{12,8},{14,10},{16,20},{18,... | collective-permute-start | bytes 3932168 | tf_op jit(solution)/shard_map/ppermute | solution.py:908
  262.1 41.9 %collective-permute-start.37 = (bf16[8,224,256]{2,1,0:T(8,128)(2,1)S(1)}, bf16[8,224,256]{2,1,0:T(8,128)(2,1)S(1)}, u32[]{:S(2)}, u32[]{:S(2)}) collective-permute-start(bf16[8,224,256]{2,1,0:T(8,128)(2,1)S(1)} %get-tuple-element.247), channel_id=1, source_target_pairs={{0,2},{2,0},{4,6},{6,4},{8,10},{10,8},{12,14},{14,12},{16,18},{18,... | collective-permute-start | bytes 2752520 | tf_op jit(solution)/shard_map/ppermute | solution.py:908
  262.8 41.3 %collective-permute-start.38 = (bf16[8,224,256]{2,1,0:T(8,128)(2,1)S(1)}, bf16[8,224,256]{2,1,0:T(8,128)(2,1)S(1)}, u32[]{:S(2)}, u32[]{:S(2)}) collective-permute-start(bf16[8,224,256]{2,1,0:T(8,128)(2,1)S(1)} %get-tuple-element.248), channel_id=1, source_target_pairs={{0,4},{2,6},{4,0},{6,2},{8,12},{10,14},{12,8},{14,10},{16,20},{18,... | collective-permute-start | bytes 2752520 | tf_op jit(solution)/shard_map/ppermute | solution.py:908
  265.2 41.7 %collective-permute-start.35 = (bf16[4,320,256]{2,1,0:T(8,128)(2,1)S(1)}, bf16[4,320,256]{2,1,0:T(8,128)(2,1)S(1)}, u32[]{:S(2)}, u32[]{:S(2)}) collective-permute-start(bf16[4,320,256]{2,1,0:T(8,128)(2,1)S(1)} %get-tuple-element.241), channel_id=1, source_target_pairs={{0,4},{2,6},{4,0},{6,2},{8,12},{10,14},{12,8},{14,10},{16,20},{18,... | collective-permute-start | bytes 1966088 | tf_op jit(solution)/shard_map/ppermute | solution.py:908
  266.2 40.7 %collective-permute-start.36 = (bf16[4,320,256]{2,1,0:T(8,128)(2,1)S(1)}, bf16[4,320,256]{2,1,0:T(8,128)(2,1)S(1)}, u32[]{:S(2)}, u32[]{:S(2)}) collective-permute-start(bf16[4,320,256]{2,1,0:T(8,128)(2,1)S(1)} %get-tuple-element.242), channel_id=1, source_target_pairs={{0,2},{2,0},{4,6},{6,4},{8,10},{10,8},{12,14},{14,12},{16,18},{18,... | collective-permute-start | bytes 1966088 | tf_op jit(solution)/shard_map/ppermute | solution.py:908
  353.7 26.4 %collective-permute-start.48 = (bf16[960,512]{1,0:T(8,128)(2,1)S(1)}, bf16[960,512]{1,0:T(8,128)(2,1)S(1)}, u32[]{:S(2)}, u32[]{:S(2)}) collective-permute-start(bf16[960,512]{1,0:T(8,128)(2,1)S(1)} %get-tuple-element.298), channel_id=1, source_target_pairs={{0,1},{1,0},{2,3},{3,2},{4,5},{5,4},{6,7},{7,6},{8,9},{9,8},{10,11... | collective-permute-start | bytes 2949128 | tf_op jit(solution)/shard_map/ppermute | solution.py:904
  (83 other events, 897.9 us)

commit v3 on v2

--- a/solution.py
+++ b/solution.py
@@ -145,7 +145,12 @@
     @pl.when(pl.program_id(0) == 0)
     def _():
         build_weights(place_ref, pieces, stage_ref, w_ref, wo_ref)
-        gain_ref[...] = stage_ref[0, :, 768:896].astype(F32).T[32:40]
+        gain_ref[...] = jnp.zeros_like(gain_ref)
+        step = stage_ref.shape[1] // 16
+        for block in range(16):
+            end = step * (block + 1)
+            tail = stage_ref[0, end - 16 : end, :step].astype(F32)
+            gain_ref[:2, end - step : end] = tail[12:14]
 
     xp = mm_tn(own_or_other(place_ref, own_ref, other_ref), e_ref[:width, :])
     scale = lax.rsqrt(jnp.sum(xp * xp, axis=-1, keepdims=True) / width + EPSILON)
@@ -1028,12 +1033,10 @@
     n_q, n_k = w_query.shape[1], w_key.shape[1]
     n_qkv = n_q + 2 * n_k
 
-    shard = jnp.concatenate(
-        [w_query, w_key, w_value, gain_attn[:, None], gain_ffn[:, None]], axis=1
-    )
-    shard = jnp.pad(shard, ((0, 0), (0, 896 - n_qkv - 2)))
-    shard = jnp.concatenate([shard, pad_cols(w_out, groups)], axis=1)
-    shard = jnp.pad(shard, ((0, 64 - per), (0, 0)))
+    shard = jnp.concatenate([w_query, w_key, w_value], axis=1)
+    shard = jnp.concatenate([jnp.pad(shard, ((0, 0), (0, 896 - n_qkv))), pad_cols(w_out, groups)], axis=1)
+    gain_rows = jnp.pad(jnp.stack([gain_attn, gain_ffn]), ((0, 62 - per), (0, PACK - per)))
+    shard = jnp.concatenate([shard, gain_rows])
     packed = pack_half(w_gate, w_up, w_down, 1, groups)[0]
 
     def halves(x):
@@ -1113,26 +1116,26 @@
     three.move()
     flat = tie(flat, *two.sent, *three.sent)
     gi_send = input_back(place_of, flat, w_qkv, xp, em, gains, spread, width)
-    *three.got, one_up, two_up = tie_all((*three.got, one_up, two_up), gi_send)
-    three.turn(gi_send)
+    out_send, outs = finish(place_of, tie(m, gi_send), acc, spread, width)
+    *three.got, one_up, two_up = tie_all((*three.got, one_up, two_up), outs)
+    three.turn(outs)
     three.move_again()
-    gi_got = swap(tie(gi_send, *three.sent))
+    gi_got, out_got = swap(tie(gi_send, *three.sent)), swap(tie(out_send, *three.sent))
     two_up = two.go_up(tie(two_up, *three.sent))
     two.sent[2] = tie(two.sent[2], *three.sent)
     two_down = two.start_down()
-    out_send, outs = finish(place_of, tie(m, *three.sent), acc, spread, width)
-    first = tie(one.total(one_up, one_down), outs)
-    *three.got, gi_got, two_up = tie_all((*three.got, gi_got, two_up), outs)
+    first = tie(one.total(one_up, one_down), *three.sent)
+    wide_of = lambda t: t.transpose(1, 0, 2).reshape(t.shape[1], -1)
+    gu = first.reshape(5, 2, 64, 256)
+    gate, upper = wide_of(gu[:, 0])[:per], wide_of(gu[:, 1])[:per]
+    outs = put_other(outs, out_got, core)
+    *three.got, gi_got, two_up = tie_all((*three.got, gi_got, two_up), outs, gate, upper)
     three.climb(gi_got)
     last_got = three.move_up()
-    out_got = swap(out_send)
-    gis = input_back(place_of, tie(flat, *three.sent, out_send), w_qkv, xp, em, gains, spread, width, gi_got)
+    gis = input_back(place_of, tie(flat, *three.sent), w_qkv, xp, em, gains, spread, width, gi_got)
     last_got = tie_all(last_got, gis)
-    outs = put_other(outs, tie(out_got, gis), core)
     second, third = two.total(two_up, two_down), three.total(*last_got)
     third = third.reshape(64, 896)[:per]
-    gu = first.reshape(5, 2, 64, 256)
-    wide_of = lambda t: t.transpose(1, 0, 2).reshape(t.shape[1], -1)
     tokens = lambda t: jnp.swapaxes(t, 1, 2)[:, None]
     return (
         tokens(outs),
@@ -1141,8 +1144,8 @@
         third[:, n_q : n_q + n_k],
         third[:, n_q + n_k : n_qkv],
         cut_cols(wide_of(second[:, 160:])[:per], per),
-        wide_of(gu[:, 0])[:per],
-        wide_of(gu[:, 1])[:per],
+        gate,
+        upper,
         cut_cols(wide_of(second[:, :160]), per),
         third[:, n_qkv],
         third[:, n_qkv + 1],
@@ -1168,11 +1171,12 @@
     mine, other = (fine_pieces_of(p) for p in packs)
     pieces = []
     for j in range(2):
-        parts = [half(w, j) for w in full[:3]] + [gain_pair.T]
-        part = jnp.concatenate(parts, axis=1)
+        part = jnp.concatenate([half(w, j) for w in full[:3]], axis=1)
         part = jnp.pad(part, ((0, 0), (0, 896 - part.shape[1])))
         part = jnp.concatenate([part, pad_cols(half(w_o, j), count // 2)], axis=1)
-        pieces += pieces_of(pad_rows(part, count))
+        part = pad_rows(part, count)
+        part = part.at[:, per : per + 2, :per].set(gain_pair.reshape(2, count, per).transpose(1, 0, 2))
+        pieces += pieces_of(part)
     which = core // share
 
     def sequence(x):

time: 393 us -> 386 us (0.982)
  waiting for transfers between devices: 68.5 us -> 56.9 us
  starting transfers between devices: 48.1 us -> 55.3 us
    ppermute x15, waiting for transfers between devices: 43.2 us -> 34.3 us  [along_z(): lax.ppermute(x, 'dp', [(i, (i + 4 * step) % count) for i in range(count)])]
    ppermute x15, starting transfers between devices: 21.4 us -> 28.7 us  [along_z(): lax.ppermute(x, 'dp', [(i, (i + 4 * step) % count) for i in range(count)])]
  transfers between devices with their start and end apart: 57 -> 57, of which waited for: 20 -> 20; matrix products, arithmetic and copies ran while one was open for 7% -> 7% of each run, Pallas kernels for 49% -> 50%
where the time goes in v3:
time: 386 us; the launch traced here: 380 us
  Pallas kernels  225 us (58%)
  waiting for transfers between devices  56.9 us (15%)
  starting transfers between devices  55.3 us (14%)
  local copies, waits for them, and re-layouts  24.5 us (6%)
  other arithmetic  15.8 us (4%)
    pallas_call x2, Pallas kernels, feed_forward(): call(functools.partial(ffn_body, turn), [jax.ShapeDtypeStruct((seq, wide)...  69.6 us
    ppermute x15, waiting for transfers between devices, along_z(): lax.ppermute(x, 'dp', [(i, (i + 4 * step) % count) for i in range(count)])  34.3 us
    pallas_call x1, Pallas kernels, attend_back(): call(functools.partial(attend_back_body, block), [jax.ShapeDtypeStruct((G...  34.2 us
    ppermute x15, starting transfers between devices, along_z(): lax.ppermute(x, 'dp', [(i, (i + 4 * step) % count) for i in range(count)])  28.7 us
    pallas_call x1, Pallas kernels, attend(): call(functools.partial(attend_body, block), [shape, shape], (KV_HEADS,),...  24.9 us
    pallas_call x1, Pallas kernels, after(): call(functools.partial(post_body, width), [jax.ShapeDtypeStruct((seq, wid...  22.3 us
    ppermute x22, starting transfers between devices, across(): return lax.ppermute(x, 'dp', [(i, i ^ 1 << bit) for i in range(count)])  22.2 us
    pallas_call x1, Pallas kernels, pre_attention(): call(functools.partial(pre_body, width), [jax.ShapeDtypeStruct((seq, wide...  18.4 us
  transfers between devices with their start and end apart: 57, of which 20 were waited for; matrix products, arithmetic and copies ran while one was open for 7% of the time, Pallas kernels for 50%

profile of v3, /device:TPU:0, one launch (start us, length us, event | category | flops | bytes accessed | tf_op | source)
XLA Modules:
  0.0 379.9 jit_solution(15937215850901660804)
XLA Ops:
  3.5 4.1 %collective-permute-start.2 = (bf16[64,1408]{1,0:T(8,128)(2,1)S(1)}, bf16[64,1408]{1,0:T(8,128)(2,1)S(1)}, u32[]{:S(2)}, u32[]{:S(2)}) collective-permute-start(bf16[64,1408]{1,0:T(8,128)(2,1)S(1)} %pad_maximum_fusion.4), channel_id=1, source_target_pairs={{0,16},{2,18},{4,20},{6,22},{8,24},{10,26},{12,28},{14,30},{16,0},... | collective-permute-start | bytes 540680 | tf_op jit(solution)/shard_map/ppermute | solution.py:929
  18.3 3.2 fusion.5
  31.1 4.0 %collective-permute-done.5 = bf16[4,32,1408]{2,1,0:T(8,128)(2,1)S(1)} collective-permute-done((bf16[4,32,1408]{2,1,0:T(8,128)(2,1)S(1)}, bf16[4,32,1408]{2,1,0:T(8,128)(2,1)S(1)}, u32[]{:S(2)}, u32[]{:S(2)}) %collective-permute-start.5) | collective-permute-done | bytes 360480 | tf_op jit(solution)/shard_map/ppermute | solution.py:913
  41.7 13.0 %collective-permute-done.9 = bf16[960,256]{1,0:T(8,128)(2,1)S(1)} collective-permute-done((bf16[960,256]{1,0:T(8,128)(2,1)S(1)}, bf16[960,256]{1,0:T(8,128)(2,1)S(1)}, u32[]{:S(2)}, u32[]{:S(2)}) %collective-permute-start.9) | collective-permute-done | bytes 491552 | tf_op jit(solution)/shard_map/ppermute | solution.py:929
  54.7 3.5 fusion.u_ref
  58.1 10.0 %collective-permute-done.11 = bf16[960,256]{1,0:T(8,128)(2,1)S(1)} collective-permute-done((bf16[960,256]{1,0:T(8,128)(2,1)S(1)}, bf16[960,256]{1,0:T(8,128)(2,1)S(1)}, u32[]{:S(2)}, u32[]{:S(2)}) %collective-permute-start.11) | collective-permute-done | bytes 491552 | tf_op jit(solution)/shard_map/ppermute | solution.py:929
  73.8 18.4 %shard_map.212 = (bf16[1024,1024]{1,0:T(8,128)(2,1)}, bf16[1024,1024]{1,0:T(8,128)(2,1)}, bf16[15,1024,128]{2,1,0:T(8,128)(2,1)}, bf16[5,1024,128]{2,1,0:T(8,128...) custom-call(s32[4]{0:T(128)} %pad_add_fusion.place_ref, ...), custom_call_target="tpu_custom_call" | custom-call | flops 5502926848 | bytes 20000000 | tf_op jit(solution)/shard_map/pallas_call | solution.py:170
  97.0 24.9 %shard_map.213 = (bf16[15,1024,128]{2,1,0:T(8,128)(2,1)}, bf16[15,1024,128]{2,1,0:T(8,128)(2,1)}) custom-call(bf16[15,1024,128]{2,1,0:T(8,128)(2,1)} %get-tuple-element.191.q_ref, bf16[5,1024,128]{2,1,0:T(8,128)(2,1)} %get-tuple-element.192.k_ref, bf16[5,1024,128]{2,1,0:T(8,128)(2,1)} %get-tuple-element.193.v_ref), custom_call_target="tpu_custom_call" | custom-call | flops 8053063680 | bytes 15000000 | tf_op jit(solution)/shard_map/pallas_call | solution.py:229
  125.7 16.4 %shard_map.214 = (bf16[1024,1024]{1,0:T(8,128)(2,1)}, f32[1024,1024]{1,0:T(8,128)}, bf16[1024,1024]{1,0:T(8,128)(2,1)}, bf16[1024,1024]{1,0:T(8,128)(2,1)}) custom-call(s32[4]{0:T(128)} %pad_add_fusion.place_ref, bf16[15,1024,128]{2,1,0:T(8,128)(2,1)} %get-tuple-element.202.o_ref, bf16[960,512]{1,0:T(8,128)(2,1)} %get-tuple-element.349.own_ref, ...), custom_call_target="tpu_custom_call" | custom-call | flops 8589934592 | bytes 22000000 | tf_op jit(solution)/shard_map/pallas_call | solution.py:334
  142.2 4.3 %collective-permute-done.23.refs_11_.refs_3_ = bf16[4,480,256]{2,1,0:T(8,128)(2,1)S(1)} collective-permute-done((bf16[4,480,256]{2,1,0:T(8,128)(2,1)}, bf16[4,480,256]{2,1,0:T(8,128)(2,1)S(1)}, u32[]{:S(2)}, u32[]{:S(2)}) %collective-permute-start.23) | collective-permute-done | bytes 983072 | tf_op jit(solution)/shard_map/ppermute | solution.py:913
  152.4 33.4 %shard_map.215 = (f32[1024,1024]{1,0:T(8,128)}, f32[1024,1024]{1,0:T(8,128)}, bf16[16,640,256]{2,1,0:T(8,128)(2,1)}, bf16[2,2560,256]{2,1,0:T(8,128)(2,1)}, bf16[2,2560,256]{2,1,0:T(8,128)(2,1)}) custom-call(s32[4]{0:T(128)} %pad_add_fusion.place_ref, bf16[1024,1024]{1,0:T(8,128)(2,1)} %get-tuple-element.220.b_ref, ...), custom_call_target="tpu_custom_call" | custom-call | flops 24159191040 | bytes 40000000 | tf_op jit(solution)/shard_map/pallas_call | solution.py:452
  185.9 36.2 %shard_map.216 = (f32[1024,1024]{1,0:T(8,128)}, f32[1024,1024]{1,0:T(8,128)}, bf16[16,640,256]{2,1,0:T(8,128)(2,1)}, bf16[2,2560,256]{2,1,0:T(8,128)(2,1)}, bf16[2,2560,256]{2,1,0:T(8,128)(2,1)}) custom-call(s32[4]{0:T(128)} %pad_add_fusion.place_ref, bf16[1024,1024]{1,0:T(8,128)(2,1)} %get-tuple-element.220.b_ref, ...), custom_call_target="tpu_custom_call", output_to_operand_aliasing={{3}: (27, {}), {4}: (28, {})} | custom-call | flops 24159191040 | bytes 40000000 | tf_op jit(solution)/shard_map/pallas_call | solution.py:452
  225.2 3.0 shard_map.217
  232.8 22.3 %shard_map.218 = (f32[1024,1024]{1,0:T(8,128)}, bf16[15,1024,128]{2,1,0:T(8,128)(2,1)}, f32[40,1024]{1,0:T(8,128)}, bf16[2,16,64,256]{3,2,1,0:T(8,128)(2,1)}, bf...) custom-call(s32[4]{0:T(128)} %pad_add_fusion.place_ref, f32[1024,1024]{1,0:T(8,128)} %get-tuple-element.288.m_ref, ...), custom_call_target="tpu_custom_call" | custom-call | flops 12884901888 | bytes 40000000 | tf_op jit(solution)/shard_map/pallas_call | solution.py:566
  269.0 34.2 %shard_map.221 = (bf16[15,1024,128]{2,1,0:T(8,128)(2,1)S(1)}, bf16[5,1024,128]{2,1,0:T(8,128)(2,1)S(1)}, bf16[5,1024,128]{2,1,0:T(8,128)(2,1)S(1)}) custom-call(bf16[15,1024,128]{2,1,0:T(8,128)(2,1)S(1)} %copy-done.23, bf16[5,1024,128]{2,1,0:T(8,128)(2,1)S(1)} %copy-done.21, bf16[5,1024,128]{2,1,0:T(8,128)(2,1)S(1)} %copy-done.22, ...), custom_call_target="tpu_custom_call" | custom-call | flops 20132659200 | bytes 20000000 | tf_op jit(solution)/shard_map/pallas_call | solution.py:289
  307.0 3.8 %collective-permute-start.40 = (bf16[2,320,256]{2,1,0:T(8,128)(2,1)S(1)}, bf16[2,320,256]{2,1,0:T(8,128)(2,1)S(1)}, u32[]{:S(2)}, u32[]{:S(2)}) collective-permute-start(bf16[2,320,256]{2,1,0:T(8,128)(2,1)S(1)} %get-tuple-element.261), channel_id=1, source_target_pairs={{0,24},{2,26},{4,28},{6,30},{8,0},{10,2},{12,4},{14,6},{16,8},{18,... | collective-permute-start | bytes 983048 | tf_op jit(solution)/shard_map/ppermute | solution.py:929
  310.8 7.9 %shard_map.224 = (bf16[1024,1664]{1,0:T(8,128)(2,1)S(1)}, bf16[16,64,896]{2,1,0:T(8,128)(2,1)S(1)}, bf16[16,64,896]{2,1,0:T(8,128)(2,1)S(1)}) custom-call(s32[4]{0:T(128)S(1)} %copy-done.19, bf16[15,1024,128]{2,1,0:T(8,128)(2,1)S(1)} %get-tuple-element.251.dq_ref, bf16[5,1024,128]{2,1,0:T(8,128)(2,1)S(1)} %get-tuple-element.252.dk_ref, ...), custom_call_target="tpu_custom_call" | custom-call | flops 3489660928 | bytes 20000000 | tf_op jit(solution)/shard_map/pallas_call | solution.py:660
  323.1 2.9 collective-permute-start.46
  329.6 4.6 %shard_map.227 = bf16[960,512]{1,0:T(8,128)(2,1)S(1)} custom-call(s32[4]{0:T(128)S(1)} %copy-done.19, bf16[1024,1664]{1,0:T(8,128)(2,1)S(1)} %get-tuple-element.317.flat_ref, bf16[1024,1664]{1,0:T(8,128)(2,1)S(1)} %copy-done.2, bf16[1024,1024]{1,0:T(8,128)(2,1)S(1)} %copy-done.4, f32[1024,1024]{1,0:T(8,128)S(1)} %copy-done.1, f32[8,1024]{1,0:T(8,128)S(1)} %copy-done.17, ...), custom_call_target="tpu_custom_call" | custom-call | flops 2751463424 | bytes 10000000 | tf_op jit(solution)/shard_map/pallas_call | solution.py:726
  334.2 4.7 %shard_map.228 = (bf16[960,512]{1,0:T(8,128)(2,1)S(1)}, bf16[2,960,512]{2,1,0:T(8,128)(2,1)}) custom-call(s32[4]{0:T(128)S(1)} %copy-done.19, f32[1024,1024]{1,0:T(8,128)S(1)} %copy-done.6, f32[1024,1024]{1,0:T(8,128)S(1)} %copy-done.7, bf16[1024,1024]{1,0:T(8,128)(2,1)S(1)} %copy-done), custom_call_target="tpu_custom_call" | custom-call | flops 2147483648 | bytes 16000000 | tf_op jit(solution)/shard_map/pallas_call | solution.py:604
  346.0 3.6 collective-permute-start.56
  349.7 5.2 %collective-permute-done.52 = bf16[2,224,256]{2,1,0:T(8,128)(2,1)S(1)} collective-permute-done((bf16[2,224,256]{2,1,0:T(8,128)(2,1)S(1)}, bf16[2,224,256]{2,1,0:T(8,128)(2,1)S(1)}, u32[]{:S(2)}, u32[]{:S(2)}) %collective-permute-start.52) | collective-permute-done | bytes 229408 | tf_op jit(solution)/shard_map/ppermute | solution.py:929
  355.6 3.2 collective-permute-start.53
  363.6 11.1 %shard_map.231 = f32[2,960,512]{2,1,0:T(8,128)} custom-call(s32[4]{0:T(128)} %pad_add_fusion.place_ref, bf16[1024,1664]{1,0:T(8,128)(2,1)} %copy-done.3, bf16[1024,1664]{1,0:T(8,128)(2,1)} %get-tuple-element.269.w_ref, bf16[1024,1024]{1,0:T(8,128)(2,1)} %get-tuple-element.204.xp_ref, f32[1024,1024]{1,0:T(8,128)} %get-tuple-element.237.em_ref, ...), custom_call_target="tpu_custom_call" | custom-call | flops 2751463424 | bytes 10000000 | tf_op jit(solution)/shard_map/pallas_call | solution.py:726
  (278 shorter events, 100.3 us)
Async XLA Ops:
  29.3 25.4 %collective-permute-start.9 = (bf16[960,256]{1,0:T(8,128)(2,1)S(1)}, bf16[960,256]{1,0:T(8,128)(2,1)S(1)}, u32[]{:S(2)}, u32[]{:S(2)}) collective-permute-start(bf16[960,256]{1,0:T(8,128)(2,1)S(1)} %maximum_bitcast_fusion), channel_id=1, source_target_pairs={{0,8},{2,10},{4,12},{6,14},{8,16},{10,18},{12,20},{14,22},{16,24},... | collective-permute-start | bytes 1474568 | tf_op jit(solution)/shard_map/ppermute | solution.py:929
  35.2 32.9 %collective-permute-start.6 = (bf16[8,32,1408]{2,1,0:T(8,128)(2,1)S(1)}, bf16[8,32,1408]{2,1,0:T(8,128)(2,1)S(1)}, u32[]{:S(2)}, u32[]{:S(2)}) collective-permute-start(bf16[8,32,1408]{2,1,0:T(8,128)(2,1)S(1)} %pad_maximum_fusion.2.refs_0_), channel_id=1, source_target_pairs={{0,4},{2,6},{4,0},{6,2},{8,12},{10,14},{12,8},{14,10},{16,20},{18,... | collective-permute-start | bytes 2162696 | tf_op jit(solution)/shard_map/ppermute | solution.py:913
  39.1 29.0 %collective-permute-start.8 = (bf16[8,32,1408]{2,1,0:T(8,128)(2,1)}, bf16[8,32,1408]{2,1,0:T(8,128)(2,1)}, u32[]{:S(2)}, u32[]{:S(2)}) collective-permute-start(bf16[8,32,1408]{2,1,0:T(8,128)(2,1)} %pad_maximum_fusion.3.refs_2_), channel_id=1, source_target_pairs={{0,2},{2,0},{4,6},{6,4},{8,10},{10,8},{12,14},{14,12},{16,18},{18,... | collective-permute-start | bytes 2162696 | tf_op jit(solution)/shard_map/ppermute | solution.py:913
  69.6 23.9 %collective-permute-start.17 = (bf16[4,480,256]{2,1,0:T(8,128)(2,1)S(1)}, bf16[4,480,256]{2,1,0:T(8,128)(2,1)}, u32[]{:S(2)}, u32[]{:S(2)}) collective-permute-start(bf16[4,480,256]{2,1,0:T(8,128)(2,1)S(1)} %get-tuple-element.196.refs_12_.refs_4_), channel_id=1, source_target_pairs={{0,4},{2,6},{4,0},{6,2},{8,12},{10,14},{12,8},{14,10},{16,20},{18,... | collective-permute-start | bytes 2949128 | tf_op jit(solution)/shard_map/ppermute | solution.py:913
  71.4 23.9 %collective-permute-start.16 = (bf16[4,480,256]{2,1,0:T(8,128)(2,1)S(1)}, bf16[4,480,256]{2,1,0:T(8,128)(2,1)}, u32[]{:S(2)}, u32[]{:S(2)}) collective-permute-start(bf16[4,480,256]{2,1,0:T(8,128)(2,1)S(1)} %get-tuple-element.195.refs_8_.refs_0_), channel_id=1, source_target_pairs={{0,2},{2,0},{4,6},{6,4},{8,10},{10,8},{12,14},{14,12},{16,18},{18,... | collective-permute-start | bytes 2949128 | tf_op jit(solution)/shard_map/ppermute | solution.py:913
  95.3 26.5 %collective-permute-start.20 = (bf16[4,480,256]{2,1,0:T(8,128)(2,1)S(1)}, bf16[4,480,256]{2,1,0:T(8,128)(2,1)S(1)}, u32[]{:S(2)}, u32[]{:S(2)}) collective-permute-start(bf16[4,480,256]{2,1,0:T(8,128)(2,1)S(1)} %get-tuple-element.195.refs_8_.refs_0_), channel_id=1, source_target_pairs={{0,1},{1,0},{2,3},{3,2},{4,5},{5,4},{6,7},{7,6},{8,9},{9,8},{10,11... | collective-permute-start | bytes 2949128 | tf_op jit(solution)/shard_map/ppermute | solution.py:909
  95.3 27.1 %collective-permute-start.18 = (bf16[4,480,256]{2,1,0:T(8,128)(2,1)S(1)}, bf16[4,480,256]{2,1,0:T(8,128)(2,1)S(1)}, u32[]{:S(2)}, u32[]{:S(2)}) collective-permute-start(bf16[4,480,256]{2,1,0:T(8,128)(2,1)S(1)} %get-tuple-element.195.refs_8_.refs_0_), channel_id=1, source_target_pairs={{0,4},{2,6},{4,0},{6,2},{8,12},{10,14},{12,8},{14,10},{16,20},{18,... | collective-permute-start | bytes 2949128 | tf_op jit(solution)/shard_map/ppermute | solution.py:913
  96.2 26.2 %collective-permute-start.21 = (bf16[4,480,256]{2,1,0:T(8,128)(2,1)S(1)}, bf16[4,480,256]{2,1,0:T(8,128)(2,1)S(1)}, u32[]{:S(2)}, u32[]{:S(2)}) collective-permute-start(bf16[4,480,256]{2,1,0:T(8,128)(2,1)S(1)} %get-tuple-element.196.refs_12_.refs_4_), channel_id=1, source_target_pairs={{0,1},{1,0},{2,3},{3,2},{4,5},{5,4},{6,7},{7,6},{8,9},{9,8},{10,11... | collective-permute-start | bytes 2949128 | tf_op jit(solution)/shard_map/ppermute | solution.py:909
  96.4 26.0 %collective-permute-start.19 = (bf16[4,480,256]{2,1,0:T(8,128)(2,1)S(1)}, bf16[4,480,256]{2,1,0:T(8,128)(2,1)S(1)}, u32[]{:S(2)}, u32[]{:S(2)}) collective-permute-start(bf16[4,480,256]{2,1,0:T(8,128)(2,1)S(1)} %get-tuple-element.196.refs_12_.refs_4_), channel_id=1, source_target_pairs={{0,2},{2,0},{4,6},{6,4},{8,10},{10,8},{12,14},{14,12},{16,18},{18,... | collective-permute-start | bytes 2949128 | tf_op jit(solution)/shard_map/ppermute | solution.py:913
  96.9 25.5 %collective-permute-start.22 = (bf16[4,480,256]{2,1,0:T(8,128)(2,1)}, bf16[4,480,256]{2,1,0:T(8,128)(2,1)S(1)}, u32[]{:S(2)}, u32[]{:S(2)}) collective-permute-start(bf16[4,480,256]{2,1,0:T(8,128)(2,1)} %collective-permute-done.16.refs_9_.refs_1_), channel_id=1, source_target_pairs={{0,1},{1,0},{2,3},{3,2},{4,5},{5,4},{6,7},{7,6},{8,9},{9,8},{10,11... | collective-permute-start | bytes 2949128 | tf_op jit(solution)/shard_map/ppermute | solution.py:909
  122.5 24.0 %collective-permute-start.23 = (bf16[4,480,256]{2,1,0:T(8,128)(2,1)}, bf16[4,480,256]{2,1,0:T(8,128)(2,1)S(1)}, u32[]{:S(2)}, u32[]{:S(2)}) collective-permute-start(bf16[4,480,256]{2,1,0:T(8,128)(2,1)} %collective-permute-done.16.refs_9_.refs_1_), channel_id=1, source_target_pairs={{0,4},{2,6},{4,0},{6,2},{8,12},{10,14},{12,8},{14,10},{16,20},{18,... | collective-permute-start | bytes 2949128 | tf_op jit(solution)/shard_map/ppermute | solution.py:913
  123.7 23.6 %collective-permute-start.24 = (bf16[4,480,256]{2,1,0:T(8,128)(2,1)}, bf16[4,480,256]{2,1,0:T(8,128)(2,1)S(1)}, u32[]{:S(2)}, u32[]{:S(2)}) collective-permute-start(bf16[4,480,256]{2,1,0:T(8,128)(2,1)} %collective-permute-done.17.refs_14_.refs_6_), channel_id=1, source_target_pairs={{0,2},{2,0},{4,6},{6,4},{8,10},{10,8},{12,14},{14,12},{16,18},{18,... | collective-permute-start | bytes 2949128 | tf_op jit(solution)/shard_map/ppermute | solution.py:913
  125.2 22.1 %collective-permute-start.27 = (bf16[4,480,256]{2,1,0:T(8,128)(2,1)S(1)}, bf16[4,480,256]{2,1,0:T(8,128)(2,1)}, u32[]{:S(2)}, u32[]{:S(2)}) collective-permute-start(bf16[4,480,256]{2,1,0:T(8,128)(2,1)S(1)} %collective-permute-done.19.refs_13_.refs_5_), channel_id=1, source_target_pairs={{0,1},{1,0},{2,3},{3,2},{4,5},{5,4},{6,7},{7,6},{8,9},{9,8},{10,11... | collective-permute-start | bytes 2949128 | tf_op jit(solution)/shard_map/ppermute | solution.py:909
  125.2 22.1 %collective-permute-start.26 = (bf16[4,480,256]{2,1,0:T(8,128)(2,1)S(1)}, bf16[4,480,256]{2,1,0:T(8,128)(2,1)}, u32[]{:S(2)}, u32[]{:S(2)}) collective-permute-start(bf16[4,480,256]{2,1,0:T(8,128)(2,1)S(1)} %collective-permute-done.18.refs_10_.refs_2_), channel_id=1, source_target_pairs={{0,1},{1,0},{2,3},{3,2},{4,5},{5,4},{6,7},{7,6},{8,9},{9,8},{10,11... | collective-permute-start | bytes 2949128 | tf_op jit(solution)/shard_map/ppermute | solution.py:909
  185.8 37.0 %collective-permute-start.30 = (bf16[16,640,256]{2,1,0:T(8,128)(2,1)}, bf16[16,640,256]{2,1,0:T(8,128)(2,1)S(1)}, u32[]{:S(2)}, u32[]{:S(2)}) collective-permute-start(bf16[16,640,256]{2,1,0:T(8,128)(2,1)} %get-tuple-element.219), channel_id=1, source_target_pairs={{0,1},{1,0},{2,3},{3,2},{4,5},{5,4},{6,7},{7,6},{8,9},{9,8},{10,11... | collective-permute-start | bytes 15728648 | tf_op jit(solution)/shard_map/ppermute | solution.py:909
  222.1 33.1 %collective-permute-start.33 = (bf16[2,2560,256]{2,1,0:T(8,128)(2,1)}, bf16[2,2560,256]{2,1,0:T(8,128)(2,1)S(1)}, u32[]{:S(2)}, u32[]{:S(2)}) collective-permute-start(bf16[2,2560,256]{2,1,0:T(8,128)(2,1)} %get-tuple-element.230), channel_id=1, source_target_pairs={{0,1},{1,0},{2,3},{3,2},{4,5},{5,4},{6,7},{7,6},{8,9},{9,8},{10,11... | collective-permute-start | bytes 7864328 | tf_op jit(solution)/shard_map/ppermute | solution.py:909
  230.4 32.6 %collective-permute-start.31 = (bf16[8,320,256]{2,1,0:T(8,128)(2,1)}, bf16[8,320,256]{2,1,0:T(8,128)(2,1)S(1)}, u32[]{:S(2)}, u32[]{:S(2)}) collective-permute-start(bf16[8,320,256]{2,1,0:T(8,128)(2,1)} %get-tuple-element.228), channel_id=1, source_target_pairs={{0,2},{2,0},{4,6},{6,4},{8,10},{10,8},{12,14},{14,12},{16,18},{18,... | collective-permute-start | bytes 3932168 | tf_op jit(solution)/shard_map/ppermute | solution.py:913
  231.9 31.2 %collective-permute-start.32 = (bf16[8,320,256]{2,1,0:T(8,128)(2,1)}, bf16[8,320,256]{2,1,0:T(8,128)(2,1)S(1)}, u32[]{:S(2)}, u32[]{:S(2)}) collective-permute-start(bf16[8,320,256]{2,1,0:T(8,128)(2,1)} %get-tuple-element.229), channel_id=1, source_target_pairs={{0,4},{2,6},{4,0},{6,2},{8,12},{10,14},{12,8},{14,10},{16,20},{18,... | collective-permute-start | bytes 3932168 | tf_op jit(solution)/shard_map/ppermute | solution.py:913
  261.3 41.9 %collective-permute-start.37 = (bf16[8,224,256]{2,1,0:T(8,128)(2,1)S(1)}, bf16[8,224,256]{2,1,0:T(8,128)(2,1)S(1)}, u32[]{:S(2)}, u32[]{:S(2)}) collective-permute-start(bf16[8,224,256]{2,1,0:T(8,128)(2,1)S(1)} %get-tuple-element.247), channel_id=1, source_target_pairs={{0,2},{2,0},{4,6},{6,4},{8,10},{10,8},{12,14},{14,12},{16,18},{18,... | collective-permute-start | bytes 2752520 | tf_op jit(solution)/shard_map/ppermute | solution.py:913
  261.9 41.3 %collective-permute-start.38 = (bf16[8,224,256]{2,1,0:T(8,128)(2,1)S(1)}, bf16[8,224,256]{2,1,0:T(8,128)(2,1)S(1)}, u32[]{:S(2)}, u32[]{:S(2)}) collective-permute-start(bf16[8,224,256]{2,1,0:T(8,128)(2,1)S(1)} %get-tuple-element.248), channel_id=1, source_target_pairs={{0,4},{2,6},{4,0},{6,2},{8,12},{10,14},{12,8},{14,10},{16,20},{18,... | collective-permute-start | bytes 2752520 | tf_op jit(solution)/shard_map/ppermute | solution.py:913
  264.4 41.7 %collective-permute-start.35 = (bf16[4,320,256]{2,1,0:T(8,128)(2,1)S(1)}, bf16[4,320,256]{2,1,0:T(8,128)(2,1)S(1)}, u32[]{:S(2)}, u32[]{:S(2)}) collective-permute-start(bf16[4,320,256]{2,1,0:T(8,128)(2,1)S(1)} %get-tuple-element.241), channel_id=1, source_target_pairs={{0,4},{2,6},{4,0},{6,2},{8,12},{10,14},{12,8},{14,10},{16,20},{18,... | collective-permute-start | bytes 1966088 | tf_op jit(solution)/shard_map/ppermute | solution.py:913
  265.3 40.8 %collective-permute-start.36 = (bf16[4,320,256]{2,1,0:T(8,128)(2,1)S(1)}, bf16[4,320,256]{2,1,0:T(8,128)(2,1)S(1)}, u32[]{:S(2)}, u32[]{:S(2)}) collective-permute-start(bf16[4,320,256]{2,1,0:T(8,128)(2,1)S(1)} %get-tuple-element.242), channel_id=1, source_target_pairs={{0,2},{2,0},{4,6},{6,4},{8,10},{10,8},{12,14},{14,12},{16,18},{18,... | collective-permute-start | bytes 1966088 | tf_op jit(solution)/shard_map/ppermute | solution.py:913
  346.0 28.7 %collective-permute-start.56 = (bf16[2,224,256]{2,1,0:T(8,128)(2,1)S(1)}, bf16[2,224,256]{2,1,0:T(8,128)(2,1)S(1)}, u32[]{:S(2)}, u32[]{:S(2)}) collective-permute-start(bf16[2,224,256]{2,1,0:T(8,128)(2,1)S(1)} %get-tuple-element.324), channel_id=1, source_target_pairs={{0,24},{2,26},{4,28},{6,30},{8,0},{10,2},{12,4},{14,6},{16,8},{18,... | collective-permute-start | bytes 688136 | tf_op jit(solution)/shard_map/ppermute | solution.py:929
  355.6 21.9 %collective-permute-start.53 = (bf16[2,32,896]{2,1,0:T(8,128)(2,1)S(1)}, bf16[2,32,896]{2,1,0:T(8,128)(2,1)S(1)}, u32[]{:S(2)}, u32[]{:S(2)}) collective-permute-start(bf16[2,32,896]{2,1,0:T(8,128)(2,1)S(1)} %get-tuple-element.314), channel_id=1, source_target_pairs={{0,8},{2,10},{4,12},{6,14},{8,16},{10,18},{12,20},{14,22},{16,24},... | collective-permute-start | bytes 344072 | tf_op jit(solution)/shard_map/ppermute | solution.py:929
  (83 other events, 838.3 us)

commit v4 on v3

--- a/solution.py
+++ b/solution.py
@@ -1097,7 +1097,7 @@
     one.turn(em)
     one.move_again()
     two = RowSum(
-        place_of, count, (blocked(d_keep), blocked(tie(d_got, em)), o_keep, o_got), read_quarters, 224
+        place_of, count, (blocked(d_keep), blocked(tie(d_got, em)), tie(o_keep, *one.sent), o_got), read_quarters, 224
     )
     two.move()
     do = tie(do, *one.sent, *two.sent)

time: 386 us -> 387 us (level)
    ppermute x22, waiting for transfers between devices: 14.7 us -> 22 us  [across(): return lax.ppermute(x, 'dp', [(i, i ^ 1 << bit) for i in range(count)])]
  transfers between devices with their start and end apart: 57 -> 57, of which waited for: 20 -> 21; matrix products, arithmetic and copies ran while one was open for 7% -> 7% of each run, Pallas kernels for 50% -> 50%
where the time goes in v4:
time: 387 us; the launch traced here: 381 us
  Pallas kernels  224 us (58%)
  waiting for transfers between devices  60.3 us (16%)
  starting transfers between devices  55.5 us (14%)
  local copies, waits for them, and re-layouts  23.3 us (6%)
  other arithmetic  15.8 us (4%)
    pallas_call x2, Pallas kernels, feed_forward(): call(functools.partial(ffn_body, turn), [jax.ShapeDtypeStruct((seq, wide)...  69.6 us
    ppermute x15, waiting for transfers between devices, along_z(): lax.ppermute(x, 'dp', [(i, (i + 4 * step) % count) for i in range(count)])  33.2 us
    pallas_call x1, Pallas kernels, attend_back(): call(functools.partial(attend_back_body, block), [jax.ShapeDtypeStruct((G...  32.9 us
    ppermute x15, starting transfers between devices, along_z(): lax.ppermute(x, 'dp', [(i, (i + 4 * step) % count) for i in range(count)])  28.7 us
    pallas_call x1, Pallas kernels, attend(): call(functools.partial(attend_body, block), [shape, shape], (KV_HEADS,),...  24.9 us
    ppermute x22, starting transfers between devices, across(): return lax.ppermute(x, 'dp', [(i, i ^ 1 << bit) for i in range(count)])  22.5 us
    pallas_call x1, Pallas kernels, after(): call(functools.partial(post_body, width), [jax.ShapeDtypeStruct((seq, wid...  22.3 us
    ppermute x22, waiting for transfers between devices, across(): return lax.ppermute(x, 'dp', [(i, i ^ 1 << bit) for i in range(count)])  22 us
  transfers between devices with their start and end apart: 57, of which 21 were waited for; matrix products, arithmetic and copies ran while one was open for 7% of the time, Pallas kernels for 50%

profile of v4, /device:TPU:0, one launch (start us, length us, event | category | flops | bytes accessed | tf_op | source)
XLA Modules:
  0.0 380.8 jit_solution(9381823512628904508)
XLA Ops:
  3.5 4.1 %collective-permute-start.2 = (bf16[64,1408]{1,0:T(8,128)(2,1)S(1)}, bf16[64,1408]{1,0:T(8,128)(2,1)S(1)}, u32[]{:S(2)}, u32[]{:S(2)}) collective-permute-start(bf16[64,1408]{1,0:T(8,128)(2,1)S(1)} %pad_maximum_fusion.4), channel_id=1, source_target_pairs={{0,16},{2,18},{4,20},{6,22},{8,24},{10,26},{12,28},{14,30},{16,0},... | collective-permute-start | bytes 540680 | tf_op jit(solution)/shard_map/ppermute | solution.py:929
  18.3 3.2 fusion.5
  31.1 4.0 %collective-permute-done.5 = bf16[4,32,1408]{2,1,0:T(8,128)(2,1)S(1)} collective-permute-done((bf16[4,32,1408]{2,1,0:T(8,128)(2,1)S(1)}, bf16[4,32,1408]{2,1,0:T(8,128)(2,1)S(1)}, u32[]{:S(2)}, u32[]{:S(2)}) %collective-permute-start.5) | collective-permute-done | bytes 360480 | tf_op jit(solution)/shard_map/ppermute | solution.py:913
  41.7 13.0 %collective-permute-done.9 = bf16[960,256]{1,0:T(8,128)(2,1)S(1)} collective-permute-done((bf16[960,256]{1,0:T(8,128)(2,1)S(1)}, bf16[960,256]{1,0:T(8,128)(2,1)S(1)}, u32[]{:S(2)}, u32[]{:S(2)}) %collective-permute-start.9) | collective-permute-done | bytes 491552 | tf_op jit(solution)/shard_map/ppermute | solution.py:929
  54.7 3.5 fusion.u_ref
  58.1 10.0 %collective-permute-done.11 = bf16[960,256]{1,0:T(8,128)(2,1)S(1)} collective-permute-done((bf16[960,256]{1,0:T(8,128)(2,1)S(1)}, bf16[960,256]{1,0:T(8,128)(2,1)S(1)}, u32[]{:S(2)}, u32[]{:S(2)}) %collective-permute-start.11) | collective-permute-done | bytes 491552 | tf_op jit(solution)/shard_map/ppermute | solution.py:929
  73.8 18.4 %shard_map.212 = (bf16[1024,1024]{1,0:T(8,128)(2,1)}, bf16[1024,1024]{1,0:T(8,128)(2,1)}, bf16[15,1024,128]{2,1,0:T(8,128)(2,1)}, bf16[5,1024,128]{2,1,0:T(8,128...) custom-call(s32[4]{0:T(128)} %pad_add_fusion.place_ref, ...), custom_call_target="tpu_custom_call" | custom-call | flops 5502926848 | bytes 20000000 | tf_op jit(solution)/shard_map/pallas_call | solution.py:170
  97.0 24.9 %shard_map.213 = (bf16[15,1024,128]{2,1,0:T(8,128)(2,1)}, bf16[15,1024,128]{2,1,0:T(8,128)(2,1)}) custom-call(bf16[15,1024,128]{2,1,0:T(8,128)(2,1)} %get-tuple-element.192.q_ref, bf16[5,1024,128]{2,1,0:T(8,128)(2,1)} %get-tuple-element.193.k_ref, bf16[5,1024,128]{2,1,0:T(8,128)(2,1)} %get-tuple-element.194.v_ref), custom_call_target="tpu_custom_call" | custom-call | flops 8053063680 | bytes 15000000 | tf_op jit(solution)/shard_map/pallas_call | solution.py:229
  125.7 16.4 %shard_map.214 = (bf16[1024,1024]{1,0:T(8,128)(2,1)}, f32[1024,1024]{1,0:T(8,128)}, bf16[1024,1024]{1,0:T(8,128)(2,1)}, bf16[1024,1024]{1,0:T(8,128)(2,1)}) custom-call(s32[4]{0:T(128)} %pad_add_fusion.place_ref, bf16[15,1024,128]{2,1,0:T(8,128)(2,1)} %get-tuple-element.203.o_ref, bf16[960,512]{1,0:T(8,128)(2,1)} %get-tuple-element.351.own_ref, ...), custom_call_target="tpu_custom_call" | custom-call | flops 8589934592 | bytes 22000000 | tf_op jit(solution)/shard_map/pallas_call | solution.py:334
  142.1 4.3 %collective-permute-done.23.refs_11_.refs_3_ = bf16[4,480,256]{2,1,0:T(8,128)(2,1)S(1)} collective-permute-done((bf16[4,480,256]{2,1,0:T(8,128)(2,1)}, bf16[4,480,256]{2,1,0:T(8,128)(2,1)S(1)}, u32[]{:S(2)}, u32[]{:S(2)}) %collective-permute-start.23) | collective-permute-done | bytes 983072 | tf_op jit(solution)/shard_map/ppermute | solution.py:913
  152.4 33.4 %shard_map.215 = (f32[1024,1024]{1,0:T(8,128)}, f32[1024,1024]{1,0:T(8,128)}, bf16[16,640,256]{2,1,0:T(8,128)(2,1)}, bf16[2,2560,256]{2,1,0:T(8,128)(2,1)}, bf16[2,2560,256]{2,1,0:T(8,128)(2,1)}) custom-call(s32[4]{0:T(128)} %pad_add_fusion.place_ref, bf16[1024,1024]{1,0:T(8,128)(2,1)} %get-tuple-element.221.b_ref, ...), custom_call_target="tpu_custom_call" | custom-call | flops 24159191040 | bytes 40000000 | tf_op jit(solution)/shard_map/pallas_call | solution.py:452
  185.9 36.3 %shard_map.216 = (f32[1024,1024]{1,0:T(8,128)}, f32[1024,1024]{1,0:T(8,128)}, bf16[16,640,256]{2,1,0:T(8,128)(2,1)}, bf16[2,2560,256]{2,1,0:T(8,128)(2,1)}, bf16[2,2560,256]{2,1,0:T(8,128)(2,1)}) custom-call(s32[4]{0:T(128)} %pad_add_fusion.place_ref, bf16[1024,1024]{1,0:T(8,128)(2,1)} %get-tuple-element.221.b_ref, ...), custom_call_target="tpu_custom_call", output_to_operand_aliasing={{3}: (27, {}), {4}: (28, {})} | custom-call | flops 24159191040 | bytes 40000000 | tf_op jit(solution)/shard_map/pallas_call | solution.py:452
  225.2 3.2 shard_map.217
  233.0 22.3 %shard_map.218 = (f32[1024,1024]{1,0:T(8,128)}, bf16[15,1024,128]{2,1,0:T(8,128)(2,1)}, f32[40,1024]{1,0:T(8,128)}, bf16[2,16,64,256]{3,2,1,0:T(8,128)(2,1)}, bf...) custom-call(s32[4]{0:T(128)} %pad_add_fusion.place_ref, f32[1024,1024]{1,0:T(8,128)} %get-tuple-element.290.m_ref, ...), custom_call_target="tpu_custom_call" | custom-call | flops 12884901888 | bytes 40000000 | tf_op jit(solution)/shard_map/pallas_call | solution.py:566
  255.4 6.1 %collective-permute-done.31.refs_1_ = bf16[8,320,256]{2,1,0:T(8,128)(2,1)S(1)} collective-permute-done((bf16[8,320,256]{2,1,0:T(8,128)(2,1)}, bf16[8,320,256]{2,1,0:T(8,128)(2,1)S(1)}, u32[]{:S(2)}, u32[]{:S(2)}) %collective-permute-start.31) | collective-permute-done | bytes 1310752 | tf_op jit(solution)/shard_map/ppermute | solution.py:913
  272.5 32.9 %shard_map.221 = (bf16[15,1024,128]{2,1,0:T(8,128)(2,1)S(1)}, bf16[5,1024,128]{2,1,0:T(8,128)(2,1)S(1)}, bf16[5,1024,128]{2,1,0:T(8,128)(2,1)S(1)}) custom-call(bf16[15,1024,128]{2,1,0:T(8,128)(2,1)S(1)} %copy-done.23, bf16[5,1024,128]{2,1,0:T(8,128)(2,1)S(1)} %copy-done.21, bf16[5,1024,128]{2,1,0:T(8,128)(2,1)S(1)} %copy-done.22, ...), custom_call_target="tpu_custom_call" | custom-call | flops 20132659200 | bytes 20000000 | tf_op jit(solution)/shard_map/pallas_call | solution.py:289
  308.8 3.8 %collective-permute-start.40 = (bf16[2,320,256]{2,1,0:T(8,128)(2,1)S(1)}, bf16[2,320,256]{2,1,0:T(8,128)(2,1)S(1)}, u32[]{:S(2)}, u32[]{:S(2)}) collective-permute-start(bf16[2,320,256]{2,1,0:T(8,128)(2,1)S(1)} %get-tuple-element.263), channel_id=1, source_target_pairs={{0,24},{2,26},{4,28},{6,30},{8,0},{10,2},{12,4},{14,6},{16,8},{18,... | collective-permute-start | bytes 983048 | tf_op jit(solution)/shard_map/ppermute | solution.py:929
  312.7 7.6 %shard_map.224 = (bf16[1024,1664]{1,0:T(8,128)(2,1)S(1)}, bf16[16,64,896]{2,1,0:T(8,128)(2,1)S(1)}, bf16[16,64,896]{2,1,0:T(8,128)(2,1)S(1)}) custom-call(s32[4]{0:T(128)S(1)} %copy-done.19, bf16[15,1024,128]{2,1,0:T(8,128)(2,1)S(1)} %get-tuple-element.253.dq_ref, bf16[5,1024,128]{2,1,0:T(8,128)(2,1)S(1)} %get-tuple-element.254.dk_ref, ...), custom_call_target="tpu_custom_call" | custom-call | flops 3489660928 | bytes 20000000 | tf_op jit(solution)/shard_map/pallas_call | solution.py:660
  330.4 4.6 %shard_map.227 = bf16[960,512]{1,0:T(8,128)(2,1)S(1)} custom-call(s32[4]{0:T(128)S(1)} %copy-done.19, bf16[1024,1664]{1,0:T(8,128)(2,1)S(1)} %get-tuple-element.319.flat_ref, bf16[1024,1664]{1,0:T(8,128)(2,1)S(1)} %copy-done.2, bf16[1024,1024]{1,0:T(8,128)(2,1)S(1)} %copy-done.4, f32[1024,1024]{1,0:T(8,128)S(1)} %copy-done.1, f32[8,1024]{1,0:T(8,128)S(1)} %copy-done.17, ...), custom_call_target="tpu_custom_call" | custom-call | flops 2751463424 | bytes 10000000 | tf_op jit(solution)/shard_map/pallas_call | solution.py:726
  335.0 4.6 %shard_map.228 = (bf16[960,512]{1,0:T(8,128)(2,1)S(1)}, bf16[2,960,512]{2,1,0:T(8,128)(2,1)}) custom-call(s32[4]{0:T(128)S(1)} %copy-done.19, f32[1024,1024]{1,0:T(8,128)S(1)} %copy-done.6, f32[1024,1024]{1,0:T(8,128)S(1)} %copy-done.7, bf16[1024,1024]{1,0:T(8,128)(2,1)S(1)} %copy-done), custom_call_target="tpu_custom_call" | custom-call | flops 2147483648 | bytes 16000000 | tf_op jit(solution)/shard_map/pallas_call | solution.py:604
  346.9 3.6 collective-permute-start.56
  350.6 5.2 %collective-permute-done.52 = bf16[2,224,256]{2,1,0:T(8,128)(2,1)S(1)} collective-permute-done((bf16[2,224,256]{2,1,0:T(8,128)(2,1)S(1)}, bf16[2,224,256]{2,1,0:T(8,128)(2,1)S(1)}, u32[]{:S(2)}, u32[]{:S(2)}) %collective-permute-start.52) | collective-permute-done | bytes 229408 | tf_op jit(solution)/shard_map/ppermute | solution.py:929
  356.5 3.2 collective-permute-start.53
  364.5 11.1 %shard_map.231 = f32[2,960,512]{2,1,0:T(8,128)} custom-call(s32[4]{0:T(128)} %pad_add_fusion.place_ref, bf16[1024,1664]{1,0:T(8,128)(2,1)} %copy-done.3, bf16[1024,1664]{1,0:T(8,128)(2,1)} %get-tuple-element.271.w_ref, bf16[1024,1024]{1,0:T(8,128)(2,1)} %get-tuple-element.205.xp_ref, f32[1024,1024]{1,0:T(8,128)} %get-tuple-element.238.em_ref, ...), custom_call_target="tpu_custom_call" | custom-call | flops 2751463424 | bytes 10000000 | tf_op jit(solution)/shard_map/pallas_call | solution.py:726
  (278 shorter events, 99.4 us)
Async XLA Ops:
  29.3 25.4 %collective-permute-start.9 = (bf16[960,256]{1,0:T(8,128)(2,1)S(1)}, bf16[960,256]{1,0:T(8,128)(2,1)S(1)}, u32[]{:S(2)}, u32[]{:S(2)}) collective-permute-start(bf16[960,256]{1,0:T(8,128)(2,1)S(1)} %maximum_bitcast_fusion), channel_id=1, source_target_pairs={{0,8},{2,10},{4,12},{6,14},{8,16},{10,18},{12,20},{14,22},{16,24},... | collective-permute-start | bytes 1474568 | tf_op jit(solution)/shard_map/ppermute | solution.py:929
  35.2 32.9 %collective-permute-start.6 = (bf16[8,32,1408]{2,1,0:T(8,128)(2,1)S(1)}, bf16[8,32,1408]{2,1,0:T(8,128)(2,1)S(1)}, u32[]{:S(2)}, u32[]{:S(2)}) collective-permute-start(bf16[8,32,1408]{2,1,0:T(8,128)(2,1)S(1)} %pad_maximum_fusion.2.refs_0_), channel_id=1, source_target_pairs={{0,4},{2,6},{4,0},{6,2},{8,12},{10,14},{12,8},{14,10},{16,20},{18,... | collective-permute-start | bytes 2162696 | tf_op jit(solution)/shard_map/ppermute | solution.py:913
  39.1 29.0 %collective-permute-start.8 = (bf16[8,32,1408]{2,1,0:T(8,128)(2,1)}, bf16[8,32,1408]{2,1,0:T(8,128)(2,1)}, u32[]{:S(2)}, u32[]{:S(2)}) collective-permute-start(bf16[8,32,1408]{2,1,0:T(8,128)(2,1)} %pad_maximum_fusion.3.refs_2_), channel_id=1, source_target_pairs={{0,2},{2,0},{4,6},{6,4},{8,10},{10,8},{12,14},{14,12},{16,18},{18,... | collective-permute-start | bytes 2162696 | tf_op jit(solution)/shard_map/ppermute | solution.py:913
  69.6 23.9 %collective-permute-start.17 = (bf16[4,480,256]{2,1,0:T(8,128)(2,1)S(1)}, bf16[4,480,256]{2,1,0:T(8,128)(2,1)}, u32[]{:S(2)}, u32[]{:S(2)}) collective-permute-start(bf16[4,480,256]{2,1,0:T(8,128)(2,1)S(1)} %get-tuple-element.197.refs_12_.refs_4_), channel_id=1, source_target_pairs={{0,4},{2,6},{4,0},{6,2},{8,12},{10,14},{12,8},{14,10},{16,20},{18,... | collective-permute-start | bytes 2949128 | tf_op jit(solution)/shard_map/ppermute | solution.py:913
  71.4 23.9 %collective-permute-start.16 = (bf16[4,480,256]{2,1,0:T(8,128)(2,1)S(1)}, bf16[4,480,256]{2,1,0:T(8,128)(2,1)}, u32[]{:S(2)}, u32[]{:S(2)}) collective-permute-start(bf16[4,480,256]{2,1,0:T(8,128)(2,1)S(1)} %get-tuple-element.196.refs_8_.refs_0_), channel_id=1, source_target_pairs={{0,2},{2,0},{4,6},{6,4},{8,10},{10,8},{12,14},{14,12},{16,18},{18,... | collective-permute-start | bytes 2949128 | tf_op jit(solution)/shard_map/ppermute | solution.py:913
  95.3 26.5 %collective-permute-start.20 = (bf16[4,480,256]{2,1,0:T(8,128)(2,1)S(1)}, bf16[4,480,256]{2,1,0:T(8,128)(2,1)S(1)}, u32[]{:S(2)}, u32[]{:S(2)}) collective-permute-start(bf16[4,480,256]{2,1,0:T(8,128)(2,1)S(1)} %get-tuple-element.196.refs_8_.refs_0_), channel_id=1, source_target_pairs={{0,1},{1,0},{2,3},{3,2},{4,5},{5,4},{6,7},{7,6},{8,9},{9,8},{10,11... | collective-permute-start | bytes 2949128 | tf_op jit(solution)/shard_map/ppermute | solution.py:909
  95.3 27.1 %collective-permute-start.18 = (bf16[4,480,256]{2,1,0:T(8,128)(2,1)S(1)}, bf16[4,480,256]{2,1,0:T(8,128)(2,1)S(1)}, u32[]{:S(2)}, u32[]{:S(2)}) collective-permute-start(bf16[4,480,256]{2,1,0:T(8,128)(2,1)S(1)} %get-tuple-element.196.refs_8_.refs_0_), channel_id=1, source_target_pairs={{0,4},{2,6},{4,0},{6,2},{8,12},{10,14},{12,8},{14,10},{16,20},{18,... | collective-permute-start | bytes 2949128 | tf_op jit(solution)/shard_map/ppermute | solution.py:913
  96.2 26.2 %collective-permute-start.21 = (bf16[4,480,256]{2,1,0:T(8,128)(2,1)S(1)}, bf16[4,480,256]{2,1,0:T(8,128)(2,1)S(1)}, u32[]{:S(2)}, u32[]{:S(2)}) collective-permute-start(bf16[4,480,256]{2,1,0:T(8,128)(2,1)S(1)} %get-tuple-element.197.refs_12_.refs_4_), channel_id=1, source_target_pairs={{0,1},{1,0},{2,3},{3,2},{4,5},{5,4},{6,7},{7,6},{8,9},{9,8},{10,11... | collective-permute-start | bytes 2949128 | tf_op jit(solution)/shard_map/ppermute | solution.py:909
  96.4 26.0 %collective-permute-start.19 = (bf16[4,480,256]{2,1,0:T(8,128)(2,1)S(1)}, bf16[4,480,256]{2,1,0:T(8,128)(2,1)S(1)}, u32[]{:S(2)}, u32[]{:S(2)}) collective-permute-start(bf16[4,480,256]{2,1,0:T(8,128)(2,1)S(1)} %get-tuple-element.197.refs_12_.refs_4_), channel_id=1, source_target_pairs={{0,2},{2,0},{4,6},{6,4},{8,10},{10,8},{12,14},{14,12},{16,18},{18,... | collective-permute-start | bytes 2949128 | tf_op jit(solution)/shard_map/ppermute | solution.py:913
  96.9 25.5 %collective-permute-start.22 = (bf16[4,480,256]{2,1,0:T(8,128)(2,1)}, bf16[4,480,256]{2,1,0:T(8,128)(2,1)S(1)}, u32[]{:S(2)}, u32[]{:S(2)}) collective-permute-start(bf16[4,480,256]{2,1,0:T(8,128)(2,1)} %collective-permute-done.16.refs_9_.refs_1_), channel_id=1, source_target_pairs={{0,1},{1,0},{2,3},{3,2},{4,5},{5,4},{6,7},{7,6},{8,9},{9,8},{10,11... | collective-permute-start | bytes 2949128 | tf_op jit(solution)/shard_map/ppermute | solution.py:909
  122.5 24.0 %collective-permute-start.23 = (bf16[4,480,256]{2,1,0:T(8,128)(2,1)}, bf16[4,480,256]{2,1,0:T(8,128)(2,1)S(1)}, u32[]{:S(2)}, u32[]{:S(2)}) collective-permute-start(bf16[4,480,256]{2,1,0:T(8,128)(2,1)} %collective-permute-done.16.refs_9_.refs_1_), channel_id=1, source_target_pairs={{0,4},{2,6},{4,0},{6,2},{8,12},{10,14},{12,8},{14,10},{16,20},{18,... | collective-permute-start | bytes 2949128 | tf_op jit(solution)/shard_map/ppermute | solution.py:913
  123.7 23.6 %collective-permute-start.24 = (bf16[4,480,256]{2,1,0:T(8,128)(2,1)}, bf16[4,480,256]{2,1,0:T(8,128)(2,1)S(1)}, u32[]{:S(2)}, u32[]{:S(2)}) collective-permute-start(bf16[4,480,256]{2,1,0:T(8,128)(2,1)} %collective-permute-done.17.refs_14_.refs_6_), channel_id=1, source_target_pairs={{0,2},{2,0},{4,6},{6,4},{8,10},{10,8},{12,14},{14,12},{16,18},{18,... | collective-permute-start | bytes 2949128 | tf_op jit(solution)/shard_map/ppermute | solution.py:913
  125.2 22.1 %collective-permute-start.27 = (bf16[4,480,256]{2,1,0:T(8,128)(2,1)S(1)}, bf16[4,480,256]{2,1,0:T(8,128)(2,1)S(1)}, u32[]{:S(2)}, u32[]{:S(2)}) collective-permute-start(bf16[4,480,256]{2,1,0:T(8,128)(2,1)S(1)} %collective-permute-done.19.refs_13_.refs_5_), channel_id=1, source_target_pairs={{0,1},{1,0},{2,3},{3,2},{4,5},{5,4},{6,7},{7,6},{8,9},{9,8},{10,11... | collective-permute-start | bytes 2949128 | tf_op jit(solution)/shard_map/ppermute | solution.py:909
  125.2 22.1 %collective-permute-start.26 = (bf16[4,480,256]{2,1,0:T(8,128)(2,1)S(1)}, bf16[4,480,256]{2,1,0:T(8,128)(2,1)}, u32[]{:S(2)}, u32[]{:S(2)}) collective-permute-start(bf16[4,480,256]{2,1,0:T(8,128)(2,1)S(1)} %collective-permute-done.18.refs_10_.refs_2_), channel_id=1, source_target_pairs={{0,1},{1,0},{2,3},{3,2},{4,5},{5,4},{6,7},{7,6},{8,9},{9,8},{10,11... | collective-permute-start | bytes 2949128 | tf_op jit(solution)/shard_map/ppermute | solution.py:909
  185.8 37.0 %collective-permute-start.30 = (bf16[16,640,256]{2,1,0:T(8,128)(2,1)}, bf16[16,640,256]{2,1,0:T(8,128)(2,1)S(1)}, u32[]{:S(2)}, u32[]{:S(2)}) collective-permute-start(bf16[16,640,256]{2,1,0:T(8,128)(2,1)} %get-tuple-element.220), channel_id=1, source_target_pairs={{0,1},{1,0},{2,3},{3,2},{4,5},{5,4},{6,7},{7,6},{8,9},{9,8},{10,11... | collective-permute-start | bytes 15728648 | tf_op jit(solution)/shard_map/ppermute | solution.py:909
  222.2 33.2 %collective-permute-start.33 = (bf16[2,2560,256]{2,1,0:T(8,128)(2,1)}, bf16[2,2560,256]{2,1,0:T(8,128)(2,1)S(1)}, u32[]{:S(2)}, u32[]{:S(2)}) collective-permute-start(bf16[2,2560,256]{2,1,0:T(8,128)(2,1)} %get-tuple-element.231), channel_id=1, source_target_pairs={{0,1},{1,0},{2,3},{3,2},{4,5},{5,4},{6,7},{7,6},{8,9},{9,8},{10,11... | collective-permute-start | bytes 7864328 | tf_op jit(solution)/shard_map/ppermute | solution.py:909
  230.6 30.9 %collective-permute-start.31 = (bf16[8,320,256]{2,1,0:T(8,128)(2,1)}, bf16[8,320,256]{2,1,0:T(8,128)(2,1)S(1)}, u32[]{:S(2)}, u32[]{:S(2)}) collective-permute-start(bf16[8,320,256]{2,1,0:T(8,128)(2,1)} %get-tuple-element.229), channel_id=1, source_target_pairs={{0,2},{2,0},{4,6},{6,4},{8,10},{10,8},{12,14},{14,12},{16,18},{18,... | collective-permute-start | bytes 3932168 | tf_op jit(solution)/shard_map/ppermute | solution.py:913
  232.1 30.6 %collective-permute-start.32 = (bf16[8,320,256]{2,1,0:T(8,128)(2,1)}, bf16[8,320,256]{2,1,0:T(8,128)(2,1)S(1)}, u32[]{:S(2)}, u32[]{:S(2)}) collective-permute-start(bf16[8,320,256]{2,1,0:T(8,128)(2,1)} %get-tuple-element.230), channel_id=1, source_target_pairs={{0,4},{2,6},{4,0},{6,2},{8,12},{10,14},{12,8},{14,10},{16,20},{18,... | collective-permute-start | bytes 3932168 | tf_op jit(solution)/shard_map/ppermute | solution.py:913
  264.0 43.9 %collective-permute-start.35 = (bf16[4,320,256]{2,1,0:T(8,128)(2,1)S(1)}, bf16[4,320,256]{2,1,0:T(8,128)(2,1)S(1)}, u32[]{:S(2)}, u32[]{:S(2)}) collective-permute-start(bf16[4,320,256]{2,1,0:T(8,128)(2,1)S(1)} %get-tuple-element.242), channel_id=1, source_target_pairs={{0,4},{2,6},{4,0},{6,2},{8,12},{10,14},{12,8},{14,10},{16,20},{18,... | collective-permute-start | bytes 1966088 | tf_op jit(solution)/shard_map/ppermute | solution.py:913
  264.9 43.0 %collective-permute-start.36 = (bf16[4,320,256]{2,1,0:T(8,128)(2,1)S(1)}, bf16[4,320,256]{2,1,0:T(8,128)(2,1)S(1)}, u32[]{:S(2)}, u32[]{:S(2)}) collective-permute-start(bf16[4,320,256]{2,1,0:T(8,128)(2,1)S(1)} %get-tuple-element.243), channel_id=1, source_target_pairs={{0,2},{2,0},{4,6},{6,4},{8,10},{10,8},{12,14},{14,12},{16,18},{18,... | collective-permute-start | bytes 1966088 | tf_op jit(solution)/shard_map/ppermute | solution.py:913
  267.6 37.7 %collective-permute-start.37 = (bf16[8,224,256]{2,1,0:T(8,128)(2,1)S(1)}, bf16[8,224,256]{2,1,0:T(8,128)(2,1)S(1)}, u32[]{:S(2)}, u32[]{:S(2)}) collective-permute-start(bf16[8,224,256]{2,1,0:T(8,128)(2,1)S(1)} %get-tuple-element.249), channel_id=1, source_target_pairs={{0,2},{2,0},{4,6},{6,4},{8,10},{10,8},{12,14},{14,12},{16,18},{18,... | collective-permute-start | bytes 2752520 | tf_op jit(solution)/shard_map/ppermute | solution.py:913
  269.1 36.2 %collective-permute-start.38 = (bf16[8,224,256]{2,1,0:T(8,128)(2,1)S(1)}, bf16[8,224,256]{2,1,0:T(8,128)(2,1)S(1)}, u32[]{:S(2)}, u32[]{:S(2)}) collective-permute-start(bf16[8,224,256]{2,1,0:T(8,128)(2,1)S(1)} %get-tuple-element.250), channel_id=1, source_target_pairs={{0,4},{2,6},{4,0},{6,2},{8,12},{10,14},{12,8},{14,10},{16,20},{18,... | collective-permute-start | bytes 2752520 | tf_op jit(solution)/shard_map/ppermute | solution.py:913
  346.9 28.8 %collective-permute-start.56 = (bf16[2,224,256]{2,1,0:T(8,128)(2,1)S(1)}, bf16[2,224,256]{2,1,0:T(8,128)(2,1)S(1)}, u32[]{:S(2)}, u32[]{:S(2)}) collective-permute-start(bf16[2,224,256]{2,1,0:T(8,128)(2,1)S(1)} %get-tuple-element.326), channel_id=1, source_target_pairs={{0,24},{2,26},{4,28},{6,30},{8,0},{10,2},{12,4},{14,6},{16,8},{18,... | collective-permute-start | bytes 688136 | tf_op jit(solution)/shard_map/ppermute | solution.py:929
  356.5 21.9 %collective-permute-start.53 = (bf16[2,32,896]{2,1,0:T(8,128)(2,1)S(1)}, bf16[2,32,896]{2,1,0:T(8,128)(2,1)S(1)}, u32[]{:S(2)}, u32[]{:S(2)}) collective-permute-start(bf16[2,32,896]{2,1,0:T(8,128)(2,1)S(1)} %get-tuple-element.316), channel_id=1, source_target_pairs={{0,8},{2,10},{4,12},{6,14},{8,16},{10,18},{12,20},{14,22},{16,24},... | collective-permute-start | bytes 344072 | tf_op jit(solution)/shard_map/ppermute | solution.py:929
  (83 other events, 870.7 us)
